TPU v7x, 256 devices: a whole 4x4x8 slice. The times are simulated.
256 devices in a mesh: flop: 64 (over z, x, core), turn: 4 (over y).
Axes of the slice: x: 4, y: 4, z: 8, core: 2. Of those that a mesh axis runs over, the one named last changes fastest.
Arguments:
- ranges: float32 [2, 1326], replicated, may hold values from 0.05 to 1
- flop_regret: float32 [64, 4, 1326], P('flop'), may hold values from 0.01 to 1
- flop_cards: int32 [64, 3], P('flop'), may hold values from 0 to 51, as said below
- live_turns: int32 [64, 4], P('flop'), may hold values from 1 to 24, as said below
- turn_card: int32 [64, 96], P('flop', 'turn'), may hold values from 0 to 51, as said below
- river_cards: int32 [64, 96, 2], P('flop', 'turn'), may hold values from 0 to 51, as said below
- strength: float32 [64, 96, 2, 1326], P('flop', 'turn'), may hold values from 0 to 1
- turn_regret: float32 [64, 96, 4, 4, 1326], P('flop', 'turn'), may hold values from 0.01 to 1
Outputs:
- new_flop_regret: float32 [64, 4, 1326], P('flop')
- new_turn_regret: float32 [64, 96, 4, 4, 1326], P('flop', 'turn')
- root_value: float32 [2, 1326], replicated
Inputs may be any that keep to these rules, and one draw needn't show every extreme that they name: `live_turns`: for each flop the 4 counts add up to 49, one device holds exactly 24, and the counts of the other devices differ from one another by at most one. `flop_cards`: three different cards. `turn_card`: the live slots of one flop hold its 49 turn cards, all different and none on the flop. `river_cards`: the rivers of a slot differ from one another, from the flop and from the slot's turn card.
All inputs are finite; a program needn't handle non-finite values.
Results may differ from a plain program's by a relative error of at most 0.0003.
Values sent between devices are 32-bit elements; how exact they have to be, the bound alone decides.
No kernel may reach another device: no remote copies, remote signals or barrier semaphores. Data moves between devices by JAX's collectives and lax.ppermute only.
A program may use at most 64 MiB of HBM per device.

v0:
```python
import jax
import jax.numpy as jnp
import numpy as np
from jax import lax
from jax.sharding import PartitionSpec as P

CARDS = 52
H = 1326
TURNS = 49
TS = 24
RIV = 2


bet_sizes = (0.25, 0.5, 1.0, 2.0)


def hand_table():
    card_low, card_high = np.triu_indices(CARDS, 1)
    return (jnp.asarray(card_low, jnp.int32), jnp.asarray(card_high, jnp.int32))


def pot_table():
    growth = 1.0 + 2.0 * np.asarray(bet_sizes)
    return jnp.asarray(np.outer(growth, growth) / (2.0 * H * RIV), jnp.float32)


def unblocked(card_low, card_high, board):
    struck = (card_low[None, :] == board[:, None]) | (card_high[None, :] == board[:, None])
    return jnp.where(jnp.any(struck, axis=0), 0.0, 1.0).astype(jnp.float32)


def slot_terms(
    reach_one,
    reach_zero,
    pot_gain,
    flop_board,
    card_low,
    card_high,
    turn_id,
    river_ids,
    strengths,
    regrets,
):
    actions = regrets.shape[0]
    hands = regrets.shape[2]
    sigma_turn = regrets / jnp.sum(regrets, axis=1, keepdims=True)
    reach_other = (
        (reach_one[None, None, :] * sigma_turn)
        .astype(jnp.bfloat16)
        .reshape(actions * actions, hands)
    )
    early = jnp.concatenate([flop_board, turn_id[None]])
    disjoint = (
        (card_low[:, None] != card_low[None, :])
        & (card_low[:, None] != card_high[None, :])
        & (card_high[:, None] != card_low[None, :])
        & (card_high[:, None] != card_high[None, :])
    )

    def river_step(totals, inputs):
        river_id, strength_row = inputs
        alive = unblocked(card_low, card_high, jnp.concatenate([early, river_id[None]]))
        outcome = jnp.sign(strength_row[:, None] - strength_row[None, :]) * jnp.where(
            disjoint, alive[:, None] * alive[None, :], 0.0
        )
        outcome = outcome.astype(jnp.bfloat16)
        toward = lax.dot_general(
            reach_other, outcome, (((1,), (1,)), ((), ())), preferred_element_type=jnp.float32
        )
        against = jnp.dot(reach_zero, outcome, preferred_element_type=jnp.float32)
        return ((totals[0] + toward, totals[1] + against), None)

    start = (
        jnp.zeros((actions * actions, hands), jnp.float32),
        jnp.zeros((actions, hands), jnp.float32),
    )
    (toward, against), _ = lax.scan(river_step, start, (river_ids, strengths))
    value_zero = jnp.sum(pot_gain[:, :, None] * toward.reshape(actions, actions, hands), axis=1)
    action_one = -pot_gain[:, :, None] * against[:, None, :]
    value_one = jnp.sum(sigma_turn * action_one, axis=1)
    new_turn = jnp.maximum(regrets + action_one - value_one[:, None, :], 0.0)
    return (value_zero, value_one, new_turn)


def run_slots(turn_ids, river_ids, strengths, regrets, is_live, reach_one, reach_zero, flop_board):
    card_low, card_high = hand_table()
    pot_gain = pot_table()

    def one_slot(inputs):
        return slot_terms(
            reach_one,
            reach_zero,
            pot_gain,
            flop_board,
            card_low,
            card_high,
            inputs[0],
            inputs[1],
            inputs[2],
            inputs[3],
        )

    value_zero, value_one, new_turn = lax.map(one_slot, (turn_ids, river_ids, strengths, regrets))
    sum_zero = jnp.sum(jnp.where(is_live[:, None, None], value_zero, 0.0), axis=0)
    sum_one = jnp.sum(jnp.where(is_live[:, None, None], value_one, 0.0), axis=0)
    new_turn = jnp.where(is_live[:, None, None, None], new_turn, 0.0)
    return (sum_zero, sum_one, new_turn)


def on_device(
    ranges, flop_regret, flop_cards, live_turns, turn_card, river_cards, strength, turn_regret
):
    turn_devs = lax.axis_size("turn")
    flop_devs = lax.axis_size("flop")
    my_index = lax.axis_index("turn")
    counts = live_turns[0]
    starts = jnp.cumsum(counts) - counts
    my_count = jnp.take(counts, my_index)
    my_start = jnp.take(starts, my_index)
    regrets_flop = flop_regret[0]
    sigma_flop = regrets_flop / jnp.sum(regrets_flop, axis=0, keepdims=True)
    reach_zero = (ranges[0][None, :] * sigma_flop).astype(jnp.bfloat16)
    reach_second = ranges[1]
    flop_board = flop_cards[0]
    local_slots = jnp.arange(TS, dtype=jnp.int32)
    own_live = local_slots < my_count
    share = (TURNS + turn_devs - 1) // turn_devs
    device_list = jnp.arange(turn_devs, dtype=jnp.int32)
    positions = my_index * share + jnp.arange(share, dtype=jnp.int32)
    holder = (positions[:, None] >= starts[None, :]) & (
        positions[:, None] < (starts + counts)[None, :]
    )
    share_live = positions < TURNS
    places = jnp.minimum(my_start + local_slots, turn_devs * share - 1)
    gathered = (
        lax.all_gather(turn_card.astype(jnp.float32), "turn", axis=1, tiled=True),
        lax.all_gather(river_cards.astype(jnp.float32), "turn", axis=1, tiled=True),
        lax.all_gather(strength, "turn", axis=1, tiled=True),
        lax.all_gather(turn_regret, "turn", axis=1, tiled=True),
    )
    source_rows = jnp.sum(
        jnp.where(holder, device_list[None, :] * TS + positions[:, None] - starts[None, :], 0),
        axis=1,
    )
    sum_zero, sum_one, share_turn = run_slots(
        jnp.take(gathered[0][0], source_rows, axis=0).astype(jnp.int32),
        jnp.take(gathered[1][0], source_rows, axis=0).astype(jnp.int32),
        jnp.take(gathered[2][0], source_rows, axis=0),
        jnp.take(gathered[3][0], source_rows, axis=0),
        share_live,
        reach_second,
        reach_zero,
        flop_board,
    )
    returned = lax.all_gather(share_turn, "turn", axis=0, tiled=True)
    new_turn = jnp.where(own_live[:, None, None, None], jnp.take(returned, places, axis=0), 0.0)
    totals = lax.psum(jnp.stack([sum_zero, sum_one]), "turn")
    action_value = totals[0] / TURNS
    node_zero = jnp.sum(sigma_flop * action_value, axis=0)
    node_one = jnp.sum(totals[1], axis=0) / TURNS
    new_flop = jnp.maximum(regrets_flop + action_value - node_zero[None, :], 0.0)
    root_value = lax.psum(jnp.stack([node_zero, node_one]) / flop_devs, "flop")
    return (new_flop[None], new_turn[None], root_value)


def solution(mesh):
    placed = (
        P(),
        P("flop", None, None),
        P("flop", None),
        P("flop", None),
        P("flop", "turn"),
        P("flop", "turn", None),
        P("flop", "turn", None, None),
        P("flop", "turn", None, None, None),
    )
    return jax.shard_map(
        on_device,
        mesh=mesh,
        in_specs=placed,
        out_specs=(P("flop", None, None), P("flop", "turn", None, None, None), P()),
        check_vma=False,
    )
```

profile of v0, /device:TPU:1, one launch (start us, length us, event | category | flops | bytes accessed | tf_op | source)
XLA Modules:
  0.0 722.3 jit_solution(9767701825504635265)
XLA Ops:
  9.6 9.5 %all-reduce = f32[96]{0:T(128)S(1)} all-reduce(f32[96]{0:T(128)S(1)} %bitcast_dynamic-update-slice_fusion.2), channel_id=1, replica_groups=mesh['flop'=64,'turn'=4] {'turn'}, use_global_device_ids=true, to_apply=%add | all-reduce | flops 96 | bytes 768 | tf_op jit(solution)/shard_map/squeeze | solution.py:146
  19.9 14.7 %all_gather.16 = f32[1,96,2,1326]{3,2,0,1:T(2,128)S(1)} all-gather(f32[1,24,2,1326]{3,2,0,1:T(2,128)S(1)} %bitcast.92), channel_id=1, replica_groups=mesh['flop'=64,'turn'=4] {'turn'}, dimensions={1}, use_global_device_ids=true | all-gather | bytes 1272960 | tf_op jit(solution)/shard_map/all_gather | solution.py:138
  35.4 10.2 %all_gather.15 = f32[1,96,2]{2,0,1:T(1,128)S(1)} all-gather(f32[1,24,2]{2,0,1:T(1,128)S(1)} %copy.25), channel_id=1, replica_groups=mesh['flop'=64,'turn'=4] {'turn'}, dimensions={1}, use_global_device_ids=true | all-gather | bytes 960 | tf_op jit(solution)/shard_map/all_gather | solution.py:137
  49.4 55.5 %all-gather.3.cloned.1.call-done = f32[1,96,4,4,1326]{4,3,2,0,1:T(4,128)} async-done(((f32[1,24,4,4,1326]{4,3,2,0,1:T(4,128)}), f32[1,96,4,4,1326]{4,3,2,0,1:T(4,128)}) %all-gather.3.cloned.1.call-update) | async-done | bytes 8146960 | tf_op jit(solution)/shard_map/all_gather | solution.py:139
  104.9 4.8 gather_fusion.3
  110.8 333.3 %while.45 = (s32[]{:T(128)}, f32[13,4,1326]{2,1,0:T(4,128)S(1)}, f32[13,4,1326]{2,1,0:T(4,128)S(1)}, f32[13,4,4,1326]{3,2,1,0:T(4,128)S(1)}, s32[13,2]{1,0:T(8,1...) while((s32[]{:T(128)}, f32[13,4,1326]{2,1,0:T(4,128)S(1)}, ...), condition=%wide.region_10.11_spmd.clone.clone.clone, body=%wide.region_3.10_spmd.sunk.clone.clone.sunk.clone | while | flops 116406888 | bytes 2007517 | solution.py:103
  113.4 22.8 %while.44 = (s32[]{:T(128)}, f32[16,1326]{1,0:T(8,128)S(1)}, f32[4,1326]{1,0:T(4,128)S(1)}, f32[2,1326]{1,0:T(2,128)S(1)}, s32[2]{0:T(128)S(1)}, /*index=5*/s32[...) while((s32[]{:T(128)}, f32[16,1326]{1,0:T(8,128)S(1)}, ...), condition=%wide.region_7.7_spmd.clone.clone.clone, body=%wide.region_5.6_spmd.sunk.clone.clone.clone.sunk | while | flops 116125776 | bytes 379492 | solution.py:77
  115.4 4.7 fusion.34
  126.8 4.7 fusion.34
  139.0 22.8 %while.44 = (s32[]{:T(128)}, f32[16,1326]{1,0:T(8,128)S(1)}, f32[4,1326]{1,0:T(4,128)S(1)}, f32[2,1326]{1,0:T(2,128)S(1)}, s32[2]{0:T(128)S(1)}, /*index=5*/s32[...) while((s32[]{:T(128)}, f32[16,1326]{1,0:T(8,128)S(1)}, ...), condition=%wide.region_7.7_spmd.clone.clone.clone, body=%wide.region_5.6_spmd.sunk.clone.clone.clone.sunk | while | flops 116125776 | bytes 379492 | solution.py:77
  141.0 4.7 fusion.34
  152.5 4.7 fusion.34
  164.6 22.8 %while.44 = (s32[]{:T(128)}, f32[16,1326]{1,0:T(8,128)S(1)}, f32[4,1326]{1,0:T(4,128)S(1)}, f32[2,1326]{1,0:T(2,128)S(1)}, s32[2]{0:T(128)S(1)}, /*index=5*/s32[...) while((s32[]{:T(128)}, f32[16,1326]{1,0:T(8,128)S(1)}, ...), condition=%wide.region_7.7_spmd.clone.clone.clone, body=%wide.region_5.6_spmd.sunk.clone.clone.clone.sunk | while | flops 116125776 | bytes 379492 | solution.py:77
  166.7 4.7 fusion.34
  178.1 4.7 fusion.34
  190.2 22.8 %while.44 = (s32[]{:T(128)}, f32[16,1326]{1,0:T(8,128)S(1)}, f32[4,1326]{1,0:T(4,128)S(1)}, f32[2,1326]{1,0:T(2,128)S(1)}, s32[2]{0:T(128)S(1)}, /*index=5*/s32[...) while((s32[]{:T(128)}, f32[16,1326]{1,0:T(8,128)S(1)}, ...), condition=%wide.region_7.7_spmd.clone.clone.clone, body=%wide.region_5.6_spmd.sunk.clone.clone.clone.sunk | while | flops 116125776 | bytes 379492 | solution.py:77
  192.3 4.7 fusion.34
  203.7 4.7 fusion.34
  215.8 22.8 %while.44 = (s32[]{:T(128)}, f32[16,1326]{1,0:T(8,128)S(1)}, f32[4,1326]{1,0:T(4,128)S(1)}, f32[2,1326]{1,0:T(2,128)S(1)}, s32[2]{0:T(128)S(1)}, /*index=5*/s32[...) while((s32[]{:T(128)}, f32[16,1326]{1,0:T(8,128)S(1)}, ...), condition=%wide.region_7.7_spmd.clone.clone.clone, body=%wide.region_5.6_spmd.sunk.clone.clone.clone.sunk | while | flops 116125776 | bytes 379492 | solution.py:77
  241.5 22.8 %while.44 = (s32[]{:T(128)}, f32[16,1326]{1,0:T(8,128)S(1)}, f32[4,1326]{1,0:T(4,128)S(1)}, f32[2,1326]{1,0:T(2,128)S(1)}, s32[2]{0:T(128)S(1)}, /*index=5*/s32[...) while((s32[]{:T(128)}, f32[16,1326]{1,0:T(8,128)S(1)}, ...), condition=%wide.region_7.7_spmd.clone.clone.clone, body=%wide.region_5.6_spmd.sunk.clone.clone.clone.sunk | while | flops 116125776 | bytes 379492 | solution.py:77
  267.1 22.8 %while.44 = (s32[]{:T(128)}, f32[16,1326]{1,0:T(8,128)S(1)}, f32[4,1326]{1,0:T(4,128)S(1)}, f32[2,1326]{1,0:T(2,128)S(1)}, s32[2]{0:T(128)S(1)}, /*index=5*/s32[...) while((s32[]{:T(128)}, f32[16,1326]{1,0:T(8,128)S(1)}, ...), condition=%wide.region_7.7_spmd.clone.clone.clone, body=%wide.region_5.6_spmd.sunk.clone.clone.clone.sunk | while | flops 116125776 | bytes 379492 | solution.py:77
  269.1 4.7 fusion.34
  292.7 22.8 %while.44 = (s32[]{:T(128)}, f32[16,1326]{1,0:T(8,128)S(1)}, f32[4,1326]{1,0:T(4,128)S(1)}, f32[2,1326]{1,0:T(2,128)S(1)}, s32[2]{0:T(128)S(1)}, /*index=5*/s32[...) while((s32[]{:T(128)}, f32[16,1326]{1,0:T(8,128)S(1)}, ...), condition=%wide.region_7.7_spmd.clone.clone.clone, body=%wide.region_5.6_spmd.sunk.clone.clone.clone.sunk | while | flops 116125776 | bytes 379492 | solution.py:77
  294.8 4.7 fusion.34
  318.3 22.8 %while.44 = (s32[]{:T(128)}, f32[16,1326]{1,0:T(8,128)S(1)}, f32[4,1326]{1,0:T(4,128)S(1)}, f32[2,1326]{1,0:T(2,128)S(1)}, s32[2]{0:T(128)S(1)}, /*index=5*/s32[...) while((s32[]{:T(128)}, f32[16,1326]{1,0:T(8,128)S(1)}, ...), condition=%wide.region_7.7_spmd.clone.clone.clone, body=%wide.region_5.6_spmd.sunk.clone.clone.clone.sunk | while | flops 116125776 | bytes 379492 | solution.py:77
  343.9 22.8 %while.44 = (s32[]{:T(128)}, f32[16,1326]{1,0:T(8,128)S(1)}, f32[4,1326]{1,0:T(4,128)S(1)}, f32[2,1326]{1,0:T(2,128)S(1)}, s32[2]{0:T(128)S(1)}, /*index=5*/s32[...) while((s32[]{:T(128)}, f32[16,1326]{1,0:T(8,128)S(1)}, ...), condition=%wide.region_7.7_spmd.clone.clone.clone, body=%wide.region_5.6_spmd.sunk.clone.clone.clone.sunk | while | flops 116125776 | bytes 379492 | solution.py:77
  369.6 22.8 %while.44 = (s32[]{:T(128)}, f32[16,1326]{1,0:T(8,128)S(1)}, f32[4,1326]{1,0:T(4,128)S(1)}, f32[2,1326]{1,0:T(2,128)S(1)}, s32[2]{0:T(128)S(1)}, /*index=5*/s32[...) while((s32[]{:T(128)}, f32[16,1326]{1,0:T(8,128)S(1)}, ...), condition=%wide.region_7.7_spmd.clone.clone.clone, body=%wide.region_5.6_spmd.sunk.clone.clone.clone.sunk | while | flops 116125776 | bytes 379492 | solution.py:77
  395.2 22.8 %while.44 = (s32[]{:T(128)}, f32[16,1326]{1,0:T(8,128)S(1)}, f32[4,1326]{1,0:T(4,128)S(1)}, f32[2,1326]{1,0:T(2,128)S(1)}, s32[2]{0:T(128)S(1)}, /*index=5*/s32[...) while((s32[]{:T(128)}, f32[16,1326]{1,0:T(8,128)S(1)}, ...), condition=%wide.region_7.7_spmd.clone.clone.clone, body=%wide.region_5.6_spmd.sunk.clone.clone.clone.sunk | while | flops 116125776 | bytes 379492 | solution.py:77
  420.8 22.8 %while.44 = (s32[]{:T(128)}, f32[16,1326]{1,0:T(8,128)S(1)}, f32[4,1326]{1,0:T(4,128)S(1)}, f32[2,1326]{1,0:T(2,128)S(1)}, s32[2]{0:T(128)S(1)}, /*index=5*/s32[...) while((s32[]{:T(128)}, f32[16,1326]{1,0:T(8,128)S(1)}, ...), condition=%wide.region_7.7_spmd.clone.clone.clone, body=%wide.region_5.6_spmd.sunk.clone.clone.clone.sunk | while | flops 116125776 | bytes 379492 | solution.py:77
  434.3 4.7 fusion.34
  448.4 11.9 %psum.14 = f32[2,4,1326]{2,1,0:T(4,128)S(1)} all-reduce(f32[2,4,1326]{2,1,0:T(4,128)S(1)} %pad_maximum_fusion), channel_id=1, replica_groups=mesh['flop'=64,'turn'=4] {'turn'}, use_global_device_ids=true, to_apply=%region_13.14 | all-reduce | flops 10608 | bytes 84864 | tf_op jit(solution)/shard_map/psum | solution.py:157
  461.0 248.1 %psum.15 = f32[2,1326]{1,0:T(2,128)} all-reduce(f32[2,1326]{1,0:T(2,128)S(1)} %maximum_multiply_fusion), channel_id=1, replica_groups=mesh['flop'=64,'turn'=4] {'flop'}, use_global_device_ids=true, to_apply=%region_16.17 | all-reduce | flops 2652 | bytes 21216 | tf_op jit(solution)/shard_map/psum | solution.py:162
  (521 shorter events, 297.9 us)
Async XLA Ops:
  7.2 12.7 %copy-start.5 = (f32[1,24,2,1326]{3,2,1,0:T(2,128)S(1)}, f32[1,24,2,1326]{3,2,1,0:T(2,128)}, u32[]{:S(2)}) copy-start(f32[1,24,2,1326]{3,2,1,0:T(2,128)} %param.21) | copy-start | bytes 763780
  7.2 97.7 %all-gather.3.cloned.1.call-start = ((), (), s32[]{:S(2)}) async-start(), calls=%async_computation | async-start | bytes 10813440 | tf_op jit(solution)/shard_map/all_gather | solution.py:139
  7.3 28.0 %copy-start.14 = (s32[1,24,2]{1,2,0:T(2,128)S(1)}, s32[1,24,2]{1,2,0:T(2,128)}, u32[]{:S(2)}) copy-start(s32[1,24,2]{1,2,0:T(2,128)} %param.20) | copy-start | bytes 580
  7.3 38.9 %copy-start.2 = (f32[1,4,1326]{2,1,0:T(4,128)S(1)}, f32[1,4,1326]{2,1,0:T(4,128)}, u32[]{:S(2)}) copy-start(f32[1,4,1326]{2,1,0:T(4,128)} %param.16) | copy-start | bytes 63652
  7.3 40.0 %copy-start.10 = (f32[2,1326]{1,0:T(2,128)S(1)}, f32[2,1326]{1,0:T(2,128)}, u32[]{:S(2)}) copy-start(f32[2,1326]{1,0:T(2,128)} %param.15) | copy-start | bytes 31828
  7.9 701.1 %all-gather.5.cloned.1.call-start = ((), (), s32[]{:S(2)}) async-start(), calls=%async_computation.1 | async-start | bytes 5857280 | tf_op jit(solution)/shard_map/all_gather | solution.py:155
  8.2 26.3 %copy-start.15 = (s32[4,1]{0,1:T(1,128)}, s32[4,1]{0,1:T(1,128)S(1)}, u32[]{:S(2)}) copy-start(s32[4,1]{0,1:T(1,128)S(1)} %reduce-window.4) | copy-start | bytes 52
  46.2 58.7 %copy-start.7 = (f32[1326]{0:T(1024)}, f32[1326]{0:T(1024)S(1)}, u32[]{:S(2)}) copy-start(f32[1326]{0:T(1024)S(1)} %reduce_sum.88) | copy-start | bytes 15916
  47.3 57.6 %copy-start.12 = (pred[13]{0:T(512)(128)(4,1)}, pred[13]{0:T(512)(128)(4,1)S(1)}, u32[]{:S(2)}) copy-start(pred[13]{0:T(512)(128)(4,1)S(1)} %get-tuple-element.460) | copy-start | bytes 43
  104.9 5.9 copy-start
  104.9 5.9 copy-start.1
  104.9 5.9 copy-start.4
  104.9 5.9 copy-start.6
  104.9 5.9 copy-start.9
  110.8 333.3 %copy-start.13 = (pred[13]{0:T(512)(128)(4,1)S(1)}, pred[13]{0:T(512)(128)(4,1)}, u32[]{:S(2)}) copy-start(pred[13]{0:T(512)(128)(4,1)} %broadcast_compare_fusion) | copy-start | bytes 43
  115.4 4.7 copy-start.11
  126.8 4.7 copy-start.11
  141.0 4.7 copy-start.11
  152.4 4.7 copy-start.11
  166.6 4.7 copy-start.11
  178.1 4.7 copy-start.11
  192.3 4.7 copy-start.11
  203.7 4.7 copy-start.11
  217.9 4.7 copy-start.11
  229.3 4.7 copy-start.11
  243.5 4.7 copy-start.11
  254.9 4.7 copy-start.11
  269.1 4.7 copy-start.11
  383.0 4.7 copy-start.11
  408.7 4.7 copy-start.11
  444.1 16.1 %copy-start.3 = (f32[1,4,1326]{2,1,0:T(4,128)S(1)}, f32[1,4,1326]{2,1,0:T(4,128)}, u32[]{:S(2)}) copy-start(f32[1,4,1326]{2,1,0:T(4,128)} %param.16) | copy-start | bytes 63652
  444.1 16.1 %copy-start.8 = (f32[1326]{0:T(1024)S(1)}, f32[1326]{0:T(1024)}, u32[]{:S(2)}) copy-start(f32[1326]{0:T(1024)} %copy-done.7) | copy-start | bytes 15916
  (17 other events, 60.4 us)
Sparse Core Ops, SparseCore 0:
  9.8 94.9 all-gather.2
  445.6 55.2 all-gather.4
where the time goes:
time: 727 us; the launch traced here: 722 us
  blocking collectives  294 us (40%)
  matrix products  243 us (33%)
  local copies, waits for them, and re-layouts  57.4 us (8%)
  waiting for transfers between devices  56.1 us (8%)
  other arithmetic  53.1 us (7%)
  between operations  16.5 us (2%)
    psum x1, blocking collectives, on_device(): root_value = lax.psum(jnp.stack([node_zero, node_one]) / flop_devs, 'flop')  248 us
    dot_general x26, matrix products, river_step(): lax.dot_general(reach_other, outcome, (((1,), (1,)), ((), ())), preferred...  122 us
    dot_general x26, matrix products, river_step(): against = jnp.dot(reach_zero, outcome, preferred_element_type=jnp.float32)  121 us
    all_gather x1, waiting for transfers between devices, on_device(): lax.all_gather(turn_regret, 'turn', axis=1, tiled=True)  55.5 us
    concatenate x26, other arithmetic, river_step(): jnp.concatenate([early, river_id[None]])  34.3 us
    squeeze x39, local copies, waits for them, and re-layouts, run_slots(): lax.map(one_slot, (turn_ids, river_ids, strengths, regrets))  18.7 us
    dynamic_slice x52, local copies, waits for them, and re-layouts, slot_terms(): (toward, against), _ = lax.scan(river_step, start, (river_ids, strengths))  15.8 us
    all_gather x1, blocking collectives, on_device(): lax.all_gather(strength, 'turn', axis=1, tiled=True)  14.7 us
  transfers between devices with their start and end apart: 2, of which 1 were waited for; matrix products, arithmetic and copies ran while one was open for 1% of the time, Pallas kernels for 0%

commit v1 on v0

v1 whole, which is shorter than its diff:
```python
import jax
import jax.numpy as jnp
import numpy as np
from jax import lax
from jax.experimental import pallas as pl
from jax.experimental.pallas import tpu as pltpu
from jax.sharding import PartitionSpec as P

CARDS = 52
H = 1326
HP = 1408
A = 4
TURNS = 49
TS = 24
RIV = 2
FLOPS = 64
BLOCK = 256
BIG = 2.0**126

bet_sizes = (0.25, 0.5, 1.0, 2.0)
card_low, card_high = np.triu_indices(CARDS, 1)
growth = 1.0 + 2.0 * np.asarray(bet_sizes)
pot = (np.outer(growth, growth) / (2.0 * H * RIV)).astype(np.float32)


def tables():
    alive = np.ones((56, HP), np.float32)
    for card in range(CARDS):
        alive[card, :H] = (card_low != card) & (card_high != card)
    alive[:, H:] = 0.0
    disjoint = np.zeros((HP, HP), np.float32)
    disjoint[:H, :H] = (
        (card_low[:, None] != card_low[None, :])
        & (card_low[:, None] != card_high[None, :])
        & (card_high[:, None] != card_low[None, :])
        & (card_high[:, None] != card_high[None, :])
    )
    return alive, disjoint.astype(jnp.bfloat16)


BLOCKS = [(start, min(BLOCK, 1328 - start)) for start in range(0, HP, BLOCK)]


def swap_halves(x):
    return jnp.concatenate([x[4:8], x[0:4]], axis=0)


def rounded(x):
    return x.astype(jnp.bfloat16).astype(jnp.float32)


def kernel(
    flop_cards, live_turns, turn_card, river_cards,
    ranges_in, flop_regret_in, strength_in, turn_regret, alive_in, keep_in,
    new_turn, sums, root,
    ranges, flop_regret, strength, alive_table, keep, lose,
    regrets, reach, strong_in, strong_out, found, total, one_total, spread, blank,
    small_sems, keep_sems, in_sems, out_sems,
):
    me = lax.axis_index("turn")
    count = live_turns[0, me]

    def regret_copy(slot, b):
        return pltpu.make_async_copy(
            turn_regret.at[0, slot, :, b],
            regrets.at[slot, b // 2, pl.ds((b % 2) * 4, 4)],
            in_sems.at[slot, b],
        )

    def result_copy(slot, b):
        return pltpu.make_async_copy(
            regrets.at[slot, b // 2, pl.ds((b % 2) * 4, 4)],
            new_turn.at[0, slot, :, b],
            out_sems.at[slot, b],
        )

    def blank_copy(slot):
        return pltpu.make_async_copy(blank, new_turn.at[0, slot], out_sems.at[slot, 0])

    small = [
        pltpu.make_async_copy(source, target, small_sems.at[n])
        for n, (source, target) in enumerate(
            [
                (ranges_in, ranges),
                (flop_regret_in, flop_regret),
                (alive_in, alive_table),
                (strength_in, strength),
            ]
        )
    ]
    masks = [
        pltpu.make_async_copy(
            keep_in.at[pl.ds(start, BLOCK if start + BLOCK <= HP else 128)],
            keep.at[pl.ds(start, BLOCK if start + BLOCK <= HP else 128)],
            keep_sems.at[n],
        )
        for n, (start, rows) in enumerate(BLOCKS)
    ]
    for copy in small:
        copy.start()
    for b in range(A):
        regret_copy(0, b).start()
    for copy in masks:
        copy.start()

    def fetch(slot, carry):
        for b in range(A):
            regret_copy(slot, b).start()
        return carry

    lax.fori_loop(1, count, fetch, 0)
    blank[...] = jnp.zeros_like(blank)

    def clear(slot, carry):
        blank_copy(slot).start()
        return carry

    lax.fori_loop(count, TS, clear, 0)
    reach[...] = jnp.zeros_like(reach)
    strong_in[...] = jnp.zeros_like(strong_in)
    total[...] = jnp.zeros_like(total)
    one_total[...] = jnp.zeros_like(one_total)
    for copy in small:
        copy.wait()

    regrets_flop = flop_regret[0]
    sigma_flop = regrets_flop / jnp.sum(regrets_flop, axis=0, keepdims=True)
    reach_zero = rounded(ranges[0:1, :] * sigma_flop)
    reach[8:16, :H] = jnp.concatenate([reach_zero, reach_zero], axis=0)
    flop_alive = (
        alive_table[pl.ds(flop_cards[0, 0], 1), :]
        * alive_table[pl.ds(flop_cards[0, 1], 1), :]
        * alive_table[pl.ds(flop_cards[0, 2], 1), :]
    )
    row = lax.broadcasted_iota(jnp.int32, (8, 1), 0)
    upper = row < 4
    pots = []
    for k in range(2):
        column = jnp.zeros((8, 1), jnp.float32)
        for n in range(8):
            column = jnp.where(row == n, float(pot[n % 4, 2 * k + n // 4]), column)
        pots.append(column)
    for n, (start, rows) in enumerate(BLOCKS):
        masks[n].wait()
        lose[start : start + rows, :] = -keep[start : start + rows, :]

    def slot_step(slot, carry):
        for b in range(A):
            regret_copy(slot, b).wait()
        first, second = regrets[slot, 0], regrets[slot, 1]
        summed = first + second
        inverse = 1.0 / (summed + swap_halves(summed))
        sigma_first, sigma_second = first * inverse, second * inverse
        second_range = ranges[1:2, :]
        weight = (
            rounded(second_range * sigma_first) * pots[0]
            + rounded(second_range * sigma_second) * pots[1]
        )
        weight = weight + swap_halves(weight)
        reach[0:8, :H] = jnp.where(upper, weight, weight - rounded(weight))
        spreading = sigma_first * pots[0] + sigma_second * pots[1]
        spread[...] = spreading + swap_halves(spreading)
        strong_in[0:RIV, :H] = strength[0, slot] * BIG
        strong_out[...] = strong_in[...].T
        turn_alive = flop_alive * alive_table[pl.ds(turn_card[0, slot], 1), :]
        for r in range(RIV):
            alive = turn_alive * alive_table[pl.ds(river_cards[0, r, slot], 1), :]
            given = (reach[...] * alive).astype(jnp.bfloat16)
            for start, rows in BLOCKS:
                own = jnp.broadcast_to(strong_out[start : start + rows, r : r + 1], (rows, 128))
                for other in range(0, HP, BLOCK):
                    stop = min(other + BLOCK, HP)
                    gap = jnp.concatenate(
                        [
                            own - strong_in[r : r + 1, lane : lane + 128]
                            for lane in range(other, stop, 128)
                        ],
                        axis=1,
                    ).astype(jnp.bfloat16)
                    outcome = jnp.maximum(
                        jnp.minimum(gap, keep[start : start + rows, other:stop]),
                        lose[start : start + rows, other:stop],
                    )
                    gave = jnp.dot(
                        given[:, start : start + rows], outcome,
                        preferred_element_type=jnp.float32,
                    )
                    if start == 0:
                        found[r, :, other:stop] = gave
                    else:
                        found[r, :, other:stop] += gave
            if r == 0:
                values = found[r] * -alive
            else:
                values = values + found[r] * -alive
        total[...] += values[0:8, :]
        against = values[8:16, :H]
        spreading = spread[...]
        one_total[...] += against * spreading
        for k in range(2):
            regrets[slot, k] = jnp.maximum(
                regrets[slot, k] + against * (pots[k] - spreading), 0.0
            )
        for b in range(A):
            result_copy(slot, b).start()
        return carry

    lax.fori_loop(0, count, slot_step, 0)
    whole = total[0:4, :H] + total[4:8, :H]
    sums[0:4, :] = whole
    scale = 1.0 / (TURNS * FLOPS)
    sums[4:5, :] = jnp.sum(sigma_flop * whole, axis=0, keepdims=True) * scale
    sums[5:6, :] = jnp.sum(one_total[0:4, :], axis=0, keepdims=True) * scale
    root[...] = sigma_flop

    def settle(slot, carry):
        for b in range(A):
            result_copy(slot, b).wait()
        return carry

    lax.fori_loop(0, count, settle, 0)

    def settle_blank(slot, carry):
        blank_copy(slot).wait()
        return carry

    lax.fori_loop(count, TS, settle_blank, 0)


def exchange(x, axis, flips):
    size = lax.axis_size(axis)
    for flip in flips:
        if flip < size:
            x = x + lax.ppermute(x, axis, [(n, n ^ flip) for n in range(size)])
    return x


def on_device(
    ranges, flop_regret, flop_cards, live_turns, turn_card, river_cards, strength, turn_regret
):
    alive, disjoint = tables()
    smem = pl.BlockSpec(memory_space=pltpu.SMEM)
    vmem = pl.BlockSpec(memory_space=pltpu.VMEM)
    hbm = pl.BlockSpec(memory_space=pltpu.HBM)
    new_turn, sums, sigma_flop = pl.pallas_call(
        kernel,
        out_shape=(
            jax.ShapeDtypeStruct(turn_regret.shape, jnp.float32),
            jax.ShapeDtypeStruct((6, H), jnp.float32),
            jax.ShapeDtypeStruct((A, H), jnp.float32),
        ),
        in_specs=[smem] * 4 + [hbm] * 6,
        out_specs=(hbm, vmem, vmem),
        scratch_shapes=[
            pltpu.VMEM((2, H), jnp.float32),
            pltpu.VMEM((1, A, H), jnp.float32),
            pltpu.VMEM((1, TS, RIV, H), jnp.float32),
            pltpu.VMEM((56, HP), jnp.float32),
            pltpu.VMEM((HP, HP), jnp.bfloat16),
            pltpu.VMEM((HP, HP), jnp.bfloat16),
            pltpu.VMEM((TS, 2, 8, H), jnp.float32),
            pltpu.VMEM((16, HP), jnp.float32),
            pltpu.VMEM((8, HP), jnp.float32),
            pltpu.VMEM((HP, 8), jnp.float32),
            pltpu.VMEM((RIV, 16, HP), jnp.float32),
            pltpu.VMEM((8, HP), jnp.float32),
            pltpu.VMEM((8, H), jnp.float32),
            pltpu.VMEM((8, H), jnp.float32),
            pltpu.VMEM((A, A, H), jnp.float32),
            pltpu.SemaphoreType.DMA((4,)),
            pltpu.SemaphoreType.DMA((len(BLOCKS),)),
            pltpu.SemaphoreType.DMA((TS, A)),
            pltpu.SemaphoreType.DMA((TS, A)),
        ],
        compiler_params=pltpu.CompilerParams(vmem_limit_bytes=60 * 1024 * 1024),
        name="subtrees",
    )(
        flop_cards, live_turns, turn_card, jnp.swapaxes(river_cards, 1, 2),
        ranges, flop_regret, strength, turn_regret, jnp.asarray(alive), jnp.asarray(disjoint),
    )
    regrets_flop = flop_regret[0]
    turns = exchange(sums, "turn", (1, 2))
    action_value = turns[0:4] / TURNS
    node_zero = jnp.sum(sigma_flop * action_value, axis=0)
    new_flop = jnp.maximum(regrets_flop + action_value - node_zero[None, :], 0.0)
    root_value = exchange(turns[4:6], "flop", (1, 2, 4, 8, 16, 32))
    return (new_flop[None], new_turn, root_value)


def solution(mesh):
    placed = (
        P(),
        P("flop", None, None),
        P("flop", None),
        P("flop", None),
        P("flop", "turn"),
        P("flop", "turn", None),
        P("flop", "turn", None, None),
        P("flop", "turn", None, None, None),
    )
    return jax.shard_map(
        on_device,
        mesh=mesh,
        in_specs=placed,
        out_specs=(P("flop", None, None), P("flop", "turn", None, None, None), P()),
        check_vma=False,
    )
```

time: 727 us -> 95.5 us (0.13)
  the two profiles are of different devices: /device:TPU:1 before, /device:TPU:2 now
where the time goes in v1:
time: 95.5 us; the launch traced here: 95.3 us
  Pallas kernels  55.6 us (58%)
  waiting for transfers between devices  21.2 us (22%)
  starting transfers between devices  15 us (16%)
  other arithmetic  2.84 us (3%)
    pallas_call x1, Pallas kernels, on_device(): pl.pallas_call(kernel, out_shape=(jax.ShapeDtypeStruct(turn_regret.shape,...  55.6 us
    ppermute x8, waiting for transfers between devices, exchange(): x = x + lax.ppermute(x, axis, [(n, n ^ flip) for n in range(size)])  21.2 us
    ppermute x8, starting transfers between devices, exchange(): x = x + lax.ppermute(x, axis, [(n, n ^ flip) for n in range(size)])  15 us
  transfers between devices with their start and end apart: 8, of which 8 were waited for; matrix products, arithmetic and copies ran while one was open for 1% of the time, Pallas kernels for 0%

profile of v1, /device:TPU:2, one launch (start us, length us, event | category | flops | bytes accessed | tf_op | source)
XLA Modules:
  0.0 95.3 jit_solution(12287553868326097716)
XLA Ops:
  0.6 0.0 copy-start
  0.6 55.6 %subtrees.1 = (f32[1,24,4,4,1326]{4,3,2,1,0:T(4,128)}, f32[6,1326]{1,0:T(8,128)}, f32[4,1326]{1,0:T(4,128)}) custom-call(s32[1,3]{1,0:T(1,128)} %flop_cards.1, s32[1,4]{1,0:T(1,128)} %live_turns.1, s32[1,24]{1,0:T(1,128)} %turn_card.1, s32[1,2,24]{2,1,0:T(2,128)} %bitcast.11, f32[2,1326]{1,0:T(2,128)} %ranges_in.1, f32[1,4,1326]{2,1,0:T(4,128)} %flop_regret_in.1, ...), custom_call_target="tpu_custom_call" | custom-call | tf_op jit(solution)/shard_map/subtrees/pallas_call | solution.py:245
  56.2 0.1 collective-permute-start
  56.3 4.2 %collective-permute-done = f32[6,1326]{1,0:T(8,128)S(1)} collective-permute-done((f32[6,1326]{1,0:T(8,128)}, f32[6,1326]{1,0:T(8,128)S(1)}, u32[]{:S(2)}, u32[]{:S(2)}) %collective-permute-start) | collective-permute-done | bytes 31856 | tf_op jit(solution)/shard_map/ppermute | solution.py:234
  60.6 0.8 add.27
  61.4 0.0 collective-permute-start.1
  61.4 5.5 %collective-permute-done.1 = f32[6,1326]{1,0:T(8,128)S(1)} collective-permute-done((f32[6,1326]{1,0:T(8,128)S(1)}, f32[6,1326]{1,0:T(8,128)S(1)}, u32[]{:S(2)}, u32[]{:S(2)}) %collective-permute-start.1) | collective-permute-done | bytes 31856 | tf_op jit(solution)/shard_map/ppermute | solution.py:234
  67.0 0.1 collective-permute-start.2
  67.1 1.2 %collective-permute-done.2 = f32[2,1326]{1,0:T(2,128)S(1)} collective-permute-done((f32[2,1326]{1,0:T(2,128)S(1)}, f32[2,1326]{1,0:T(2,128)S(1)}, u32[]{:S(2)}, u32[]{:S(2)}) %collective-permute-start.2) | collective-permute-done | bytes 10640 | tf_op jit(solution)/shard_map/ppermute | solution.py:234
  68.2 0.3 collective-permute-start.3
  68.5 3.5 %collective-permute-done.3 = f32[2,1326]{1,0:T(2,128)S(1)} collective-permute-done((f32[2,1326]{1,0:T(2,128)S(1)}, f32[2,1326]{1,0:T(2,128)S(1)}, u32[]{:S(2)}, u32[]{:S(2)}) %collective-permute-start.3) | collective-permute-done | bytes 10640 | tf_op jit(solution)/shard_map/ppermute | solution.py:234
  72.0 2.2 %collective-permute-start.4 = (f32[2,1326]{1,0:T(2,128)S(1)}, f32[2,1326]{1,0:T(2,128)S(1)}, u32[]{:S(2)}, u32[]{:S(2)}) collective-permute-start(f32[2,1326]{1,0:T(2,128)S(1)} %add.31), channel_id=1, source_target_pairs={{0,16},{4,20},{8,24},{12,28},{16,0},{20,4},{24,8},{28,12},{32,48},... | collective-permute-start | bytes 31832 | tf_op jit(solution)/shard_map/ppermute | solution.py:234
  74.2 3.1 %collective-permute-done.4 = f32[2,1326]{1,0:T(2,128)S(1)} collective-permute-done((f32[2,1326]{1,0:T(2,128)S(1)}, f32[2,1326]{1,0:T(2,128)S(1)}, u32[]{:S(2)}, u32[]{:S(2)}) %collective-permute-start.4) | collective-permute-done | bytes 10640 | tf_op jit(solution)/shard_map/ppermute | solution.py:234
  77.3 2.0 %collective-permute-start.5 = (f32[2,1326]{1,0:T(2,128)S(1)}, f32[2,1326]{1,0:T(2,128)S(1)}, u32[]{:S(2)}, u32[]{:S(2)}) collective-permute-start(f32[2,1326]{1,0:T(2,128)S(1)} %add.32), channel_id=1, source_target_pairs={{0,32},{4,36},{8,40},{12,44},{16,48},{20,52},{24,56},{28,60},{32,0... | collective-permute-start | bytes 31832 | tf_op jit(solution)/shard_map/ppermute | solution.py:234
  79.3 1.8 %collective-permute-done.5 = f32[2,1326]{1,0:T(2,128)S(1)} collective-permute-done((f32[2,1326]{1,0:T(2,128)S(1)}, f32[2,1326]{1,0:T(2,128)S(1)}, u32[]{:S(2)}, u32[]{:S(2)}) %collective-permute-start.5) | collective-permute-done | bytes 10640 | tf_op jit(solution)/shard_map/ppermute | solution.py:234
  81.1 3.4 %collective-permute-start.6 = (f32[2,1326]{1,0:T(2,128)S(1)}, f32[2,1326]{1,0:T(2,128)S(1)}, u32[]{:S(2)}, u32[]{:S(2)}) collective-permute-start(f32[2,1326]{1,0:T(2,128)S(1)} %add.33), channel_id=1, source_target_pairs={{0,64},{4,68},{8,72},{12,76},{16,80},{20,84},{24,88},{28,92},{32,9... | collective-permute-start | bytes 31832 | tf_op jit(solution)/shard_map/ppermute | solution.py:234
  84.4 0.8 multiply_reduce_fusion
  85.2 0.9 collective-permute-done.6
  86.1 6.9 %collective-permute-start.7 = (f32[2,1326]{1,0:T(2,128)S(1)}, f32[2,1326]{1,0:T(2,128)S(1)}, u32[]{:S(2)}, u32[]{:S(2)}) collective-permute-start(f32[2,1326]{1,0:T(2,128)S(1)} %add.34), channel_id=1, source_target_pairs={{0,128},{4,132},{8,136},{12,140},{16,144},{20,148},{24,152},{28,15... | collective-permute-start | bytes 31832 | tf_op jit(solution)/shard_map/ppermute | solution.py:234
  93.0 0.0 copy-done
  93.0 0.6 fusion.2
  93.6 1.0 %collective-permute-done.7 = f32[2,1326]{1,0:T(2,128)S(1)} collective-permute-done((f32[2,1326]{1,0:T(2,128)S(1)}, f32[2,1326]{1,0:T(2,128)S(1)}, u32[]{:S(2)}, u32[]{:S(2)}) %collective-permute-start.7) | collective-permute-done | bytes 10640 | tf_op jit(solution)/shard_map/ppermute | solution.py:234
  94.7 0.6 add.35
  (7 shorter events, 0.1 us)
Async XLA Ops:
  0.6 92.4 %copy-start = (f32[1,4,1326]{2,1,0:T(4,128)S(1)}, f32[1,4,1326]{2,1,0:T(4,128)}, u32[]{:S(2)}) copy-start(f32[1,4,1326]{2,1,0:T(4,128)} %flop_regret_in.1) | copy-start | bytes 63652
  56.2 4.3 %collective-permute-start = (f32[6,1326]{1,0:T(8,128)}, f32[6,1326]{1,0:T(8,128)S(1)}, u32[]{:S(2)}, u32[]{:S(2)}) collective-permute-start(f32[6,1326]{1,0:T(8,128)} %get-tuple-element.6), channel_id=1, source_target_pairs={{0,1},{1,0},{2,3},{3,2},{4,5},{5,4},{6,7},{7,6},{8,9},{9,8},{10,11... | collective-permute-start | bytes 95480 | tf_op jit(solution)/shard_map/ppermute | solution.py:234
  61.4 5.6 %collective-permute-start.1 = (f32[6,1326]{1,0:T(8,128)S(1)}, f32[6,1326]{1,0:T(8,128)S(1)}, u32[]{:S(2)}, u32[]{:S(2)}) collective-permute-start(f32[6,1326]{1,0:T(8,128)S(1)} %add.27), channel_id=1, source_target_pairs={{0,2},{1,3},{2,0},{3,1},{4,6},{5,7},{6,4},{7,5},{8,10},{9,11},{10,... | collective-permute-start | bytes 95480 | tf_op jit(solution)/shard_map/ppermute | solution.py:234
  67.0 1.3 %collective-permute-start.2 = (f32[2,1326]{1,0:T(2,128)S(1)}, f32[2,1326]{1,0:T(2,128)S(1)}, u32[]{:S(2)}, u32[]{:S(2)}) collective-permute-start(f32[2,1326]{1,0:T(2,128)S(1)} %slice.9), channel_id=1, source_target_pairs={{0,4},{4,0},{8,12},{12,8},{16,20},{20,16},{24,28},{28,24},{32,36},... | collective-permute-start | bytes 31832 | tf_op jit(solution)/shard_map/ppermute | solution.py:234
  68.2 3.8 %collective-permute-start.3 = (f32[2,1326]{1,0:T(2,128)S(1)}, f32[2,1326]{1,0:T(2,128)S(1)}, u32[]{:S(2)}, u32[]{:S(2)}) collective-permute-start(f32[2,1326]{1,0:T(2,128)S(1)} %slice_add_fusion), channel_id=1, source_target_pairs={{0,8},{4,12},{8,0},{12,4},{16,24},{20,28},{24,16},{28,20},{32,40},... | collective-permute-start | bytes 31832 | tf_op jit(solution)/shard_map/ppermute | solution.py:234
  72.0 5.3 %collective-permute-start.4 = (f32[2,1326]{1,0:T(2,128)S(1)}, f32[2,1326]{1,0:T(2,128)S(1)}, u32[]{:S(2)}, u32[]{:S(2)}) collective-permute-start(f32[2,1326]{1,0:T(2,128)S(1)} %add.31), channel_id=1, source_target_pairs={{0,16},{4,20},{8,24},{12,28},{16,0},{20,4},{24,8},{28,12},{32,48},... | collective-permute-start | bytes 31832 | tf_op jit(solution)/shard_map/ppermute | solution.py:234
  77.3 3.8 %collective-permute-start.5 = (f32[2,1326]{1,0:T(2,128)S(1)}, f32[2,1326]{1,0:T(2,128)S(1)}, u32[]{:S(2)}, u32[]{:S(2)}) collective-permute-start(f32[2,1326]{1,0:T(2,128)S(1)} %add.32), channel_id=1, source_target_pairs={{0,32},{4,36},{8,40},{12,44},{16,48},{20,52},{24,56},{28,60},{32,0... | collective-permute-start | bytes 31832 | tf_op jit(solution)/shard_map/ppermute | solution.py:234
  81.1 5.0 %collective-permute-start.6 = (f32[2,1326]{1,0:T(2,128)S(1)}, f32[2,1326]{1,0:T(2,128)S(1)}, u32[]{:S(2)}, u32[]{:S(2)}) collective-permute-start(f32[2,1326]{1,0:T(2,128)S(1)} %add.33), channel_id=1, source_target_pairs={{0,64},{4,68},{8,72},{12,76},{16,80},{20,84},{24,88},{28,92},{32,9... | collective-permute-start | bytes 31832 | tf_op jit(solution)/shard_map/ppermute | solution.py:234
  86.1 8.6 %collective-permute-start.7 = (f32[2,1326]{1,0:T(2,128)S(1)}, f32[2,1326]{1,0:T(2,128)S(1)}, u32[]{:S(2)}, u32[]{:S(2)}) collective-permute-start(f32[2,1326]{1,0:T(2,128)S(1)} %add.34), channel_id=1, source_target_pairs={{0,128},{4,132},{8,136},{12,140},{16,144},{20,148},{24,152},{28,15... | collective-permute-start | bytes 31832 | tf_op jit(solution)/shard_map/ppermute | solution.py:234

commit v2 on v1

--- a/solution.py
+++ b/solution.py
@@ -9,6 +9,9 @@
 CARDS = 52
 H = 1326
 HP = 1408
+LEFT = 48
+C = 1128
+CP = 1152
 A = 4
 TURNS = 49
 TS = 24
@@ -23,22 +26,33 @@
 pot = (np.outer(growth, growth) / (2.0 * H * RIV)).astype(np.float32)
 
 
+def spread_rows(values, rows, fill):
+    out = np.full((rows * 128,), fill, np.int32)
+    out[: len(values)] = values
+    return out.reshape(rows, 128)
+
+
 def tables():
-    alive = np.ones((56, HP), np.float32)
-    for card in range(CARDS):
-        alive[card, :H] = (card_low != card) & (card_high != card)
-    alive[:, H:] = 0.0
-    disjoint = np.zeros((HP, HP), np.float32)
-    disjoint[:H, :H] = (
-        (card_low[:, None] != card_low[None, :])
-        & (card_low[:, None] != card_high[None, :])
-        & (card_high[:, None] != card_low[None, :])
-        & (card_high[:, None] != card_high[None, :])
-    )
-    return alive, disjoint.astype(jnp.bfloat16)
-
-
-BLOCKS = [(start, min(BLOCK, 1328 - start)) for start in range(0, HP, BLOCK)]
+    low, high = np.triu_indices(LEFT, 1)
+    index = np.stack(
+        [
+            spread_rows(low, 16, 0),
+            spread_rows(high, 16, 1),
+            spread_rows(card_low, 16, 0),
+            spread_rows(card_high, 16, 1),
+        ]
+    )
+    disjoint = np.zeros((CP, CP), np.float32)
+    disjoint[:C, :C] = (
+        (low[:, None] != low[None, :])
+        & (low[:, None] != high[None, :])
+        & (high[:, None] != low[None, :])
+        & (high[:, None] != high[None, :])
+    )
+    return index, disjoint.astype(jnp.bfloat16)
+
+
+BLOCKS = [(start, min(BLOCK, 1136 - start)) for start in range(0, CP, BLOCK)]
 
 
 def swap_halves(x):
@@ -51,10 +65,10 @@
 
 def kernel(
     flop_cards, live_turns, turn_card, river_cards,
-    ranges_in, flop_regret_in, strength_in, turn_regret, alive_in, keep_in,
+    ranges_in, flop_regret_in, strength_in, turn_regret, index_in, keep_in,
     new_turn, sums, root,
-    ranges, flop_regret, strength, alive_table, keep, lose,
-    regrets, reach, strong_in, strong_out, found, total, one_total, spread, blank,
+    ranges, flop_regret, strength, index, keep,
+    regrets, wide, lane, alive, columns, found, back, total, one_total, spread, blank,
     small_sems, keep_sems, in_sems, out_sems,
 ):
     me = lax.axis_index("turn")
@@ -83,15 +97,15 @@
             [
                 (ranges_in, ranges),
                 (flop_regret_in, flop_regret),
-                (alive_in, alive_table),
+                (index_in, index),
                 (strength_in, strength),
             ]
         )
     ]
     masks = [
         pltpu.make_async_copy(
-            keep_in.at[pl.ds(start, BLOCK if start + BLOCK <= HP else 128)],
-            keep.at[pl.ds(start, BLOCK if start + BLOCK <= HP else 128)],
+            keep_in.at[pl.ds(start, BLOCK if start + BLOCK <= CP else 128)],
+            keep.at[pl.ds(start, BLOCK if start + BLOCK <= CP else 128)],
             keep_sems.at[n],
         )
         for n, (start, rows) in enumerate(BLOCKS)
@@ -116,8 +130,8 @@
         return carry
 
     lax.fori_loop(count, TS, clear, 0)
-    reach[...] = jnp.zeros_like(reach)
-    strong_in[...] = jnp.zeros_like(strong_in)
+    wide[...] = jnp.zeros_like(wide)
+    back[...] = jnp.zeros_like(back)
     total[...] = jnp.zeros_like(total)
     one_total[...] = jnp.zeros_like(one_total)
     for copy in small:
@@ -126,12 +140,11 @@
     regrets_flop = flop_regret[0]
     sigma_flop = regrets_flop / jnp.sum(regrets_flop, axis=0, keepdims=True)
     reach_zero = rounded(ranges[0:1, :] * sigma_flop)
-    reach[8:16, :H] = jnp.concatenate([reach_zero, reach_zero], axis=0)
-    flop_alive = (
-        alive_table[pl.ds(flop_cards[0, 0], 1), :]
-        * alive_table[pl.ds(flop_cards[0, 1], 1), :]
-        * alive_table[pl.ds(flop_cards[0, 2], 1), :]
-    )
+    wide[1, 0:4, :H] = reach_zero
+    first_card, second_card, third_card = (flop_cards[0, n] for n in range(3))
+    first_card, second_card = jnp.minimum(first_card, second_card), jnp.maximum(first_card, second_card)
+    second_card, third_card = jnp.minimum(second_card, third_card), jnp.maximum(second_card, third_card)
+    first_card, second_card = jnp.minimum(first_card, second_card), jnp.maximum(first_card, second_card)
     row = lax.broadcasted_iota(jnp.int32, (8, 1), 0)
     upper = row < 4
     pots = []
@@ -140,9 +153,8 @@
         for n in range(8):
             column = jnp.where(row == n, float(pot[n % 4, 2 * k + n // 4]), column)
         pots.append(column)
-    for n, (start, rows) in enumerate(BLOCKS):
-        masks[n].wait()
-        lose[start : start + rows, :] = -keep[start : start + rows, :]
+    for copy in masks:
+        copy.wait()
 
     def slot_step(slot, carry):
         for b in range(A):
@@ -157,44 +169,106 @@
             + rounded(second_range * sigma_second) * pots[1]
         )
         weight = weight + swap_halves(weight)
-        reach[0:8, :H] = jnp.where(upper, weight, weight - rounded(weight))
+        wide[0, :, :H] = jnp.where(upper, weight, weight - rounded(weight))
         spreading = sigma_first * pots[0] + sigma_second * pots[1]
         spread[...] = spreading + swap_halves(spreading)
-        strong_in[0:RIV, :H] = strength[0, slot] * BIG
-        strong_out[...] = strong_in[...].T
-        turn_alive = flop_alive * alive_table[pl.ds(turn_card[0, slot], 1), :]
+        wide[1, 4:6, :H] = strength[0, slot] * BIG
+
+        dead, card = [], turn_card[0, slot]
+        for flop_card in (first_card, second_card, third_card):
+            dead.append(jnp.minimum(flop_card, card))
+            card = jnp.maximum(flop_card, card)
+        dead.append(card)
+        low, high = index[0], index[1]
+        for card in dead:
+            low = low + (low >= card).astype(jnp.int32)
+            high = high + (high >= card).astype(jnp.int32)
+        lane[0] = ((low * (2 * CARDS - 1 - low)) >> 1) + high - low - 1
         for r in range(RIV):
-            alive = turn_alive * alive_table[pl.ds(river_cards[0, r, slot], 1), :]
-            given = (reach[...] * alive).astype(jnp.bfloat16)
-            for start, rows in BLOCKS:
-                own = jnp.broadcast_to(strong_out[start : start + rows, r : r + 1], (rows, 128))
-                for other in range(0, HP, BLOCK):
-                    stop = min(other + BLOCK, HP)
+            river = river_cards[0, r, slot]
+            alive[r] = jnp.where((low == river) | (high == river), 0.0, -1.0)
+        low, high = index[2], index[3]
+        lost = (low == dead[0]) | (high == dead[0])
+        for card in dead[1:]:
+            lost = lost | (low == card) | (high == card)
+        less_low, less_high = jnp.zeros_like(low), jnp.zeros_like(high)
+        for card in dead:
+            less_low = less_low + (low > card).astype(jnp.int32)
+            less_high = less_high + (high > card).astype(jnp.int32)
+        low, high = low - less_low, high - less_high
+        place = ((low * (2 * LEFT - 1 - low)) >> 1) + high - low - 1
+        lane[1] = jnp.where(lost, -1, place)
+
+        packed = [[], []]
+        for k in range(CP // 128):
+            offset = jnp.broadcast_to(lane[0, k : k + 1, :], (8, 128)) - 128 * k
+            spot = offset & 127
+            for group in range(2):
+                parts = [
+                    jnp.take_along_axis(
+                        wide[group, :, 128 * (k + m) : 128 * (k + m + 1)], spot, axis=1
+                    )
+                    for m in range(3)
+                ]
+                packed[group].append(
+                    jnp.where(offset < 128, parts[0], jnp.where(offset < 256, parts[1], parts[2]))
+                )
+        columns[...] = jnp.concatenate(packed[1], axis=1).T
+        given = []
+        for r in range(RIV):
+            pieces = []
+            for k in range(CP // 128):
+                mask = -alive[r, k : k + 1, :]
+                zeros = jnp.where(upper, packed[1][k], swap_halves(packed[1][k]))
+                pieces.append(
+                    jnp.concatenate([packed[0][k] * mask, zeros * mask], axis=0).astype(jnp.bfloat16)
+                )
+            given.append(jnp.concatenate(pieces, axis=1))
+        for start, rows in BLOCKS:
+            own = [
+                jnp.broadcast_to(columns[start : start + rows, 4 + r : 5 + r], (rows, 128))
+                for r in range(RIV)
+            ]
+            for other in range(0, CP, BLOCK):
+                stop = min(other + BLOCK, CP)
+                most = keep[start : start + rows, other:stop]
+                least = -most
+                for r in range(RIV):
                     gap = jnp.concatenate(
                         [
-                            own - strong_in[r : r + 1, lane : lane + 128]
-                            for lane in range(other, stop, 128)
+                            own[r] - packed[1][k][4 + r : 5 + r, :]
+                            for k in range(other // 128, stop // 128)
                         ],
                         axis=1,
                     ).astype(jnp.bfloat16)
-                    outcome = jnp.maximum(
-                        jnp.minimum(gap, keep[start : start + rows, other:stop]),
-                        lose[start : start + rows, other:stop],
-                    )
+                    outcome = jnp.maximum(jnp.minimum(gap, most), least)
                     gave = jnp.dot(
-                        given[:, start : start + rows], outcome,
+                        given[r][:, start : start + rows], outcome,
                         preferred_element_type=jnp.float32,
                     )
                     if start == 0:
                         found[r, :, other:stop] = gave
                     else:
                         found[r, :, other:stop] += gave
-            if r == 0:
-                values = found[r] * -alive
-            else:
-                values = values + found[r] * -alive
-        total[...] += values[0:8, :]
-        against = values[8:16, :H]
+        merged = []
+        for k in range(CP // 128):
+            values = [
+                found[r, :, 128 * k : 128 * (k + 1)] * alive[r, k : k + 1, :] for r in range(RIV)
+            ]
+            values = values[0] + values[1]
+            merged.append(
+                jnp.where(upper, values[0:8] + swap_halves(values[0:8]), values[8:16])
+            )
+        for k in range(HP // 128):
+            place = jnp.broadcast_to(lane[1, k : k + 1, :], (8, 128))
+            spot = place & 127
+            result = jnp.zeros((8, 128), jnp.float32)
+            for m in range(max(0, k - 2), min(k + 1, CP // 128)):
+                part = jnp.take_along_axis(merged[m], spot, axis=1)
+                result = jnp.where((place >> 7) == m, part, result)
+            total[:, 128 * k : 128 * (k + 1)] += result
+            back[:, 128 * k : 128 * (k + 1)] = jnp.where(upper, swap_halves(result), result)
+        against = back[:, :H]
         spreading = spread[...]
         one_total[...] += against * spreading
         for k in range(2):
@@ -206,7 +280,7 @@
         return carry
 
     lax.fori_loop(0, count, slot_step, 0)
-    whole = total[0:4, :H] + total[4:8, :H]
+    whole = total[0:4, :H]
     sums[0:4, :] = whole
     scale = 1.0 / (TURNS * FLOPS)
     sums[4:5, :] = jnp.sum(sigma_flop * whole, axis=0, keepdims=True) * scale
@@ -235,10 +309,19 @@
     return x
 
 
+def spread_sum(x, axis):
+    size = lax.axis_size(axis)
+    share = -(-x.size // size)
+    flat = jnp.pad(x.reshape(-1), (0, share * size - x.size)).reshape(size, share)
+    mine = jnp.sum(lax.all_to_all(flat, axis, 0, 0, tiled=True), axis=0)
+    whole = lax.all_to_all(jnp.broadcast_to(mine, (size, share)), axis, 0, 0, tiled=True)
+    return whole.reshape(-1)[: x.size].reshape(x.shape)
+
+
 def on_device(
     ranges, flop_regret, flop_cards, live_turns, turn_card, river_cards, strength, turn_regret
 ):
-    alive, disjoint = tables()
+    index, disjoint = tables()
     smem = pl.BlockSpec(memory_space=pltpu.SMEM)
     vmem = pl.BlockSpec(memory_space=pltpu.VMEM)
     hbm = pl.BlockSpec(memory_space=pltpu.HBM)
@@ -255,14 +338,15 @@
             pltpu.VMEM((2, H), jnp.float32),
             pltpu.VMEM((1, A, H), jnp.float32),
             pltpu.VMEM((1, TS, RIV, H), jnp.float32),
-            pltpu.VMEM((56, HP), jnp.float32),
-            pltpu.VMEM((HP, HP), jnp.bfloat16),
-            pltpu.VMEM((HP, HP), jnp.bfloat16),
+            pltpu.VMEM((4, 16, 128), jnp.int32),
+            pltpu.VMEM((CP, CP), jnp.bfloat16),
             pltpu.VMEM((TS, 2, 8, H), jnp.float32),
-            pltpu.VMEM((16, HP), jnp.float32),
+            pltpu.VMEM((2, 8, HP), jnp.float32),
+            pltpu.VMEM((2, 16, 128), jnp.int32),
+            pltpu.VMEM((RIV, 16, 128), jnp.float32),
+            pltpu.VMEM((CP, 8), jnp.float32),
+            pltpu.VMEM((RIV, 16, CP), jnp.float32),
             pltpu.VMEM((8, HP), jnp.float32),
-            pltpu.VMEM((HP, 8), jnp.float32),
-            pltpu.VMEM((RIV, 16, HP), jnp.float32),
             pltpu.VMEM((8, HP), jnp.float32),
             pltpu.VMEM((8, H), jnp.float32),
             pltpu.VMEM((8, H), jnp.float32),
@@ -276,14 +360,14 @@
         name="subtrees",
     )(
         flop_cards, live_turns, turn_card, jnp.swapaxes(river_cards, 1, 2),
-        ranges, flop_regret, strength, turn_regret, jnp.asarray(alive), jnp.asarray(disjoint),
+        ranges, flop_regret, strength, turn_regret, jnp.asarray(index), jnp.asarray(disjoint),
     )
     regrets_flop = flop_regret[0]
     turns = exchange(sums, "turn", (1, 2))
     action_value = turns[0:4] / TURNS
     node_zero = jnp.sum(sigma_flop * action_value, axis=0)
     new_flop = jnp.maximum(regrets_flop + action_value - node_zero[None, :], 0.0)
-    root_value = exchange(turns[4:6], "flop", (1, 2, 4, 8, 16, 32))
+    root_value = spread_sum(turns[4:6], "flop")
     return (new_flop[None], new_turn, root_value)
 
 

time: 95.5 us -> 104 us (1.089)
  the two profiles are of different devices: /device:TPU:2 before, /device:TPU:1 now
where the time goes in v2:
time: 104 us; the launch traced here: 103 us
  starting transfers between devices  51.3 us (49%)
  Pallas kernels  23.6 us (23%)
  waiting for transfers between devices  21.8 us (21%)
  other arithmetic  2.99 us (3%)
  local copies, waits for them, and re-layouts  2.78 us (3%)
    ppermute x2, starting transfers between devices, exchange(): x = x + lax.ppermute(x, axis, [(n, n ^ flip) for n in range(size)])  31.9 us
    pallas_call x1, Pallas kernels, on_device(): pl.pallas_call(kernel, out_shape=(jax.ShapeDtypeStruct(turn_regret.shape,...  23.6 us
    all_to_all x1, starting transfers between devices, spread_sum(): mine = jnp.sum(lax.all_to_all(flat, axis, 0, 0, tiled=True), axis=0)  14.7 us
    all_to_all x1, waiting for transfers between devices, spread_sum(): lax.all_to_all(jnp.broadcast_to(mine, (size, share)), axis, 0, 0, tiled=T...  8.85 us
    all_to_all x1, waiting for transfers between devices, spread_sum(): mine = jnp.sum(lax.all_to_all(flat, axis, 0, 0, tiled=True), axis=0)  8.61 us
    all_to_all x1, starting transfers between devices, spread_sum(): lax.all_to_all(jnp.broadcast_to(mine, (size, share)), axis, 0, 0, tiled=T...  4.71 us
    ppermute x2, waiting for transfers between devices, exchange(): x = x + lax.ppermute(x, axis, [(n, n ^ flip) for n in range(size)])  4.3 us
  transfers between devices with their start and end apart: 4, of which 4 were waited for; matrix products, arithmetic and copies ran while one was open for 1% of the time, Pallas kernels for 0%

profile of v2, /device:TPU:1, one launch (start us, length us, event | category | flops | bytes accessed | tf_op | source)
XLA Modules:
  0.0 103.2 jit_solution(14987963002591610148)
XLA Ops:
  0.6 0.0 copy-start
  0.6 23.6 %subtrees.1 = (f32[1,24,4,4,1326]{4,3,2,1,0:T(4,128)}, f32[6,1326]{1,0:T(8,128)}, f32[4,1326]{1,0:T(4,128)}) custom-call(s32[1,3]{1,0:T(1,128)} %flop_cards.1, s32[1,4]{1,0:T(1,128)} %live_turns.1, s32[1,24]{1,0:T(1,128)} %turn_card.1, s32[1,2,24]{2,1,0:T(2,128)} %bitcast.14, f32[2,1326]{1,0:T(2,128)} %ranges_in.1, f32[1,4,1326]{2,1,0:T(4,128)} %flop_regret_in.1, ...), custom_call_target="tpu_custom_call" | custom-call | tf_op jit(solution)/shard_map/subtrees/pallas_call | solution.py:328
  24.2 0.3 collective-permute-start
  24.6 2.9 %collective-permute-done = f32[6,1326]{1,0:T(8,128)S(1)} collective-permute-done((f32[6,1326]{1,0:T(8,128)}, f32[6,1326]{1,0:T(8,128)S(1)}, u32[]{:S(2)}, u32[]{:S(2)}) %collective-permute-start) | collective-permute-done | bytes 31856 | tf_op jit(solution)/shard_map/ppermute | solution.py:308
  27.4 0.8 add.11
  28.2 31.6 %collective-permute-start.1 = (f32[6,1326]{1,0:T(8,128)S(1)}, f32[6,1326]{1,0:T(8,128)S(1)}, u32[]{:S(2)}, u32[]{:S(2)}) collective-permute-start(f32[6,1326]{1,0:T(8,128)S(1)} %add.11), channel_id=1, source_target_pairs={{0,2},{1,3},{2,0},{3,1},{4,6},{5,7},{6,4},{7,5},{8,10},{9,11},{10,... | collective-permute-start | bytes 95480 | tf_op jit(solution)/shard_map/ppermute | solution.py:308
  59.8 1.4 %collective-permute-done.1 = f32[6,1326]{1,0:T(8,128)S(1)} collective-permute-done((f32[6,1326]{1,0:T(8,128)S(1)}, f32[6,1326]{1,0:T(8,128)S(1)}, u32[]{:S(2)}, u32[]{:S(2)}) %collective-permute-start.1) | collective-permute-done | bytes 31856 | tf_op jit(solution)/shard_map/ppermute | solution.py:308
  61.3 0.1 reshape.25
  61.4 0.7 all_to_all.10
  62.1 14.7 %all-to-all-start = ((f32[64,1,42]{2,1,0:T(1,128)}), f32[64,1,42]{2,1,0:T(1,128)S(1)}, u32[]{:S(2)}, u32[]{:S(2)}) async-start(f32[64,1,42]{2,1,0:T(1,128)} %bitcast.3), calls=%async_computation | async-start | bytes 65536 | tf_op jit(solution)/shard_map/all_to_all | solution.py:316
  76.8 0.8 multiply_reduce_fusion
  77.6 8.6 %all-to-all-done = f32[64,1,42]{2,1,0:T(1,128)S(1)} async-done(((f32[64,1,42]{2,1,0:T(1,128)}), f32[64,1,42]{2,1,0:T(1,128)S(1)}, u32[]{:S(2)}, u32[]{:S(2)}) %all-to-all-start) | async-done | bytes 10784 | tf_op jit(solution)/shard_map/all_to_all | solution.py:316
  86.2 0.1 reduce_sum.19
  86.3 0.6 broadcast_in_dim.8
  86.9 4.7 %all-to-all-start.1 = ((f32[64,1,42]{2,1,0:T(1,128)}), f32[64,1,42]{2,1,0:T(1,128)S(1)}, u32[]{:S(2)}, u32[]{:S(2)}) async-start(f32[64,1,42]{2,1,0:T(1,128)} %broadcast_in_dim.8), calls=%async_computation.1 | async-start | bytes 65536 | tf_op jit(solution)/shard_map/all_to_all | solution.py:317
  91.6 0.0 copy-done
  91.6 0.6 fusion.2
  92.3 8.9 %all-to-all-done.1 = f32[64,1,42]{2,1,0:T(1,128)S(1)} async-done(((f32[64,1,42]{2,1,0:T(1,128)}), f32[64,1,42]{2,1,0:T(1,128)S(1)}, u32[]{:S(2)}, u32[]{:S(2)}) %all-to-all-start.1) | async-done | bytes 10784 | tf_op jit(solution)/shard_map/all_to_all | solution.py:317
  101.1 0.5 broadcast.10
  101.6 0.7 reduce.4
  102.3 0.1 reshape.26
  102.5 0.7 reshape.27
  (3 shorter events, 0.0 us)
Async XLA Ops:
  0.6 91.0 %copy-start = (f32[1,4,1326]{2,1,0:T(4,128)S(1)}, f32[1,4,1326]{2,1,0:T(4,128)}, u32[]{:S(2)}) copy-start(f32[1,4,1326]{2,1,0:T(4,128)} %flop_regret_in.1) | copy-start | bytes 63652
  24.2 3.2 %collective-permute-start = (f32[6,1326]{1,0:T(8,128)}, f32[6,1326]{1,0:T(8,128)S(1)}, u32[]{:S(2)}, u32[]{:S(2)}) collective-permute-start(f32[6,1326]{1,0:T(8,128)} %get-tuple-element.6), channel_id=1, source_target_pairs={{0,1},{1,0},{2,3},{3,2},{4,5},{5,4},{6,7},{7,6},{8,9},{9,8},{10,11... | collective-permute-start | bytes 95480 | tf_op jit(solution)/shard_map/ppermute | solution.py:308
  28.2 33.0 %collective-permute-start.1 = (f32[6,1326]{1,0:T(8,128)S(1)}, f32[6,1326]{1,0:T(8,128)S(1)}, u32[]{:S(2)}, u32[]{:S(2)}) collective-permute-start(f32[6,1326]{1,0:T(8,128)S(1)} %add.11), channel_id=1, source_target_pairs={{0,2},{1,3},{2,0},{3,1},{4,6},{5,7},{6,4},{7,5},{8,10},{9,11},{10,... | collective-permute-start | bytes 95480 | tf_op jit(solution)/shard_map/ppermute | solution.py:308
  62.1 24.1 %all-to-all-start = ((f32[64,1,42]{2,1,0:T(1,128)}), f32[64,1,42]{2,1,0:T(1,128)S(1)}, u32[]{:S(2)}, u32[]{:S(2)}) async-start(f32[64,1,42]{2,1,0:T(1,128)} %bitcast.3), calls=%async_computation | async-start | bytes 65536 | tf_op jit(solution)/shard_map/all_to_all | solution.py:316
  86.9 14.2 %all-to-all-start.1 = ((f32[64,1,42]{2,1,0:T(1,128)}), f32[64,1,42]{2,1,0:T(1,128)S(1)}, u32[]{:S(2)}, u32[]{:S(2)}) async-start(f32[64,1,42]{2,1,0:T(1,128)} %broadcast_in_dim.8), calls=%async_computation.1 | async-start | bytes 65536 | tf_op jit(solution)/shard_map/all_to_all | solution.py:317

commit v3 on v2

--- a/solution.py
+++ b/solution.py
@@ -68,11 +68,17 @@
     ranges_in, flop_regret_in, strength_in, turn_regret, index_in, keep_in,
     new_turn, sums, root,
     ranges, flop_regret, strength, index, keep,
-    regrets, wide, lane, alive, columns, found, back, total, one_total, spread, blank,
+    regrets, wide_a, wide_b, lane_a, lane_b, alive_a, alive_b, columns_a, columns_b,
+    found_a, found_b, back_a, back_b, spread_a, spread_b, total, one_total, blank,
     small_sems, keep_sems, in_sems, out_sems,
 ):
+    wides, lanes, alives = (wide_a, wide_b), (lane_a, lane_b), (alive_a, alive_b)
+    columnses, founds, backs = (columns_a, columns_b), (found_a, found_b), (back_a, back_b)
+    spreads = (spread_a, spread_b)
     me = lax.axis_index("turn")
     count = live_turns[0, me]
+    pairs = (count + 1) // 2
+    used = 2 * pairs
 
     def regret_copy(slot, b):
         return pltpu.make_async_copy(
@@ -122,16 +128,16 @@
             regret_copy(slot, b).start()
         return carry
 
-    lax.fori_loop(1, count, fetch, 0)
+    lax.fori_loop(1, used, fetch, 0)
     blank[...] = jnp.zeros_like(blank)
 
     def clear(slot, carry):
         blank_copy(slot).start()
         return carry
 
-    lax.fori_loop(count, TS, clear, 0)
-    wide[...] = jnp.zeros_like(wide)
-    back[...] = jnp.zeros_like(back)
+    lax.fori_loop(used, TS, clear, 0)
+    for ref in wides + backs:
+        ref[...] = jnp.zeros_like(ref)
     total[...] = jnp.zeros_like(total)
     one_total[...] = jnp.zeros_like(one_total)
     for copy in small:
@@ -140,7 +146,8 @@
     regrets_flop = flop_regret[0]
     sigma_flop = regrets_flop / jnp.sum(regrets_flop, axis=0, keepdims=True)
     reach_zero = rounded(ranges[0:1, :] * sigma_flop)
-    wide[1, 0:4, :H] = reach_zero
+    for wide in wides:
+        wide[1, 0:4, :H] = reach_zero
     first_card, second_card, third_card = (flop_cards[0, n] for n in range(3))
     first_card, second_card = jnp.minimum(first_card, second_card), jnp.maximum(first_card, second_card)
     second_card, third_card = jnp.minimum(second_card, third_card), jnp.maximum(second_card, third_card)
@@ -156,7 +163,8 @@
     for copy in masks:
         copy.wait()
 
-    def slot_step(slot, carry):
+    def prepare(slot, side):
+        wide, lane, alive, columns, spread = wides[side], lanes[side], alives[side], columnses[side], spreads[side]
         for b in range(A):
             regret_copy(slot, b).wait()
         first, second = regrets[slot, 0], regrets[slot, 1]
@@ -224,6 +232,10 @@
                     jnp.concatenate([packed[0][k] * mask, zeros * mask], axis=0).astype(jnp.bfloat16)
                 )
             given.append(jnp.concatenate(pieces, axis=1))
+        return packed, given
+
+    def multiply(side, packed, given):
+        columns, found = columnses[side], founds[side]
         for start, rows in BLOCKS:
             own = [
                 jnp.broadcast_to(columns[start : start + rows, 4 + r : 5 + r], (rows, 128))
@@ -250,6 +262,10 @@
                         found[r, :, other:stop] = gave
                     else:
                         found[r, :, other:stop] += gave
+
+    def finish(slot, side, live):
+        lane, alive, found = lanes[side], alives[side], founds[side]
+        back, spread = backs[side], spreads[side]
         merged = []
         for k in range(CP // 128):
             values = [
@@ -266,20 +282,30 @@
             for m in range(max(0, k - 2), min(k + 1, CP // 128)):
                 part = jnp.take_along_axis(merged[m], spot, axis=1)
                 result = jnp.where((place >> 7) == m, part, result)
+            if live is not None:
+                result = result * live
             total[:, 128 * k : 128 * (k + 1)] += result
             back[:, 128 * k : 128 * (k + 1)] = jnp.where(upper, swap_halves(result), result)
         against = back[:, :H]
         spreading = spread[...]
         one_total[...] += against * spreading
         for k in range(2):
-            regrets[slot, k] = jnp.maximum(
-                regrets[slot, k] + against * (pots[k] - spreading), 0.0
-            )
+            updated = jnp.maximum(regrets[slot, k] + against * (pots[k] - spreading), 0.0)
+            regrets[slot, k] = updated if live is None else updated * live
         for b in range(A):
             result_copy(slot, b).start()
+
+
+    def pair_step(pair, carry):
+        slots = (2 * pair, 2 * pair + 1)
+        live = (None, (slots[1] < count).astype(jnp.float32))
+        ready = [prepare(slots[side], side) for side in range(2)]
+        for side in range(2):
+            multiply(side, *ready[side])
+            finish(slots[side], side, live[side])
         return carry
 
-    lax.fori_loop(0, count, slot_step, 0)
+    lax.fori_loop(0, pairs, pair_step, 0)
     whole = total[0:4, :H]
     sums[0:4, :] = whole
     scale = 1.0 / (TURNS * FLOPS)
@@ -292,30 +318,19 @@
             result_copy(slot, b).wait()
         return carry
 
-    lax.fori_loop(0, count, settle, 0)
+    lax.fori_loop(0, used, settle, 0)
 
     def settle_blank(slot, carry):
         blank_copy(slot).wait()
         return carry
 
-    lax.fori_loop(count, TS, settle_blank, 0)
-
-
-def exchange(x, axis, flips):
-    size = lax.axis_size(axis)
-    for flip in flips:
-        if flip < size:
-            x = x + lax.ppermute(x, axis, [(n, n ^ flip) for n in range(size)])
-    return x
-
-
-def spread_sum(x, axis):
-    size = lax.axis_size(axis)
-    share = -(-x.size // size)
-    flat = jnp.pad(x.reshape(-1), (0, share * size - x.size)).reshape(size, share)
-    mine = jnp.sum(lax.all_to_all(flat, axis, 0, 0, tiled=True), axis=0)
-    whole = lax.all_to_all(jnp.broadcast_to(mine, (size, share)), axis, 0, 0, tiled=True)
-    return whole.reshape(-1)[: x.size].reshape(x.shape)
+    lax.fori_loop(used, TS, settle_blank, 0)
+
+
+def group_sum(x, axis, groups=None):
+    size = lax.axis_size(axis) if groups is None else len(groups[0])
+    copies = jnp.broadcast_to(x, (size, *x.shape))
+    return jnp.sum(lax.all_to_all(copies, axis, 0, 0, axis_index_groups=groups, tiled=True), axis=0)
 
 
 def on_device(
@@ -341,14 +356,14 @@
             pltpu.VMEM((4, 16, 128), jnp.int32),
             pltpu.VMEM((CP, CP), jnp.bfloat16),
             pltpu.VMEM((TS, 2, 8, H), jnp.float32),
-            pltpu.VMEM((2, 8, HP), jnp.float32),
-            pltpu.VMEM((2, 16, 128), jnp.int32),
-            pltpu.VMEM((RIV, 16, 128), jnp.float32),
-            pltpu.VMEM((CP, 8), jnp.float32),
-            pltpu.VMEM((RIV, 16, CP), jnp.float32),
+            *[pltpu.VMEM((2, 8, HP), jnp.float32)] * 2,
+            *[pltpu.VMEM((2, 16, 128), jnp.int32)] * 2,
+            *[pltpu.VMEM((RIV, 16, 128), jnp.float32)] * 2,
+            *[pltpu.VMEM((CP, 8), jnp.float32)] * 2,
+            *[pltpu.VMEM((RIV, 16, CP), jnp.float32)] * 2,
+            *[pltpu.VMEM((8, HP), jnp.float32)] * 2,
+            *[pltpu.VMEM((8, H), jnp.float32)] * 2,
             pltpu.VMEM((8, HP), jnp.float32),
-            pltpu.VMEM((8, HP), jnp.float32),
-            pltpu.VMEM((8, H), jnp.float32),
             pltpu.VMEM((8, H), jnp.float32),
             pltpu.VMEM((A, A, H), jnp.float32),
             pltpu.SemaphoreType.DMA((4,)),
@@ -363,11 +378,15 @@
         ranges, flop_regret, strength, turn_regret, jnp.asarray(index), jnp.asarray(disjoint),
     )
     regrets_flop = flop_regret[0]
-    turns = exchange(sums, "turn", (1, 2))
+    turns = group_sum(sums, "turn")
     action_value = turns[0:4] / TURNS
     node_zero = jnp.sum(sigma_flop * action_value, axis=0)
     new_flop = jnp.maximum(regrets_flop + action_value - node_zero[None, :], 0.0)
-    root_value = spread_sum(turns[4:6], "flop")
+    near = [[8 * z + k for k in range(8)] for z in range(8)]
+    far = [[8 * z + k for z in range(8)] for k in range(8)]
+    root_value = turns[4:6]
+    if lax.axis_size("flop") == FLOPS:
+        root_value = group_sum(group_sum(root_value, "flop", near), "flop", far)
     return (new_flop[None], new_turn, root_value)
 
 

time: 104 us -> 87 us (0.84)
  starting transfers between devices: 51.3 us -> 13.3 us
  blocking collectives: 0 us -> 34.1 us
  waiting for transfers between devices: 21.8 us -> 11.2 us
    all_to_all x0 -> x1, blocking collectives: none -> 34.1 us  [group_sum(): lax.all_to_all(copies, axis, 0, 0, axis_index_groups=groups, tiled=True)]
    ppermute x2 -> x0, starting transfers between devices: 31.9 us -> none  [exchange(): x = x + lax.ppermute(x, axis, [(n, n ^ flip) for n in range(size)])]
    all_to_all x2, waiting for transfers between devices: 17.5 us -> 11.2 us  [group_sum(): lax.all_to_all(copies, axis, 0, 0, axis_index_groups=groups, tiled=True)]
    all_to_all x2, starting transfers between devices: 19.4 us -> 13.3 us  [group_sum(): lax.all_to_all(copies, axis, 0, 0, axis_index_groups=groups, tiled=True)]
    ppermute x2 -> x0, waiting for transfers between devices: 4.3 us -> none  [exchange(): x = x + lax.ppermute(x, axis, [(n, n ^ flip) for n in range(size)])]
    broadcast_in_dim x1 -> x3, local copies, waits for them, and re-layouts: 0.62 us -> 2.09 us  [group_sum(): copies = jnp.broadcast_to(x, (size, *x.shape))]
    all_to_all x2 -> x0, local copies, waits for them, and re-layouts: 1.25 us -> none  [the longest x1 0.74 us: spread_sum(): mine = jnp.sum(lax.all_to_all(flat, axis, 0, 0, tiled=True), axis=0)]
  transfers between devices with their start and end apart: 4 -> 2, of which waited for: 4 -> 2; matrix products, arithmetic and copies ran while one was open for 1% -> 2% of each run, Pallas kernels for 0% -> 0%
where the time goes in v3:
time: 87 us; the launch traced here: 86.6 us
  blocking collectives  34.1 us (39%)
  Pallas kernels  23.2 us (27%)
  starting transfers between devices  13.3 us (15%)
  waiting for transfers between devices  11.2 us (13%)
  local copies, waits for them, and re-layouts  2.11 us (2%)
  other arithmetic  2.07 us (2%)
    all_to_all x1, blocking collectives, group_sum(): lax.all_to_all(copies, axis, 0, 0, axis_index_groups=groups, tiled=True)  34.1 us
    pallas_call x1, Pallas kernels, on_device(): pl.pallas_call(kernel, out_shape=(jax.ShapeDtypeStruct(turn_regret.shape,...  23.2 us
    all_to_all x2, starting transfers between devices, group_sum(): lax.all_to_all(copies, axis, 0, 0, axis_index_groups=groups, tiled=True)  13.3 us
    all_to_all x2, waiting for transfers between devices, group_sum(): lax.all_to_all(copies, axis, 0, 0, axis_index_groups=groups, tiled=True)  11.2 us
    broadcast_in_dim x3, local copies, waits for them, and re-layouts, group_sum(): copies = jnp.broadcast_to(x, (size, *x.shape))  2.09 us
  transfers between devices with their start and end apart: 2, of which 2 were waited for; matrix products, arithmetic and copies ran while one was open for 2% of the time, Pallas kernels for 0%

profile of v3, /device:TPU:1, one launch (start us, length us, event | category | flops | bytes accessed | tf_op | source)
XLA Modules:
  0.0 86.6 jit_solution(14299926678811517075)
XLA Ops:
  0.6 0.0 copy-start
  0.6 23.2 %subtrees.1 = (f32[1,24,4,4,1326]{4,3,2,1,0:T(4,128)}, f32[6,1326]{1,0:T(8,128)}, f32[4,1326]{1,0:T(4,128)}) custom-call(s32[1,3]{1,0:T(1,128)} %flop_cards.1, s32[1,4]{1,0:T(1,128)} %live_turns.1, s32[1,24]{1,0:T(1,128)} %turn_card.1, s32[1,2,24]{2,1,0:T(2,128)} %bitcast.11, f32[2,1326]{1,0:T(2,128)} %ranges_in.1, f32[1,4,1326]{2,1,0:T(4,128)} %flop_regret_in.1, ...), custom_call_target="tpu_custom_call" | custom-call | tf_op jit(solution)/shard_map/subtrees/pallas_call | solution.py:343
  23.8 0.8 broadcast_in_dim.13
  24.6 34.1 %all_to_all.15 = f32[4,6,1326]{2,1,0:T(8,128)S(1)} all-to-all(f32[4,6,1326]{2,1,0:T(8,128)S(1)} %broadcast_in_dim.13), channel_id=1, replica_groups=mesh['flop'=64,'turn'=4] {'turn'}, dimensions={0} | all-to-all | bytes 254592 | tf_op jit(solution)/shard_map/all_to_all | solution.py:333
  58.8 0.6 broadcast_in_dim.15
  59.4 5.1 %all-to-all-start.1 = ((f32[8,2,1326]{2,1,0:T(2,128)}), f32[8,2,1326]{2,1,0:T(2,128)S(1)}, u32[]{:S(2)}, u32[]{:S(2)}) async-start(f32[8,2,1326]{2,1,0:T(2,128)} %broadcast_in_dim.15), calls=%async_computation.1 | async-start | bytes 180224 | tf_op jit(solution)/shard_map/all_to_all | solution.py:333
  64.5 0.8 multiply_reduce_fusion
  65.3 4.2 %all-to-all-done.1 = f32[8,2,1326]{2,1,0:T(2,128)S(1)} async-done(((f32[8,2,1326]{2,1,0:T(2,128)}), f32[8,2,1326]{2,1,0:T(2,128)S(1)}, u32[]{:S(2)}, u32[]{:S(2)}) %all-to-all-start.1) | async-done | bytes 84896 | tf_op jit(solution)/shard_map/all_to_all | solution.py:333
  69.5 0.6 broadcast_in_dim.16
  70.1 8.2 %all-to-all-start.2 = ((f32[8,2,1326]{2,1,0:T(2,128)}), f32[8,2,1326]{2,1,0:T(2,128)S(1)}, u32[]{:S(2)}, u32[]{:S(2)}) async-start(f32[8,2,1326]{2,1,0:T(2,128)} %broadcast_in_dim.16), calls=%async_computation.2 | async-start | bytes 180224 | tf_op jit(solution)/shard_map/all_to_all | solution.py:333
  78.3 0.0 copy-done
  78.3 0.6 fusion.2
  79.0 7.0 %all-to-all-done.2 = f32[8,2,1326]{2,1,0:T(2,128)S(1)} async-done(((f32[8,2,1326]{2,1,0:T(2,128)}), f32[8,2,1326]{2,1,0:T(2,128)S(1)}, u32[]{:S(2)}, u32[]{:S(2)}) %all-to-all-start.2) | async-done | bytes 84896 | tf_op jit(solution)/shard_map/all_to_all | solution.py:333
  85.9 0.6 reduce_sum.39
  (3 shorter events, 0.1 us)
Async XLA Ops:
  0.6 77.7 %copy-start = (f32[1,4,1326]{2,1,0:T(4,128)S(1)}, f32[1,4,1326]{2,1,0:T(4,128)}, u32[]{:S(2)}) copy-start(f32[1,4,1326]{2,1,0:T(4,128)} %flop_regret_in.1) | copy-start | bytes 63652
  59.4 10.0 %all-to-all-start.1 = ((f32[8,2,1326]{2,1,0:T(2,128)}), f32[8,2,1326]{2,1,0:T(2,128)S(1)}, u32[]{:S(2)}, u32[]{:S(2)}) async-start(f32[8,2,1326]{2,1,0:T(2,128)} %broadcast_in_dim.15), calls=%async_computation.1 | async-start | bytes 180224 | tf_op jit(solution)/shard_map/all_to_all | solution.py:333
  70.1 15.8 %all-to-all-start.2 = ((f32[8,2,1326]{2,1,0:T(2,128)}), f32[8,2,1326]{2,1,0:T(2,128)S(1)}, u32[]{:S(2)}, u32[]{:S(2)}) async-start(f32[8,2,1326]{2,1,0:T(2,128)} %broadcast_in_dim.16), calls=%async_computation.2 | async-start | bytes 180224 | tf_op jit(solution)/shard_map/all_to_all | solution.py:333

commit v4 on v3

--- a/solution.py
+++ b/solution.py
@@ -18,6 +18,7 @@
 RIV = 2
 FLOPS = 64
 BLOCK = 256
+PIECE = 32
 BIG = 2.0**126
 
 bet_sizes = (0.25, 0.5, 1.0, 2.0)
@@ -68,12 +69,12 @@
     ranges_in, flop_regret_in, strength_in, turn_regret, index_in, keep_in,
     new_turn, sums, root,
     ranges, flop_regret, strength, index, keep,
-    regrets, wide_a, wide_b, lane_a, lane_b, alive_a, alive_b, columns_a, columns_b,
+    regrets, wide_a, wide_b, lane_a, lane_b, alive_a, alive_b, bands_a, bands_b,
     found_a, found_b, back_a, back_b, spread_a, spread_b, total, one_total, blank,
     small_sems, keep_sems, in_sems, out_sems,
 ):
     wides, lanes, alives = (wide_a, wide_b), (lane_a, lane_b), (alive_a, alive_b)
-    columnses, founds, backs = (columns_a, columns_b), (found_a, found_b), (back_a, back_b)
+    bandses, founds, backs = (bands_a, bands_b), (found_a, found_b), (back_a, back_b)
     spreads = (spread_a, spread_b)
     me = lax.axis_index("turn")
     count = live_turns[0, me]
@@ -164,7 +165,7 @@
         copy.wait()
 
     def prepare(slot, side):
-        wide, lane, alive, columns, spread = wides[side], lanes[side], alives[side], columnses[side], spreads[side]
+        wide, lane, alive, bands, spread = wides[side], lanes[side], alives[side], bandses[side], spreads[side]
         for b in range(A):
             regret_copy(slot, b).wait()
         first, second = regrets[slot, 0], regrets[slot, 1]
@@ -221,7 +222,9 @@
                 packed[group].append(
                     jnp.where(offset < 128, parts[0], jnp.where(offset < 256, parts[1], parts[2]))
                 )
-        columns[...] = jnp.concatenate(packed[1], axis=1).T
+        turned = jnp.concatenate(packed[1], axis=1).T
+        for r in range(RIV):
+            bands[r] = jnp.broadcast_to(turned[:, 4 + r : 5 + r], (CP, 128))
         given = []
         for r in range(RIV):
             pieces = []
@@ -235,33 +238,31 @@
         return packed, given
 
     def multiply(side, packed, given):
-        columns, found = columnses[side], founds[side]
-        for start, rows in BLOCKS:
-            own = [
-                jnp.broadcast_to(columns[start : start + rows, 4 + r : 5 + r], (rows, 128))
-                for r in range(RIV)
-            ]
-            for other in range(0, CP, BLOCK):
-                stop = min(other + BLOCK, CP)
-                most = keep[start : start + rows, other:stop]
-                least = -most
+        found, bands = founds[side], bandses[side]
+        for other in range(0, CP, BLOCK):
+            stop = min(other + BLOCK, CP)
+            tiles = range(other // 128, stop // 128)
+            gave = [None] * RIV
+            for start, rows in BLOCKS:
+                pieces = [[] for _ in range(RIV)]
+                for top in range(start, start + rows, PIECE):
+                    end = min(top + PIECE, start + rows)
+                    most = keep[top:end, other:stop]
+                    least = -most
+                    for r in range(RIV):
+                        own = bands[r, top:end, :]
+                        gap = jnp.concatenate(
+                            [own - packed[1][k][4 + r : 5 + r, :] for k in tiles], axis=1
+                        ).astype(jnp.bfloat16)
+                        pieces[r].append(jnp.maximum(jnp.minimum(gap, most), least))
                 for r in range(RIV):
-                    gap = jnp.concatenate(
-                        [
-                            own[r] - packed[1][k][4 + r : 5 + r, :]
-                            for k in range(other // 128, stop // 128)
-                        ],
-                        axis=1,
-                    ).astype(jnp.bfloat16)
-                    outcome = jnp.maximum(jnp.minimum(gap, most), least)
-                    gave = jnp.dot(
-                        given[r][:, start : start + rows], outcome,
+                    part = jnp.dot(
+                        given[r][:, start : start + rows], jnp.concatenate(pieces[r], axis=0),
                         preferred_element_type=jnp.float32,
                     )
-                    if start == 0:
-                        found[r, :, other:stop] = gave
-                    else:
-                        found[r, :, other:stop] += gave
+                    gave[r] = part if gave[r] is None else gave[r] + part
+            for r in range(RIV):
+                found[r, :, other:stop] = gave[r]
 
     def finish(slot, side, live):
         lane, alive, found = lanes[side], alives[side], founds[side]
@@ -359,7 +360,7 @@
             *[pltpu.VMEM((2, 8, HP), jnp.float32)] * 2,
             *[pltpu.VMEM((2, 16, 128), jnp.int32)] * 2,
             *[pltpu.VMEM((RIV, 16, 128), jnp.float32)] * 2,
-            *[pltpu.VMEM((CP, 8), jnp.float32)] * 2,
+            *[pltpu.VMEM((RIV, CP, 128), jnp.float32)] * 2,
             *[pltpu.VMEM((RIV, 16, CP), jnp.float32)] * 2,
             *[pltpu.VMEM((8, HP), jnp.float32)] * 2,
             *[pltpu.VMEM((8, H), jnp.float32)] * 2,
@@ -378,15 +379,21 @@
         ranges, flop_regret, strength, turn_regret, jnp.asarray(index), jnp.asarray(disjoint),
     )
     regrets_flop = flop_regret[0]
-    turns = group_sum(sums, "turn")
-    action_value = turns[0:4] / TURNS
+    turns = sums[0:4]
+    for flip in (1, 2):
+        turns = turns + lax.ppermute(turns, "turn", [(n, n ^ flip) for n in range(4)])
+    action_value = turns / TURNS
     node_zero = jnp.sum(sigma_flop * action_value, axis=0)
     new_flop = jnp.maximum(regrets_flop + action_value - node_zero[None, :], 0.0)
-    near = [[8 * z + k for k in range(8)] for z in range(8)]
-    far = [[8 * z + k for z in range(8)] for k in range(8)]
-    root_value = turns[4:6]
+    root_value = sums[4:6]
     if lax.axis_size("flop") == FLOPS:
-        root_value = group_sum(group_sum(root_value, "flop", near), "flop", far)
+        everyone = np.arange(4 * FLOPS).reshape(8, 4, 2, 4)
+        near = everyone.transpose(0, 2, 1, 3).reshape(16, 16).tolist()
+        far = everyone.transpose(1, 3, 0, 2).reshape(16, 16).tolist()
+        for groups in (near, far):
+            root_value = group_sum(root_value, ("flop", "turn"), groups)
+    else:
+        root_value = lax.psum(root_value, "turn")
     return (new_flop[None], new_turn, root_value)
 
 

time: 87 us -> 91 us (1.046)
  starting transfers between devices: 13.3 us -> 51 us
  blocking collectives: 34.1 us -> 0 us
  Pallas kernels: 23.2 us -> 21.1 us
    all_to_all x1 -> x0, blocking collectives: 34.1 us -> none  [group_sum(): lax.all_to_all(copies, axis, 0, 0, axis_index_groups=groups, tiled=True)]
    all_to_all x2, starting transfers between devices: 13.3 us -> 42.4 us  [group_sum(): lax.all_to_all(copies, axis, 0, 0, axis_index_groups=groups, tiled=True)]
    ppermute x0 -> x2, starting transfers between devices: none -> 8.65 us  [on_device(): lax.ppermute(turns, 'turn', [(n, n ^ flip) for n in range(4)])]
    pallas_call x1, Pallas kernels: 23.2 us -> 21.1 us  [on_device(): pl.pallas_call(kernel, out_shape=(jax.ShapeDtypeStruct(turn_regret.shape,...]
    slice x1 -> x2, local copies, waits for them, and re-layouts: 0.01 us -> 1.59 us  [the longest x1 0.8 us: on_device(): root_value = sums[4:6]]
    ppermute x0 -> x2, waiting for transfers between devices: none -> 1.4 us  [on_device(): lax.ppermute(turns, 'turn', [(n, n ^ flip) for n in range(4)])]
    broadcast_in_dim x3 -> x2, local copies, waits for them, and re-layouts: 2.09 us -> 1.42 us  [group_sum(): copies = jnp.broadcast_to(x, (size, *x.shape))]
  transfers between devices with their start and end apart: 2 -> 4, of which waited for: 2 -> 3; matrix products, arithmetic and copies ran while one was open for 2% -> 4% of each run, Pallas kernels for 0% -> 0%
where the time goes in v4:
time: 91 us; the launch traced here: 90.5 us
  starting transfers between devices  51 us (56%)
  Pallas kernels  21.1 us (23%)
  waiting for transfers between devices  11.8 us (13%)
  local copies, waits for them, and re-layouts  3.01 us (3%)
  other arithmetic  2.91 us (3%)
    all_to_all x2, starting transfers between devices, group_sum(): lax.all_to_all(copies, axis, 0, 0, axis_index_groups=groups, tiled=True)  42.4 us
    pallas_call x1, Pallas kernels, on_device(): pl.pallas_call(kernel, out_shape=(jax.ShapeDtypeStruct(turn_regret.shape,...  21.1 us
    all_to_all x2, waiting for transfers between devices, group_sum(): lax.all_to_all(copies, axis, 0, 0, axis_index_groups=groups, tiled=True)  10.4 us
    ppermute x2, starting transfers between devices, on_device(): lax.ppermute(turns, 'turn', [(n, n ^ flip) for n in range(4)])  8.65 us
  transfers between devices with their start and end apart: 4, of which 3 were waited for; matrix products, arithmetic and copies ran while one was open for 4% of the time, Pallas kernels for 0%

profile of v4, /device:TPU:1, one launch (start us, length us, event | category | flops | bytes accessed | tf_op | source)
XLA Modules:
  0.0 90.5 jit_solution(6018084830648928927)
XLA Ops:
  0.6 0.0 copy-start
  0.6 21.1 %subtrees.1 = (f32[1,24,4,4,1326]{4,3,2,1,0:T(4,128)}, f32[6,1326]{1,0:T(8,128)}, f32[4,1326]{1,0:T(4,128)}) custom-call(s32[1,3]{1,0:T(1,128)} %flop_cards.1, s32[1,4]{1,0:T(1,128)} %live_turns.1, s32[1,24]{1,0:T(1,128)} %turn_card.1, s32[1,2,24]{2,1,0:T(2,128)} %bitcast.11, f32[2,1326]{1,0:T(2,128)} %ranges_in.1, f32[1,4,1326]{2,1,0:T(4,128)} %flop_regret_in.1, ...), custom_call_target="tpu_custom_call" | custom-call | tf_op jit(solution)/shard_map/subtrees/pallas_call | solution.py:344
  21.8 0.8 slice.6
  22.6 5.8 %collective-permute-start = (f32[4,1326]{1,0:T(4,128)S(1)}, f32[4,1326]{1,0:T(4,128)S(1)}, u32[]{:S(2)}, u32[]{:S(2)}) collective-permute-start(f32[4,1326]{1,0:T(4,128)S(1)} %slice.6), channel_id=1, source_target_pairs={{0,1},{1,0},{2,3},{3,2},{4,5},{5,4},{6,7},{7,6},{8,9},{9,8},{10,11... | collective-permute-start | bytes 63656 | tf_op jit(solution)/shard_map/ppermute | solution.py:384
  28.4 0.8 slice.7
  29.2 0.7 broadcast_in_dim.11
  29.9 32.1 %all-to-all-start = ((f32[16,2,1326]{2,1,0:T(2,128)}), f32[16,2,1326]{2,1,0:T(2,128)S(1)}, u32[]{:S(2)}, u32[]{:S(2)}) async-start(f32[16,2,1326]{2,1,0:T(2,128)} %broadcast_in_dim.11), calls=%async_computation | async-start | bytes 360448 | tf_op jit(solution)/shard_map/all_to_all | solution.py:334
  62.0 0.0 collective-permute-done
  62.0 0.8 slice_add_fusion
  62.8 2.9 %collective-permute-start.1 = (f32[4,1326]{1,0:T(4,128)S(1)}, f32[4,1326]{1,0:T(4,128)S(1)}, u32[]{:S(2)}, u32[]{:S(2)}) collective-permute-start(f32[4,1326]{1,0:T(4,128)S(1)} %slice_add_fusion), channel_id=1, source_target_pairs={{0,2},{1,3},{2,0},{3,1},{4,6},{5,7},{6,4},{7,5},{8,10},{9,11},{10,... | collective-permute-start | bytes 63656 | tf_op jit(solution)/shard_map/ppermute | solution.py:384
  65.6 1.4 %collective-permute-done.1 = f32[4,1326]{1,0:T(4,128)S(1)} collective-permute-done((f32[4,1326]{1,0:T(4,128)S(1)}, f32[4,1326]{1,0:T(4,128)S(1)}, u32[]{:S(2)}, u32[]{:S(2)}) %collective-permute-start.1) | collective-permute-done | bytes 21248 | tf_op jit(solution)/shard_map/ppermute | solution.py:384
  67.0 0.8 multiply_reduce_fusion
  67.8 1.0 %all-to-all-done = f32[16,2,1326]{2,1,0:T(2,128)S(1)} async-done(((f32[16,2,1326]{2,1,0:T(2,128)}), f32[16,2,1326]{2,1,0:T(2,128)S(1)}, u32[]{:S(2)}, u32[]{:S(2)}) %all-to-all-start) | async-done | bytes 169760 | tf_op jit(solution)/shard_map/all_to_all | solution.py:334
  68.8 0.1 reduce_sum.28
  68.9 0.7 broadcast_in_dim.12
  69.6 10.3 %all-to-all-start.1 = ((f32[16,2,1326]{2,1,0:T(2,128)}), f32[16,2,1326]{2,1,0:T(2,128)S(1)}, u32[]{:S(2)}, u32[]{:S(2)}) async-start(f32[16,2,1326]{2,1,0:T(2,128)} %broadcast_in_dim.12), calls=%async_computation.1 | async-start | bytes 360448 | tf_op jit(solution)/shard_map/all_to_all | solution.py:334
  79.9 0.0 copy-done
  79.9 0.6 fusion.2
  80.5 9.3 %all-to-all-done.1 = f32[16,2,1326]{2,1,0:T(2,128)S(1)} async-done(((f32[16,2,1326]{2,1,0:T(2,128)}), f32[16,2,1326]{2,1,0:T(2,128)S(1)}, u32[]{:S(2)}, u32[]{:S(2)}) %all-to-all-start.1) | async-done | bytes 169760 | tf_op jit(solution)/shard_map/all_to_all | solution.py:334
  89.9 0.7 reduce_sum.29
Async XLA Ops:
  0.6 79.3 %copy-start = (f32[1,4,1326]{2,1,0:T(4,128)S(1)}, f32[1,4,1326]{2,1,0:T(4,128)}, u32[]{:S(2)}) copy-start(f32[1,4,1326]{2,1,0:T(4,128)} %flop_regret_in.1) | copy-start | bytes 63652
  22.6 39.4 %collective-permute-start = (f32[4,1326]{1,0:T(4,128)S(1)}, f32[4,1326]{1,0:T(4,128)S(1)}, u32[]{:S(2)}, u32[]{:S(2)}) collective-permute-start(f32[4,1326]{1,0:T(4,128)S(1)} %slice.6), channel_id=1, source_target_pairs={{0,1},{1,0},{2,3},{3,2},{4,5},{5,4},{6,7},{7,6},{8,9},{9,8},{10,11... | collective-permute-start | bytes 63656 | tf_op jit(solution)/shard_map/ppermute | solution.py:384
  29.9 39.0 %all-to-all-start = ((f32[16,2,1326]{2,1,0:T(2,128)}), f32[16,2,1326]{2,1,0:T(2,128)S(1)}, u32[]{:S(2)}, u32[]{:S(2)}) async-start(f32[16,2,1326]{2,1,0:T(2,128)} %broadcast_in_dim.11), calls=%async_computation | async-start | bytes 360448 | tf_op jit(solution)/shard_map/all_to_all | solution.py:334
  62.8 4.3 %collective-permute-start.1 = (f32[4,1326]{1,0:T(4,128)S(1)}, f32[4,1326]{1,0:T(4,128)S(1)}, u32[]{:S(2)}, u32[]{:S(2)}) collective-permute-start(f32[4,1326]{1,0:T(4,128)S(1)} %slice_add_fusion), channel_id=1, source_target_pairs={{0,2},{1,3},{2,0},{3,1},{4,6},{5,7},{6,4},{7,5},{8,10},{9,11},{10,... | collective-permute-start | bytes 63656 | tf_op jit(solution)/shard_map/ppermute | solution.py:384
  69.6 20.3 %all-to-all-start.1 = ((f32[16,2,1326]{2,1,0:T(2,128)}), f32[16,2,1326]{2,1,0:T(2,128)S(1)}, u32[]{:S(2)}, u32[]{:S(2)}) async-start(f32[16,2,1326]{2,1,0:T(2,128)} %broadcast_in_dim.12), calls=%async_computation.1 | async-start | bytes 360448 | tf_op jit(solution)/shard_map/all_to_all | solution.py:334

commit v5 on v3

--- a/solution.py
+++ b/solution.py
@@ -17,8 +17,10 @@
 TS = 24
 RIV = 2
 FLOPS = 64
+NEAR = 16
 BLOCK = 256
-BIG = 2.0**126
+BIG = 2.0**125
+FAR = 2.0**126
 
 bet_sizes = (0.25, 0.5, 1.0, 2.0)
 card_low, card_high = np.triu_indices(CARDS, 1)
@@ -49,7 +51,11 @@
         & (high[:, None] != low[None, :])
         & (high[:, None] != high[None, :])
     )
-    return index, disjoint.astype(jnp.bfloat16)
+    holds = np.zeros((CP, 128), np.float32)
+    holds[np.arange(C), low] = 1.0
+    holds[np.arange(C), high] = 1.0
+    holds[:C, LEFT] = 1.0
+    return index, disjoint.astype(jnp.bfloat16), holds.astype(jnp.bfloat16)
 
 
 BLOCKS = [(start, min(BLOCK, 1136 - start)) for start in range(0, CP, BLOCK)]
@@ -65,16 +71,16 @@
 
 def kernel(
     flop_cards, live_turns, turn_card, river_cards,
-    ranges_in, flop_regret_in, strength_in, turn_regret, index_in, keep_in,
-    new_turn, sums, root,
-    ranges, flop_regret, strength, index, keep,
-    regrets, wide_a, wide_b, lane_a, lane_b, alive_a, alive_b, columns_a, columns_b,
-    found_a, found_b, back_a, back_b, spread_a, spread_b, total, one_total, blank,
+    ranges_in, flop_regret_in, strength_in, turn_regret, index_in, keep_in, holds_in,
+    new_turn, sums, copies, root,
+    ranges, flop_regret, strength, index, keep, holds,
+    regrets, wide_a, wide_b, lane_a, lane_b, struck_a, struck_b, columns_a, columns_b,
+    surplus_a, surplus_b, found_a, found_b, back_a, back_b, spread_a, spread_b, total, one_total, blank,
     small_sems, keep_sems, in_sems, out_sems,
 ):
-    wides, lanes, alives = (wide_a, wide_b), (lane_a, lane_b), (alive_a, alive_b)
+    wides, lanes, strucks = (wide_a, wide_b), (lane_a, lane_b), (struck_a, struck_b)
     columnses, founds, backs = (columns_a, columns_b), (found_a, found_b), (back_a, back_b)
-    spreads = (spread_a, spread_b)
+    spreads, surpluses = (spread_a, spread_b), (surplus_a, surplus_b)
     me = lax.axis_index("turn")
     count = live_turns[0, me]
     pairs = (count + 1) // 2
@@ -105,6 +111,7 @@
                 (flop_regret_in, flop_regret),
                 (index_in, index),
                 (strength_in, strength),
+                (holds_in, holds),
             ]
         )
     ]
@@ -164,7 +171,8 @@
         copy.wait()
 
     def prepare(slot, side):
-        wide, lane, alive, columns, spread = wides[side], lanes[side], alives[side], columnses[side], spreads[side]
+        wide, lane, struck, columns, spread = wides[side], lanes[side], strucks[side], columnses[side], spreads[side]
+        surplus = surpluses[side]
         for b in range(A):
             regret_copy(slot, b).wait()
         first, second = regrets[slot, 0], regrets[slot, 1]
@@ -177,7 +185,9 @@
             + rounded(second_range * sigma_second) * pots[1]
         )
         weight = weight + swap_halves(weight)
-        wide[0, :, :H] = jnp.where(upper, weight, weight - rounded(weight))
+        wide[0, :, :H] = rounded(
+            jnp.where(upper, weight, weight - rounded(weight))
+        )
         spreading = sigma_first * pots[0] + sigma_second * pots[1]
         spread[...] = spreading + swap_halves(spreading)
         wide[1, 4:6, :H] = strength[0, slot] * BIG
@@ -192,9 +202,11 @@
             low = low + (low >= card).astype(jnp.int32)
             high = high + (high >= card).astype(jnp.int32)
         lane[0] = ((low * (2 * CARDS - 1 - low)) >> 1) + high - low - 1
+        rank = []
         for r in range(RIV):
             river = river_cards[0, r, slot]
-            alive[r] = jnp.where((low == river) | (high == river), 0.0, -1.0)
+            struck[r] = jnp.where((low == river) | (high == river), 1.0, 0.0)
+            rank.append(river - sum((card < river).astype(jnp.int32) for card in dead))
         low, high = index[2], index[3]
         lost = (low == dead[0]) | (high == dead[0])
         for card in dead[1:]:
@@ -221,60 +233,84 @@
                 packed[group].append(
                     jnp.where(offset < 128, parts[0], jnp.where(offset < 256, parts[1], parts[2]))
                 )
-        columns[...] = jnp.concatenate(packed[1], axis=1).T
-        given = []
+        reach, rows, given = [], [], []
+        for k in range(CP // 128):
+            blocked = [struck[r, k : k + 1, :] > 0.0 for r in range(RIV)]
+            force = [packed[1][k][4 + r : 5 + r, :] for r in range(RIV)]
+            rows.append([jnp.where(blocked[r], -FAR, force[r]) for r in range(RIV)])
+            columns[128 * k : 128 * (k + 1), :] = jnp.concatenate(
+                [jnp.where(blocked[r], FAR, force[r]) for r in range(RIV)]
+                + [jnp.zeros((8 - RIV, 128), jnp.float32)],
+                axis=0,
+            ).T
+            both = packed[0][k] + swap_halves(packed[0][k])
+            zero = jnp.where(upper, packed[1][k], swap_halves(packed[1][k]))
+            reach.append(jnp.where(upper, both, zero))
+            given.append(jnp.concatenate([packed[0][k], zero], axis=0).astype(jnp.bfloat16))
+        given = jnp.concatenate(given, axis=1)
+
+        held = jnp.dot(given, holds[...], preferred_element_type=jnp.float32)
+        held = jnp.where(upper, held[0:8] + swap_halves(held[0:8]), held[8:16])
+        card = lax.broadcasted_iota(jnp.int32, (8, 128), 1)
+        paired, with_river = jnp.zeros((8, 128), jnp.float32), []
         for r in range(RIV):
-            pieces = []
+            lower, upper_card = jnp.minimum(card, rank[r]), jnp.maximum(card, rank[r])
+            place = ((lower * (2 * LEFT - 1 - lower)) >> 1) + upper_card - lower - 1
+            place = jnp.where((card == rank[r]) | (card >= LEFT), -1, place)
+            spot = place & 127
             for k in range(CP // 128):
-                mask = -alive[r, k : k + 1, :]
-                zeros = jnp.where(upper, packed[1][k], swap_halves(packed[1][k]))
-                pieces.append(
-                    jnp.concatenate([packed[0][k] * mask, zeros * mask], axis=0).astype(jnp.bfloat16)
-                )
-            given.append(jnp.concatenate(pieces, axis=1))
-        return packed, given
-
-    def multiply(side, packed, given):
+                part = jnp.take_along_axis(reach[k], spot, axis=1)
+                paired = paired + jnp.where((place >> 7) == k, part, 0.0)
+            with_river.append(
+                jnp.take_along_axis(held, jnp.broadcast_to(rank[r], (8, 128)), axis=1)
+            )
+        everything = jnp.take_along_axis(held, jnp.full((8, 128), LEFT, jnp.int32), axis=1)
+        for k in range(CP // 128):
+            ends = [jnp.broadcast_to(index[n, k : k + 1, :], (8, 128)) for n in range(2)]
+            excess = with_river[0] + with_river[1]
+            rest = everything + 2.0 * reach[k]
+            for end in ends:
+                excess = excess - jnp.take_along_axis(paired, end, axis=1)
+                rest = rest - jnp.take_along_axis(held, end, axis=1)
+            for r in range(RIV):
+                excess = excess + struck[r, k : k + 1, :] * (rest - with_river[r])
+            surplus[:, 128 * k : 128 * (k + 1)] = excess
+        return rows, given
+
+    def multiply(side, others, given):
         columns, found = columnses[side], founds[side]
         for start, rows in BLOCKS:
             own = [
-                jnp.broadcast_to(columns[start : start + rows, 4 + r : 5 + r], (rows, 128))
+                jnp.broadcast_to(columns[start : start + rows, r : r + 1], (rows, 128))
                 for r in range(RIV)
             ]
             for other in range(0, CP, BLOCK):
                 stop = min(other + BLOCK, CP)
                 most = keep[start : start + rows, other:stop]
                 least = -most
+                outcome = None
                 for r in range(RIV):
                     gap = jnp.concatenate(
-                        [
-                            own[r] - packed[1][k][4 + r : 5 + r, :]
-                            for k in range(other // 128, stop // 128)
-                        ],
-                        axis=1,
+                        [own[r] - others[k][r] for k in range(other // 128, stop // 128)], axis=1
                     ).astype(jnp.bfloat16)
-                    outcome = jnp.maximum(jnp.minimum(gap, most), least)
-                    gave = jnp.dot(
-                        given[r][:, start : start + rows], outcome,
-                        preferred_element_type=jnp.float32,
-                    )
-                    if start == 0:
-                        found[r, :, other:stop] = gave
-                    else:
-                        found[r, :, other:stop] += gave
+                    sign = jnp.maximum(jnp.minimum(gap, most), least)
+                    outcome = sign if outcome is None else outcome + sign
+                gave = jnp.dot(
+                    given[:, start : start + rows], outcome, preferred_element_type=jnp.float32
+                )
+                if start == 0:
+                    found[:, other:stop] = gave
+                else:
+                    found[:, other:stop] += gave
 
     def finish(slot, side, live):
-        lane, alive, found = lanes[side], alives[side], founds[side]
+        lane, found, surplus = lanes[side], founds[side], surpluses[side]
         back, spread = backs[side], spreads[side]
         merged = []
         for k in range(CP // 128):
-            values = [
-                found[r, :, 128 * k : 128 * (k + 1)] * alive[r, k : k + 1, :] for r in range(RIV)
-            ]
-            values = values[0] + values[1]
-            merged.append(
-                jnp.where(upper, values[0:8] + swap_halves(values[0:8]), values[8:16])
-            )
+            values = found[:, 128 * k : 128 * (k + 1)]
+            values = jnp.where(upper, values[0:8] + swap_halves(values[0:8]), values[8:16])
+            merged.append(surplus[:, 128 * k : 128 * (k + 1)] - values)
         for k in range(HP // 128):
             place = jnp.broadcast_to(lane[1, k : k + 1, :], (8, 128))
             spot = place & 127
@@ -307,10 +343,17 @@
 
     lax.fori_loop(0, pairs, pair_step, 0)
     whole = total[0:4, :H]
-    sums[0:4, :] = whole
+    sums[...] = whole
     scale = 1.0 / (TURNS * FLOPS)
-    sums[4:5, :] = jnp.sum(sigma_flop * whole, axis=0, keepdims=True) * scale
-    sums[5:6, :] = jnp.sum(one_total[0:4, :], axis=0, keepdims=True) * scale
+    parts = jnp.concatenate(
+        [
+            jnp.sum(sigma_flop * whole, axis=0, keepdims=True) * scale,
+            jnp.sum(one_total[0:4, :], axis=0, keepdims=True) * scale,
+        ],
+        axis=0,
+    )
+    for n in range(NEAR):
+        copies[n] = parts
     root[...] = sigma_flop
 
     def settle(slot, carry):
@@ -327,46 +370,54 @@
     lax.fori_loop(used, TS, settle_blank, 0)
 
 
-def group_sum(x, axis, groups=None):
-    size = lax.axis_size(axis) if groups is None else len(groups[0])
-    copies = jnp.broadcast_to(x, (size, *x.shape))
-    return jnp.sum(lax.all_to_all(copies, axis, 0, 0, axis_index_groups=groups, tiled=True), axis=0)
+def group_sum(copies, axis, groups):
+    return jnp.sum(
+        lax.all_to_all(copies, axis, 0, 0, axis_index_groups=groups, tiled=True), axis=0
+    )
+
+
+def flip_sum(x, axis, flip):
+    size = lax.axis_size(axis)
+    return x + lax.ppermute(x, axis, [(n, n ^ flip) for n in range(size)])
 
 
 def on_device(
     ranges, flop_regret, flop_cards, live_turns, turn_card, river_cards, strength, turn_regret
 ):
-    index, disjoint = tables()
+    index, disjoint, holds = tables()
     smem = pl.BlockSpec(memory_space=pltpu.SMEM)
     vmem = pl.BlockSpec(memory_space=pltpu.VMEM)
     hbm = pl.BlockSpec(memory_space=pltpu.HBM)
-    new_turn, sums, sigma_flop = pl.pallas_call(
+    new_turn, sums, copies, sigma_flop = pl.pallas_call(
         kernel,
         out_shape=(
             jax.ShapeDtypeStruct(turn_regret.shape, jnp.float32),
-            jax.ShapeDtypeStruct((6, H), jnp.float32),
+            jax.ShapeDtypeStruct((A, H), jnp.float32),
+            jax.ShapeDtypeStruct((NEAR, 2, H), jnp.float32),
             jax.ShapeDtypeStruct((A, H), jnp.float32),
         ),
-        in_specs=[smem] * 4 + [hbm] * 6,
-        out_specs=(hbm, vmem, vmem),
+        in_specs=[smem] * 4 + [hbm] * 7,
+        out_specs=(hbm, vmem, vmem, vmem),
         scratch_shapes=[
             pltpu.VMEM((2, H), jnp.float32),
             pltpu.VMEM((1, A, H), jnp.float32),
             pltpu.VMEM((1, TS, RIV, H), jnp.float32),
             pltpu.VMEM((4, 16, 128), jnp.int32),
             pltpu.VMEM((CP, CP), jnp.bfloat16),
+            pltpu.VMEM((CP, 128), jnp.bfloat16),
             pltpu.VMEM((TS, 2, 8, H), jnp.float32),
             *[pltpu.VMEM((2, 8, HP), jnp.float32)] * 2,
             *[pltpu.VMEM((2, 16, 128), jnp.int32)] * 2,
             *[pltpu.VMEM((RIV, 16, 128), jnp.float32)] * 2,
             *[pltpu.VMEM((CP, 8), jnp.float32)] * 2,
-            *[pltpu.VMEM((RIV, 16, CP), jnp.float32)] * 2,
+            *[pltpu.VMEM((8, CP), jnp.float32)] * 2,
+            *[pltpu.VMEM((16, CP), jnp.float32)] * 2,
             *[pltpu.VMEM((8, HP), jnp.float32)] * 2,
             *[pltpu.VMEM((8, H), jnp.float32)] * 2,
             pltpu.VMEM((8, HP), jnp.float32),
             pltpu.VMEM((8, H), jnp.float32),
             pltpu.VMEM((A, A, H), jnp.float32),
-            pltpu.SemaphoreType.DMA((4,)),
+            pltpu.SemaphoreType.DMA((5,)),
             pltpu.SemaphoreType.DMA((len(BLOCKS),)),
             pltpu.SemaphoreType.DMA((TS, A)),
             pltpu.SemaphoreType.DMA((TS, A)),
@@ -375,18 +426,25 @@
         name="subtrees",
     )(
         flop_cards, live_turns, turn_card, jnp.swapaxes(river_cards, 1, 2),
-        ranges, flop_regret, strength, turn_regret, jnp.asarray(index), jnp.asarray(disjoint),
+        ranges, flop_regret, strength, turn_regret, jnp.asarray(index), jnp.asarray(disjoint), jnp.asarray(holds),
     )
     regrets_flop = flop_regret[0]
-    turns = group_sum(sums, "turn")
-    action_value = turns[0:4] / TURNS
+    turns = flip_sum(sums, "turn", 1)
+    if lax.axis_size("flop") == FLOPS:
+        near = np.arange(4 * FLOPS).reshape(8, 4, 2, 4).transpose(0, 2, 1, 3).reshape(16, NEAR)
+        far = np.arange(FLOPS).reshape(8, 8).T
+        root_value = group_sum(copies, ("flop", "turn"), near.tolist())
+        root_value = flip_sum(root_value, "flop", 1)
+        root_value, turns = lax.optimization_barrier((root_value, turns))
+        root_value = group_sum(
+            jnp.broadcast_to(root_value, (8, *root_value.shape)), "flop", far.tolist()
+        )
+    else:
+        root_value = lax.psum(copies[0], "turn")
+    turns = flip_sum(turns, "turn", 2)
+    action_value = turns / TURNS
     node_zero = jnp.sum(sigma_flop * action_value, axis=0)
     new_flop = jnp.maximum(regrets_flop + action_value - node_zero[None, :], 0.0)
-    near = [[8 * z + k for k in range(8)] for z in range(8)]
-    far = [[8 * z + k for z in range(8)] for k in range(8)]
-    root_value = turns[4:6]
-    if lax.axis_size("flop") == FLOPS:
-        root_value = group_sum(group_sum(root_value, "flop", near), "flop", far)
     return (new_flop[None], new_turn, root_value)
 
 

time: 87 us -> 93.7 us (1.077)
  starting transfers between devices: 13.3 us -> 54 us
  blocking collectives: 34.1 us -> 0 us
  local copies, waits for them, and re-layouts: 2.11 us -> 0.66 us
    all_to_all x2, starting transfers between devices: 13.3 us -> 49 us  [group_sum(): lax.all_to_all(copies, axis, 0, 0, axis_index_groups=groups, tiled=True)]
    all_to_all x1 -> x0, blocking collectives: 34.1 us -> none  [group_sum(): lax.all_to_all(copies, axis, 0, 0, axis_index_groups=groups, tiled=True)]
    ppermute x0 -> x3, starting transfers between devices: none -> 4.99 us  [flip_sum(): return x + lax.ppermute(x, axis, [(n, n ^ flip) for n in range(size)])]
    broadcast_in_dim x3 -> x1, local copies, waits for them, and re-layouts: 2.09 us -> 0.66 us  [on_device(): jnp.broadcast_to(root_value, (8, *root_value.shape))]
  transfers between devices with their start and end apart: 2 -> 5, of which waited for: 2 -> 3; matrix products, arithmetic and copies ran while one was open for 2% -> 3% of each run, Pallas kernels for 0% -> 0%
where the time goes in v5:
time: 93.7 us; the launch traced here: 93.4 us
  starting transfers between devices  54 us (58%)
  Pallas kernels  23.3 us (25%)
  waiting for transfers between devices  11.9 us (13%)
  other arithmetic  2.84 us (3%)
    all_to_all x2, starting transfers between devices, group_sum(): lax.all_to_all(copies, axis, 0, 0, axis_index_groups=groups, tiled=True)  49 us
    pallas_call x1, Pallas kernels, on_device(): pl.pallas_call(kernel, out_shape=(jax.ShapeDtypeStruct(turn_regret.shape,...  23.3 us
    all_to_all x2, waiting for transfers between devices, group_sum(): lax.all_to_all(copies, axis, 0, 0, axis_index_groups=groups, tiled=True)  11.8 us
    ppermute x3, starting transfers between devices, flip_sum(): return x + lax.ppermute(x, axis, [(n, n ^ flip) for n in range(size)])  4.99 us
  transfers between devices with their start and end apart: 5, of which 3 were waited for; matrix products, arithmetic and copies ran while one was open for 3% of the time, Pallas kernels for 0%

profile of v5, /device:TPU:1, one launch (start us, length us, event | category | flops | bytes accessed | tf_op | source)
XLA Modules:
  0.0 93.4 jit_solution(3928725751175020685)
XLA Ops:
  0.6 0.0 copy-start
  0.6 23.3 %subtrees.1 = (f32[1,24,4,4,1326]{4,3,2,1,0:T(4,128)}, f32[4,1326]{1,0:T(4,128)}, f32[16,2,1326]{2,1,0:T(2,128)}, f32[4,1326]{1,0:T(4,128)}) custom-call(s32[1,3]{1,0:T(1,128)} %flop_cards.1, s32[1,4]{1,0:T(1,128)} %live_turns.1, s32[1,24]{1,0:T(1,128)} %turn_card.1, s32[1,2,24]{2,1,0:T(2,128)} %bitcast.11, f32[2,1326]{1,0:T(2,128)} %ranges_in.1, ...), custom_call_target="tpu_custom_call" | custom-call | tf_op jit(solution)/shard_map/subtrees/pallas_call | solution.py:391
  24.0 40.8 %all-to-all-start = ((f32[16,2,1326]{2,1,0:T(2,128)}), f32[16,2,1326]{2,1,0:T(2,128)S(1)}, u32[]{:S(2)}, u32[]{:S(2)}) async-start(f32[16,2,1326]{2,1,0:T(2,128)} %get-tuple-element.9), calls=%async_computation | async-start | bytes 360448 | tf_op jit(solution)/shard_map/all_to_all | solution.py:375
  64.8 1.4 %collective-permute-start.1 = (f32[4,1326]{1,0:T(4,128)}, f32[4,1326]{1,0:T(4,128)S(1)}, u32[]{:S(2)}, u32[]{:S(2)}) collective-permute-start(f32[4,1326]{1,0:T(4,128)} %get-tuple-element.10), channel_id=1, source_target_pairs={{0,1},{1,0},{2,3},{3,2},{4,5},{5,4},{6,7},{7,6},{8,9},{9,8},{10,11... | collective-permute-start | bytes 63656 | tf_op jit(solution)/shard_map/ppermute | solution.py:381
  66.2 5.6 %all-to-all-done = f32[16,2,1326]{2,1,0:T(2,128)S(1)} async-done(((f32[16,2,1326]{2,1,0:T(2,128)}), f32[16,2,1326]{2,1,0:T(2,128)S(1)}, u32[]{:S(2)}, u32[]{:S(2)}) %all-to-all-start) | async-done | bytes 169760 | tf_op jit(solution)/shard_map/all_to_all | solution.py:375
  71.8 0.1 reduce_sum.27
  71.8 2.3 %collective-permute-start = (f32[2,1326]{1,0:T(2,128)S(1)}, f32[2,1326]{1,0:T(2,128)S(1)}, u32[]{:S(2)}, u32[]{:S(2)}) collective-permute-start(f32[2,1326]{1,0:T(2,128)S(1)} %reduce_sum.27), channel_id=1, source_target_pairs={{0,4},{4,0},{8,12},{12,8},{16,20},{20,16},{24,28},{28,24},{32,36},... | collective-permute-start | bytes 31832 | tf_op jit(solution)/shard_map/ppermute | solution.py:381
  74.2 0.0 collective-permute-done.1
  74.2 0.7 add.13
  74.9 0.1 collective-permute-done
  75.0 1.3 %collective-permute-start.2 = (f32[4,1326]{1,0:T(4,128)S(1)}, f32[4,1326]{1,0:T(4,128)S(1)}, u32[]{:S(2)}, u32[]{:S(2)}) collective-permute-start(f32[4,1326]{1,0:T(4,128)S(1)} %add.13), channel_id=1, source_target_pairs={{0,2},{1,3},{2,0},{3,1},{4,6},{5,7},{6,4},{7,5},{8,10},{9,11},{10,... | collective-permute-start | bytes 63656 | tf_op jit(solution)/shard_map/ppermute | solution.py:381
  76.3 0.7 broadcast_in_dim.8
  77.0 8.2 %all-to-all-start.1 = ((f32[8,2,1326]{2,1,0:T(2,128)}), f32[8,2,1326]{2,1,0:T(2,128)S(1)}, u32[]{:S(2)}, u32[]{:S(2)}) async-start(f32[8,2,1326]{2,1,0:T(2,128)} %broadcast_in_dim.8), calls=%async_computation.1 | async-start | bytes 180224 | tf_op jit(solution)/shard_map/all_to_all | solution.py:375
  85.2 0.0 collective-permute-done.2
  85.2 0.8 multiply_reduce_fusion
  85.9 0.0 copy-done
  85.9 0.6 fusion.2
  86.6 6.2 %all-to-all-done.1 = f32[8,2,1326]{2,1,0:T(2,128)S(1)} async-done(((f32[8,2,1326]{2,1,0:T(2,128)}), f32[8,2,1326]{2,1,0:T(2,128)S(1)}, u32[]{:S(2)}, u32[]{:S(2)}) %all-to-all-start.1) | async-done | bytes 84896 | tf_op jit(solution)/shard_map/all_to_all | solution.py:375
  92.8 0.6 reduce_sum.29
  (1 shorter events, 0.0 us)
Async XLA Ops:
  0.6 85.3 %copy-start = (f32[1,4,1326]{2,1,0:T(4,128)S(1)}, f32[1,4,1326]{2,1,0:T(4,128)}, u32[]{:S(2)}) copy-start(f32[1,4,1326]{2,1,0:T(4,128)} %flop_regret_in.1) | copy-start | bytes 63652
  24.0 47.8 %all-to-all-start = ((f32[16,2,1326]{2,1,0:T(2,128)}), f32[16,2,1326]{2,1,0:T(2,128)S(1)}, u32[]{:S(2)}, u32[]{:S(2)}) async-start(f32[16,2,1326]{2,1,0:T(2,128)} %get-tuple-element.9), calls=%async_computation | async-start | bytes 360448 | tf_op jit(solution)/shard_map/all_to_all | solution.py:375
  64.8 9.4 %collective-permute-start.1 = (f32[4,1326]{1,0:T(4,128)}, f32[4,1326]{1,0:T(4,128)S(1)}, u32[]{:S(2)}, u32[]{:S(2)}) collective-permute-start(f32[4,1326]{1,0:T(4,128)} %get-tuple-element.10), channel_id=1, source_target_pairs={{0,1},{1,0},{2,3},{3,2},{4,5},{5,4},{6,7},{7,6},{8,9},{9,8},{10,11... | collective-permute-start | bytes 63656 | tf_op jit(solution)/shard_map/ppermute | solution.py:381
  71.8 3.2 %collective-permute-start = (f32[2,1326]{1,0:T(2,128)S(1)}, f32[2,1326]{1,0:T(2,128)S(1)}, u32[]{:S(2)}, u32[]{:S(2)}) collective-permute-start(f32[2,1326]{1,0:T(2,128)S(1)} %reduce_sum.27), channel_id=1, source_target_pairs={{0,4},{4,0},{8,12},{12,8},{16,20},{20,16},{24,28},{28,24},{32,36},... | collective-permute-start | bytes 31832 | tf_op jit(solution)/shard_map/ppermute | solution.py:381
  75.0 10.1 %collective-permute-start.2 = (f32[4,1326]{1,0:T(4,128)S(1)}, f32[4,1326]{1,0:T(4,128)S(1)}, u32[]{:S(2)}, u32[]{:S(2)}) collective-permute-start(f32[4,1326]{1,0:T(4,128)S(1)} %add.13), channel_id=1, source_target_pairs={{0,2},{1,3},{2,0},{3,1},{4,6},{5,7},{6,4},{7,5},{8,10},{9,11},{10,... | collective-permute-start | bytes 63656 | tf_op jit(solution)/shard_map/ppermute | solution.py:381
  77.0 15.8 %all-to-all-start.1 = ((f32[8,2,1326]{2,1,0:T(2,128)}), f32[8,2,1326]{2,1,0:T(2,128)S(1)}, u32[]{:S(2)}, u32[]{:S(2)}) async-start(f32[8,2,1326]{2,1,0:T(2,128)} %broadcast_in_dim.8), calls=%async_computation.1 | async-start | bytes 180224 | tf_op jit(solution)/shard_map/all_to_all | solution.py:375

commit v6 on v3

--- a/solution.py
+++ b/solution.py
@@ -17,6 +17,7 @@
 TS = 24
 RIV = 2
 FLOPS = 64
+NEAR = 16
 BLOCK = 256
 BIG = 2.0**126
 
@@ -66,7 +67,7 @@
 def kernel(
     flop_cards, live_turns, turn_card, river_cards,
     ranges_in, flop_regret_in, strength_in, turn_regret, index_in, keep_in,
-    new_turn, sums, root,
+    new_turn, sums, copies, root,
     ranges, flop_regret, strength, index, keep,
     regrets, wide_a, wide_b, lane_a, lane_b, alive_a, alive_b, columns_a, columns_b,
     found_a, found_b, back_a, back_b, spread_a, spread_b, total, one_total, blank,
@@ -241,27 +242,20 @@
                 jnp.broadcast_to(columns[start : start + rows, 4 + r : 5 + r], (rows, 128))
                 for r in range(RIV)
             ]
-            for other in range(0, CP, BLOCK):
-                stop = min(other + BLOCK, CP)
-                most = keep[start : start + rows, other:stop]
-                least = -most
-                for r in range(RIV):
-                    gap = jnp.concatenate(
-                        [
-                            own[r] - packed[1][k][4 + r : 5 + r, :]
-                            for k in range(other // 128, stop // 128)
-                        ],
-                        axis=1,
-                    ).astype(jnp.bfloat16)
-                    outcome = jnp.maximum(jnp.minimum(gap, most), least)
-                    gave = jnp.dot(
-                        given[r][:, start : start + rows], outcome,
-                        preferred_element_type=jnp.float32,
-                    )
-                    if start == 0:
-                        found[r, :, other:stop] = gave
-                    else:
-                        found[r, :, other:stop] += gave
+            most = keep[start : start + rows, :]
+            least = -most
+            for r in range(RIV):
+                gap = jnp.concatenate(
+                    [own[r] - packed[1][k][4 + r : 5 + r, :] for k in range(CP // 128)], axis=1
+                ).astype(jnp.bfloat16)
+                outcome = jnp.maximum(jnp.minimum(gap, most), least)
+                gave = jnp.dot(
+                    given[r][:, start : start + rows], outcome, preferred_element_type=jnp.float32
+                )
+                if start == 0:
+                    found[r] = gave
+                else:
+                    found[r] += gave
 
     def finish(slot, side, live):
         lane, alive, found = lanes[side], alives[side], founds[side]
@@ -307,10 +301,17 @@
 
     lax.fori_loop(0, pairs, pair_step, 0)
     whole = total[0:4, :H]
-    sums[0:4, :] = whole
+    sums[...] = whole
     scale = 1.0 / (TURNS * FLOPS)
-    sums[4:5, :] = jnp.sum(sigma_flop * whole, axis=0, keepdims=True) * scale
-    sums[5:6, :] = jnp.sum(one_total[0:4, :], axis=0, keepdims=True) * scale
+    parts = jnp.concatenate(
+        [
+            jnp.sum(sigma_flop * whole, axis=0, keepdims=True) * scale,
+            jnp.sum(one_total[0:4, :], axis=0, keepdims=True) * scale,
+        ],
+        axis=0,
+    )
+    for n in range(NEAR):
+        copies[n] = parts
     root[...] = sigma_flop
 
     def settle(slot, carry):
@@ -327,10 +328,15 @@
     lax.fori_loop(used, TS, settle_blank, 0)
 
 
-def group_sum(x, axis, groups=None):
-    size = lax.axis_size(axis) if groups is None else len(groups[0])
-    copies = jnp.broadcast_to(x, (size, *x.shape))
-    return jnp.sum(lax.all_to_all(copies, axis, 0, 0, axis_index_groups=groups, tiled=True), axis=0)
+def group_sum(copies, axis, groups):
+    return jnp.sum(
+        lax.all_to_all(copies, axis, 0, 0, axis_index_groups=groups, tiled=True), axis=0
+    )
+
+
+def flip_sum(x, axis, flip):
+    size = lax.axis_size(axis)
+    return x + lax.ppermute(x, axis, [(n, n ^ flip) for n in range(size)])
 
 
 def on_device(
@@ -340,15 +346,16 @@
     smem = pl.BlockSpec(memory_space=pltpu.SMEM)
     vmem = pl.BlockSpec(memory_space=pltpu.VMEM)
     hbm = pl.BlockSpec(memory_space=pltpu.HBM)
-    new_turn, sums, sigma_flop = pl.pallas_call(
+    new_turn, sums, copies, sigma_flop = pl.pallas_call(
         kernel,
         out_shape=(
             jax.ShapeDtypeStruct(turn_regret.shape, jnp.float32),
-            jax.ShapeDtypeStruct((6, H), jnp.float32),
+            jax.ShapeDtypeStruct((A, H), jnp.float32),
+            jax.ShapeDtypeStruct((NEAR, 2, H), jnp.float32),
             jax.ShapeDtypeStruct((A, H), jnp.float32),
         ),
         in_specs=[smem] * 4 + [hbm] * 6,
-        out_specs=(hbm, vmem, vmem),
+        out_specs=(hbm, vmem, vmem, vmem),
         scratch_shapes=[
             pltpu.VMEM((2, H), jnp.float32),
             pltpu.VMEM((1, A, H), jnp.float32),
@@ -378,15 +385,21 @@
         ranges, flop_regret, strength, turn_regret, jnp.asarray(index), jnp.asarray(disjoint),
     )
     regrets_flop = flop_regret[0]
-    turns = group_sum(sums, "turn")
-    action_value = turns[0:4] / TURNS
+    others = [lax.ppermute(sums, "turn", [(n, n ^ flip) for n in range(4)]) for flip in (1, 2, 3)]
+    if lax.axis_size("flop") == FLOPS:
+        near = np.arange(4 * FLOPS).reshape(8, 4, 2, 4).transpose(0, 2, 1, 3).reshape(16, NEAR)
+        far = np.arange(FLOPS).reshape(8, 8).T
+        root_value = group_sum(copies, ("flop", "turn"), near.tolist())
+        root_value = flip_sum(root_value, "flop", 1)
+        root_value, others = lax.optimization_barrier((root_value, others))
+        root_value = group_sum(
+            jnp.broadcast_to(root_value, (8, *root_value.shape)), "flop", far.tolist()
+        )
+    else:
+        root_value = lax.psum(copies[0], "turn")
+    action_value = ((sums + others[0]) + (others[1] + others[2])) / TURNS
     node_zero = jnp.sum(sigma_flop * action_value, axis=0)
     new_flop = jnp.maximum(regrets_flop + action_value - node_zero[None, :], 0.0)
-    near = [[8 * z + k for k in range(8)] for z in range(8)]
-    far = [[8 * z + k for z in range(8)] for k in range(8)]
-    root_value = turns[4:6]
-    if lax.axis_size("flop") == FLOPS:
-        root_value = group_sum(group_sum(root_value, "flop", near), "flop", far)
     return (new_flop[None], new_turn, root_value)
 
 

time: 87 us -> 82.9 us (0.953)
  blocking collectives: 34.1 us -> 0 us
  Pallas kernels: 23.2 us -> 47.5 us
  starting transfers between devices: 13.3 us -> 21.1 us
  local copies, waits for them, and re-layouts: 2.11 us -> 0.66 us
    all_to_all x1 -> x0, blocking collectives: 34.1 us -> none  [group_sum(): lax.all_to_all(copies, axis, 0, 0, axis_index_groups=groups, tiled=True)]
    pallas_call x1, Pallas kernels: 23.2 us -> 47.5 us  [on_device(): pl.pallas_call(kernel, out_shape=(jax.ShapeDtypeStruct(turn_regret.shape,...]
    ppermute x0 -> x4, starting transfers between devices: none -> 5.54 us  [the longest x3 3.34 us: on_device(): lax.ppermute(sums, 'turn', [(n, n ^ flip) for n in range(4)])]
    all_to_all x2, starting transfers between devices: 13.3 us -> 15.5 us  [group_sum(): lax.all_to_all(copies, axis, 0, 0, axis_index_groups=groups, tiled=True)]
    all_to_all x2, waiting for transfers between devices: 11.2 us -> 9.62 us  [group_sum(): lax.all_to_all(copies, axis, 0, 0, axis_index_groups=groups, tiled=True)]
    broadcast_in_dim x3 -> x1, local copies, waits for them, and re-layouts: 2.09 us -> 0.65 us  [on_device(): jnp.broadcast_to(root_value, (8, *root_value.shape))]
  transfers between devices with their start and end apart: 2 -> 6, of which waited for: 2 -> 3; matrix products, arithmetic and copies ran while one was open for 2% -> 2% of each run, Pallas kernels for 0% -> 0%
where the time goes in v6:
time: 82.9 us; the launch traced here: 82.5 us
  Pallas kernels  47.5 us (57%)
  starting transfers between devices  21.1 us (25%)
  waiting for transfers between devices  10.5 us (13%)
  other arithmetic  2.12 us (3%)
    pallas_call x1, Pallas kernels, on_device(): pl.pallas_call(kernel, out_shape=(jax.ShapeDtypeStruct(turn_regret.shape,...  47.5 us
    all_to_all x2, starting transfers between devices, group_sum(): lax.all_to_all(copies, axis, 0, 0, axis_index_groups=groups, tiled=True)  15.5 us
    all_to_all x2, waiting for transfers between devices, group_sum(): lax.all_to_all(copies, axis, 0, 0, axis_index_groups=groups, tiled=True)  9.62 us
    ppermute x3, starting transfers between devices, on_device(): lax.ppermute(sums, 'turn', [(n, n ^ flip) for n in range(4)])  3.34 us
    ppermute x1, starting transfers between devices, flip_sum(): return x + lax.ppermute(x, axis, [(n, n ^ flip) for n in range(size)])  2.2 us
  transfers between devices with their start and end apart: 6, of which 3 were waited for; matrix products, arithmetic and copies ran while one was open for 2% of the time, Pallas kernels for 0%

profile of v6, /device:TPU:1, one launch (start us, length us, event | category | flops | bytes accessed | tf_op | source)
XLA Modules:
  0.0 82.5 jit_solution(3068562965525196551)
XLA Ops:
  0.6 0.0 copy-start
  0.6 47.5 %subtrees.1 = (f32[1,24,4,4,1326]{4,3,2,1,0:T(4,128)}, f32[4,1326]{1,0:T(4,128)}, f32[16,2,1326]{2,1,0:T(2,128)}, f32[4,1326]{1,0:T(4,128)}) custom-call(s32[1,3]{1,0:T(1,128)} %flop_cards.1, s32[1,4]{1,0:T(1,128)} %live_turns.1, s32[1,24]{1,0:T(1,128)} %turn_card.1, s32[1,2,24]{2,1,0:T(2,128)} %bitcast.11, f32[2,1326]{1,0:T(2,128)} %ranges_in.1, ...), custom_call_target="tpu_custom_call" | custom-call | tf_op jit(solution)/shard_map/subtrees/pallas_call | solution.py:349
  48.1 7.3 %all-to-all-start = ((f32[16,2,1326]{2,1,0:T(2,128)}), f32[16,2,1326]{2,1,0:T(2,128)S(1)}, u32[]{:S(2)}, u32[]{:S(2)}) async-start(f32[16,2,1326]{2,1,0:T(2,128)} %get-tuple-element.12), calls=%async_computation | async-start | bytes 360448 | tf_op jit(solution)/shard_map/all_to_all | solution.py:333
  55.5 2.6 %collective-permute-start.3 = (f32[4,1326]{1,0:T(4,128)}, f32[4,1326]{1,0:T(4,128)S(1)}, u32[]{:S(2)}, u32[]{:S(2)}) collective-permute-start(f32[4,1326]{1,0:T(4,128)} %get-tuple-element.11), channel_id=1, source_target_pairs={{0,3},{1,2},{2,1},{3,0},{4,7},{5,6},{6,5},{7,4},{8,11},{9,10},{10,... | collective-permute-start | bytes 63656 | tf_op jit(solution)/shard_map/ppermute | solution.py:388
  58.1 0.6 collective-permute-start.2
  58.6 0.2 collective-permute-start.1
  58.8 3.7 %all-to-all-done = f32[16,2,1326]{2,1,0:T(2,128)S(1)} async-done(((f32[16,2,1326]{2,1,0:T(2,128)}), f32[16,2,1326]{2,1,0:T(2,128)S(1)}, u32[]{:S(2)}, u32[]{:S(2)}) %all-to-all-start) | async-done | bytes 169760 | tf_op jit(solution)/shard_map/all_to_all | solution.py:333
  62.5 0.1 reduce_sum.27
  62.5 2.2 %collective-permute-start = (f32[2,1326]{1,0:T(2,128)S(1)}, f32[2,1326]{1,0:T(2,128)S(1)}, u32[]{:S(2)}, u32[]{:S(2)}) collective-permute-start(f32[2,1326]{1,0:T(2,128)S(1)} %reduce_sum.27), channel_id=1, source_target_pairs={{0,4},{4,0},{8,12},{12,8},{16,20},{20,16},{24,28},{28,24},{32,36},... | collective-permute-start | bytes 31832 | tf_op jit(solution)/shard_map/ppermute | solution.py:339
  64.7 0.8 %collective-permute-done = f32[2,1326]{1,0:T(2,128)S(1)} collective-permute-done((f32[2,1326]{1,0:T(2,128)S(1)}, f32[2,1326]{1,0:T(2,128)S(1)}, u32[]{:S(2)}, u32[]{:S(2)}) %collective-permute-start) | collective-permute-done | bytes 10640 | tf_op jit(solution)/shard_map/ppermute | solution.py:339
  65.6 0.0 collective-permute-done.3
  65.6 0.0 collective-permute-done.2
  65.6 0.0 collective-permute-done.1
  65.6 0.7 broadcast_in_dim.8
  66.3 8.2 %all-to-all-start.1 = ((f32[8,2,1326]{2,1,0:T(2,128)}), f32[8,2,1326]{2,1,0:T(2,128)S(1)}, u32[]{:S(2)}, u32[]{:S(2)}) async-start(f32[8,2,1326]{2,1,0:T(2,128)} %broadcast_in_dim.8), calls=%async_computation.1 | async-start | bytes 180224 | tf_op jit(solution)/shard_map/all_to_all | solution.py:333
  74.4 0.8 multiply_reduce_fusion
  75.2 0.0 copy-done
  75.2 0.6 fusion.2
  75.9 6.0 %all-to-all-done.1 = f32[8,2,1326]{2,1,0:T(2,128)S(1)} async-done(((f32[8,2,1326]{2,1,0:T(2,128)}), f32[8,2,1326]{2,1,0:T(2,128)S(1)}, u32[]{:S(2)}, u32[]{:S(2)}) %all-to-all-start.1) | async-done | bytes 84896 | tf_op jit(solution)/shard_map/all_to_all | solution.py:333
  81.8 0.6 reduce_sum.29
  (1 shorter events, 0.0 us)
Async XLA Ops:
  0.6 74.6 %copy-start = (f32[1,4,1326]{2,1,0:T(4,128)S(1)}, f32[1,4,1326]{2,1,0:T(4,128)}, u32[]{:S(2)}) copy-start(f32[1,4,1326]{2,1,0:T(4,128)} %flop_regret_in.1) | copy-start | bytes 63652
  48.1 14.3 %all-to-all-start = ((f32[16,2,1326]{2,1,0:T(2,128)}), f32[16,2,1326]{2,1,0:T(2,128)S(1)}, u32[]{:S(2)}, u32[]{:S(2)}) async-start(f32[16,2,1326]{2,1,0:T(2,128)} %get-tuple-element.12), calls=%async_computation | async-start | bytes 360448 | tf_op jit(solution)/shard_map/all_to_all | solution.py:333
  55.5 10.1 %collective-permute-start.3 = (f32[4,1326]{1,0:T(4,128)}, f32[4,1326]{1,0:T(4,128)S(1)}, u32[]{:S(2)}, u32[]{:S(2)}) collective-permute-start(f32[4,1326]{1,0:T(4,128)} %get-tuple-element.11), channel_id=1, source_target_pairs={{0,3},{1,2},{2,1},{3,0},{4,7},{5,6},{6,5},{7,4},{8,11},{9,10},{10,... | collective-permute-start | bytes 63656 | tf_op jit(solution)/shard_map/ppermute | solution.py:388
  58.1 7.5 %collective-permute-start.2 = (f32[4,1326]{1,0:T(4,128)}, f32[4,1326]{1,0:T(4,128)S(1)}, u32[]{:S(2)}, u32[]{:S(2)}) collective-permute-start(f32[4,1326]{1,0:T(4,128)} %get-tuple-element.11), channel_id=1, source_target_pairs={{0,2},{1,3},{2,0},{3,1},{4,6},{5,7},{6,4},{7,5},{8,10},{9,11},{10,... | collective-permute-start | bytes 63656 | tf_op jit(solution)/shard_map/ppermute | solution.py:388
  58.6 7.0 %collective-permute-start.1 = (f32[4,1326]{1,0:T(4,128)}, f32[4,1326]{1,0:T(4,128)S(1)}, u32[]{:S(2)}, u32[]{:S(2)}) collective-permute-start(f32[4,1326]{1,0:T(4,128)} %get-tuple-element.11), channel_id=1, source_target_pairs={{0,1},{1,0},{2,3},{3,2},{4,5},{5,4},{6,7},{7,6},{8,9},{9,8},{10,11... | collective-permute-start | bytes 63656 | tf_op jit(solution)/shard_map/ppermute | solution.py:388
  62.5 3.0 %collective-permute-start = (f32[2,1326]{1,0:T(2,128)S(1)}, f32[2,1326]{1,0:T(2,128)S(1)}, u32[]{:S(2)}, u32[]{:S(2)}) collective-permute-start(f32[2,1326]{1,0:T(2,128)S(1)} %reduce_sum.27), channel_id=1, source_target_pairs={{0,4},{4,0},{8,12},{12,8},{16,20},{20,16},{24,28},{28,24},{32,36},... | collective-permute-start | bytes 31832 | tf_op jit(solution)/shard_map/ppermute | solution.py:339
  66.3 15.6 %all-to-all-start.1 = ((f32[8,2,1326]{2,1,0:T(2,128)}), f32[8,2,1326]{2,1,0:T(2,128)S(1)}, u32[]{:S(2)}, u32[]{:S(2)}) async-start(f32[8,2,1326]{2,1,0:T(2,128)} %broadcast_in_dim.8), calls=%async_computation.1 | async-start | bytes 180224 | tf_op jit(solution)/shard_map/all_to_all | solution.py:333

commit v7 on v6

--- a/solution.py
+++ b/solution.py
@@ -70,7 +70,7 @@
     new_turn, sums, copies, root,
     ranges, flop_regret, strength, index, keep,
     regrets, wide_a, wide_b, lane_a, lane_b, alive_a, alive_b, columns_a, columns_b,
-    found_a, found_b, back_a, back_b, spread_a, spread_b, total, one_total, blank,
+    found_a, found_b, back_a, back_b, spread_a, spread_b, total, one_total, blank, selector,
     small_sems, keep_sems, in_sems, out_sems,
 ):
     wides, lanes, alives = (wide_a, wide_b), (lane_a, lane_b), (alive_a, alive_b)
@@ -137,6 +137,13 @@
         return carry
 
     lax.fori_loop(used, TS, clear, 0)
+    part = lax.broadcasted_iota(jnp.int32, (128, 128 * RIV), 0)
+    side_of = lax.broadcasted_iota(jnp.int32, (128, 128 * RIV), 1) >> 7
+    selector[...] = jnp.where((part < 3 * RIV) & ((part & 1) == side_of), 1.0, 0.0).astype(
+        jnp.bfloat16
+    )
+    for ref in columnses:
+        ref[...] = jnp.zeros_like(ref)
     for ref in wides + backs:
         ref[...] = jnp.zeros_like(ref)
     total[...] = jnp.zeros_like(total)
@@ -222,7 +229,16 @@
                 packed[group].append(
                     jnp.where(offset < 128, parts[0], jnp.where(offset < 256, parts[1], parts[2]))
                 )
-        columns[...] = jnp.concatenate(packed[1], axis=1).T
+        for k in range(CP // 128):
+            force = packed[1][k][4 : 4 + RIV, :]
+            parts = []
+            for _ in range(3):
+                parts.append(rounded(force))
+                force = force - parts[-1]
+            parts.append(jnp.zeros((8 - 3 * RIV, 128), jnp.float32))
+            columns[128 * k : 128 * (k + 1), 0:8] = jnp.concatenate(parts, axis=0).T.astype(
+                jnp.bfloat16
+            )
         given = []
         for r in range(RIV):
             pieces = []
@@ -238,24 +254,31 @@
     def multiply(side, packed, given):
         columns, found = columnses[side], founds[side]
         for start, rows in BLOCKS:
-            own = [
-                jnp.broadcast_to(columns[start : start + rows, 4 + r : 5 + r], (rows, 128))
-                for r in range(RIV)
-            ]
-            most = keep[start : start + rows, :]
-            least = -most
-            for r in range(RIV):
-                gap = jnp.concatenate(
-                    [own[r] - packed[1][k][4 + r : 5 + r, :] for k in range(CP // 128)], axis=1
-                ).astype(jnp.bfloat16)
-                outcome = jnp.maximum(jnp.minimum(gap, most), least)
-                gave = jnp.dot(
-                    given[r][:, start : start + rows], outcome, preferred_element_type=jnp.float32
-                )
-                if start == 0:
-                    found[r] = gave
-                else:
-                    found[r] += gave
+            band = jnp.dot(
+                columns[start : start + rows, :], selector[...], preferred_element_type=jnp.float32
+            )
+            own = [band[:, 128 * r : 128 * (r + 1)] for r in range(RIV)]
+            for other in range(0, CP, BLOCK):
+                stop = min(other + BLOCK, CP)
+                most = keep[start : start + rows, other:stop]
+                least = -most
+                for r in range(RIV):
+                    gap = jnp.concatenate(
+                        [
+                            own[r] - packed[1][k][4 + r : 5 + r, :]
+                            for k in range(other // 128, stop // 128)
+                        ],
+                        axis=1,
+                    ).astype(jnp.bfloat16)
+                    outcome = jnp.maximum(jnp.minimum(gap, most), least)
+                    gave = jnp.dot(
+                        given[r][:, start : start + rows], outcome,
+                        preferred_element_type=jnp.float32,
+                    )
+                    if start == 0:
+                        found[r, :, other:stop] = gave
+                    else:
+                        found[r, :, other:stop] += gave
 
     def finish(slot, side, live):
         lane, alive, found = lanes[side], alives[side], founds[side]
@@ -366,13 +389,14 @@
             *[pltpu.VMEM((2, 8, HP), jnp.float32)] * 2,
             *[pltpu.VMEM((2, 16, 128), jnp.int32)] * 2,
             *[pltpu.VMEM((RIV, 16, 128), jnp.float32)] * 2,
-            *[pltpu.VMEM((CP, 8), jnp.float32)] * 2,
+            *[pltpu.VMEM((CP, 128), jnp.bfloat16)] * 2,
             *[pltpu.VMEM((RIV, 16, CP), jnp.float32)] * 2,
             *[pltpu.VMEM((8, HP), jnp.float32)] * 2,
             *[pltpu.VMEM((8, H), jnp.float32)] * 2,
             pltpu.VMEM((8, HP), jnp.float32),
             pltpu.VMEM((8, H), jnp.float32),
             pltpu.VMEM((A, A, H), jnp.float32),
+            pltpu.VMEM((128, 128 * RIV), jnp.bfloat16),
             pltpu.SemaphoreType.DMA((4,)),
             pltpu.SemaphoreType.DMA((len(BLOCKS),)),
             pltpu.SemaphoreType.DMA((TS, A)),

time: 82.9 us -> 92.4 us (1.11)
  Pallas kernels: 47.5 us -> 57.1 us
    pallas_call x1, Pallas kernels: 47.5 us -> 57.1 us  [on_device(): pl.pallas_call(kernel, out_shape=(jax.ShapeDtypeStruct(turn_regret.shape,...]
where the time goes in v7:
time: 92.4 us; the launch traced here: 92.1 us
  Pallas kernels  57.1 us (62%)
  starting transfers between devices  21.1 us (23%)
  waiting for transfers between devices  10.5 us (11%)
  other arithmetic  2.12 us (2%)
    pallas_call x1, Pallas kernels, on_device(): pl.pallas_call(kernel, out_shape=(jax.ShapeDtypeStruct(turn_regret.shape,...  57.1 us
    all_to_all x2, starting transfers between devices, group_sum(): lax.all_to_all(copies, axis, 0, 0, axis_index_groups=groups, tiled=True)  15.5 us
    all_to_all x2, waiting for transfers between devices, group_sum(): lax.all_to_all(copies, axis, 0, 0, axis_index_groups=groups, tiled=True)  9.62 us
    ppermute x3, starting transfers between devices, on_device(): lax.ppermute(sums, 'turn', [(n, n ^ flip) for n in range(4)])  3.34 us
    ppermute x1, starting transfers between devices, flip_sum(): return x + lax.ppermute(x, axis, [(n, n ^ flip) for n in range(size)])  2.21 us
  transfers between devices with their start and end apart: 6, of which 3 were waited for; matrix products, arithmetic and copies ran while one was open for 2% of the time, Pallas kernels for 0%

profile of v7, /device:TPU:1, one launch (start us, length us, event | category | flops | bytes accessed | tf_op | source)
XLA Modules:
  0.0 92.1 jit_solution(8372654130240128047)
XLA Ops:
  0.6 0.0 copy-start
  0.6 57.1 %subtrees.1 = (f32[1,24,4,4,1326]{4,3,2,1,0:T(4,128)}, f32[4,1326]{1,0:T(4,128)}, f32[16,2,1326]{2,1,0:T(2,128)}, f32[4,1326]{1,0:T(4,128)}) custom-call(s32[1,3]{1,0:T(1,128)} %flop_cards.1, s32[1,4]{1,0:T(1,128)} %live_turns.1, s32[1,24]{1,0:T(1,128)} %turn_card.1, s32[1,2,24]{2,1,0:T(2,128)} %bitcast.11, f32[2,1326]{1,0:T(2,128)} %ranges_in.1, ...), custom_call_target="tpu_custom_call" | custom-call | tf_op jit(solution)/shard_map/subtrees/pallas_call | solution.py:372
  57.8 7.3 %all-to-all-start = ((f32[16,2,1326]{2,1,0:T(2,128)}), f32[16,2,1326]{2,1,0:T(2,128)S(1)}, u32[]{:S(2)}, u32[]{:S(2)}) async-start(f32[16,2,1326]{2,1,0:T(2,128)} %get-tuple-element.12), calls=%async_computation | async-start | bytes 360448 | tf_op jit(solution)/shard_map/all_to_all | solution.py:356
  65.1 2.6 %collective-permute-start.3 = (f32[4,1326]{1,0:T(4,128)}, f32[4,1326]{1,0:T(4,128)S(1)}, u32[]{:S(2)}, u32[]{:S(2)}) collective-permute-start(f32[4,1326]{1,0:T(4,128)} %get-tuple-element.11), channel_id=1, source_target_pairs={{0,3},{1,2},{2,1},{3,0},{4,7},{5,6},{6,5},{7,4},{8,11},{9,10},{10,... | collective-permute-start | bytes 63656 | tf_op jit(solution)/shard_map/ppermute | solution.py:412
  67.7 0.6 collective-permute-start.2
  68.3 0.2 collective-permute-start.1
  68.5 3.7 %all-to-all-done = f32[16,2,1326]{2,1,0:T(2,128)S(1)} async-done(((f32[16,2,1326]{2,1,0:T(2,128)}), f32[16,2,1326]{2,1,0:T(2,128)S(1)}, u32[]{:S(2)}, u32[]{:S(2)}) %all-to-all-start) | async-done | bytes 169760 | tf_op jit(solution)/shard_map/all_to_all | solution.py:356
  72.1 0.1 reduce_sum.27
  72.2 2.2 %collective-permute-start = (f32[2,1326]{1,0:T(2,128)S(1)}, f32[2,1326]{1,0:T(2,128)S(1)}, u32[]{:S(2)}, u32[]{:S(2)}) collective-permute-start(f32[2,1326]{1,0:T(2,128)S(1)} %reduce_sum.27), channel_id=1, source_target_pairs={{0,4},{4,0},{8,12},{12,8},{16,20},{20,16},{24,28},{28,24},{32,36},... | collective-permute-start | bytes 31832 | tf_op jit(solution)/shard_map/ppermute | solution.py:362
  74.4 0.8 collective-permute-done
  75.2 0.0 collective-permute-done.3
  75.2 0.0 collective-permute-done.2
  75.2 0.0 collective-permute-done.1
  75.2 0.7 broadcast_in_dim.8
  75.9 8.2 %all-to-all-start.1 = ((f32[8,2,1326]{2,1,0:T(2,128)}), f32[8,2,1326]{2,1,0:T(2,128)S(1)}, u32[]{:S(2)}, u32[]{:S(2)}) async-start(f32[8,2,1326]{2,1,0:T(2,128)} %broadcast_in_dim.8), calls=%async_computation.1 | async-start | bytes 180224 | tf_op jit(solution)/shard_map/all_to_all | solution.py:356
  84.1 0.8 multiply_reduce_fusion
  84.9 0.0 copy-done
  84.9 0.6 fusion.2
  85.5 6.0 %all-to-all-done.1 = f32[8,2,1326]{2,1,0:T(2,128)S(1)} async-done(((f32[8,2,1326]{2,1,0:T(2,128)}), f32[8,2,1326]{2,1,0:T(2,128)S(1)}, u32[]{:S(2)}, u32[]{:S(2)}) %all-to-all-start.1) | async-done | bytes 84896 | tf_op jit(solution)/shard_map/all_to_all | solution.py:356
  91.5 0.6 reduce_sum.29
  (1 shorter events, 0.0 us)
Async XLA Ops:
  0.6 84.2 %copy-start = (f32[1,4,1326]{2,1,0:T(4,128)S(1)}, f32[1,4,1326]{2,1,0:T(4,128)}, u32[]{:S(2)}) copy-start(f32[1,4,1326]{2,1,0:T(4,128)} %flop_regret_in.1) | copy-start | bytes 63652
  57.8 14.3 %all-to-all-start = ((f32[16,2,1326]{2,1,0:T(2,128)}), f32[16,2,1326]{2,1,0:T(2,128)S(1)}, u32[]{:S(2)}, u32[]{:S(2)}) async-start(f32[16,2,1326]{2,1,0:T(2,128)} %get-tuple-element.12), calls=%async_computation | async-start | bytes 360448 | tf_op jit(solution)/shard_map/all_to_all | solution.py:356
  65.1 10.1 %collective-permute-start.3 = (f32[4,1326]{1,0:T(4,128)}, f32[4,1326]{1,0:T(4,128)S(1)}, u32[]{:S(2)}, u32[]{:S(2)}) collective-permute-start(f32[4,1326]{1,0:T(4,128)} %get-tuple-element.11), channel_id=1, source_target_pairs={{0,3},{1,2},{2,1},{3,0},{4,7},{5,6},{6,5},{7,4},{8,11},{9,10},{10,... | collective-permute-start | bytes 63656 | tf_op jit(solution)/shard_map/ppermute | solution.py:412
  67.7 7.5 %collective-permute-start.2 = (f32[4,1326]{1,0:T(4,128)}, f32[4,1326]{1,0:T(4,128)S(1)}, u32[]{:S(2)}, u32[]{:S(2)}) collective-permute-start(f32[4,1326]{1,0:T(4,128)} %get-tuple-element.11), channel_id=1, source_target_pairs={{0,2},{1,3},{2,0},{3,1},{4,6},{5,7},{6,4},{7,5},{8,10},{9,11},{10,... | collective-permute-start | bytes 63656 | tf_op jit(solution)/shard_map/ppermute | solution.py:412
  68.3 7.0 %collective-permute-start.1 = (f32[4,1326]{1,0:T(4,128)}, f32[4,1326]{1,0:T(4,128)S(1)}, u32[]{:S(2)}, u32[]{:S(2)}) collective-permute-start(f32[4,1326]{1,0:T(4,128)} %get-tuple-element.11), channel_id=1, source_target_pairs={{0,1},{1,0},{2,3},{3,2},{4,5},{5,4},{6,7},{7,6},{8,9},{9,8},{10,11... | collective-permute-start | bytes 63656 | tf_op jit(solution)/shard_map/ppermute | solution.py:412
  72.2 3.0 %collective-permute-start = (f32[2,1326]{1,0:T(2,128)S(1)}, f32[2,1326]{1,0:T(2,128)S(1)}, u32[]{:S(2)}, u32[]{:S(2)}) collective-permute-start(f32[2,1326]{1,0:T(2,128)S(1)} %reduce_sum.27), channel_id=1, source_target_pairs={{0,4},{4,0},{8,12},{12,8},{16,20},{20,16},{24,28},{28,24},{32,36},... | collective-permute-start | bytes 31832 | tf_op jit(solution)/shard_map/ppermute | solution.py:362
  75.9 15.6 %all-to-all-start.1 = ((f32[8,2,1326]{2,1,0:T(2,128)}), f32[8,2,1326]{2,1,0:T(2,128)S(1)}, u32[]{:S(2)}, u32[]{:S(2)}) async-start(f32[8,2,1326]{2,1,0:T(2,128)} %broadcast_in_dim.8), calls=%async_computation.1 | async-start | bytes 180224 | tf_op jit(solution)/shard_map/all_to_all | solution.py:356

commit v8 on v7

--- a/solution.py
+++ b/solution.py
@@ -57,7 +57,7 @@
 
 
 def swap_halves(x):
-    return jnp.concatenate([x[4:8], x[0:4]], axis=0)
+    return pltpu.roll(x, 4, 0)
 
 
 def rounded(x):
@@ -70,12 +70,12 @@
     new_turn, sums, copies, root,
     ranges, flop_regret, strength, index, keep,
     regrets, wide_a, wide_b, lane_a, lane_b, alive_a, alive_b, columns_a, columns_b,
-    found_a, found_b, back_a, back_b, spread_a, spread_b, total, one_total, blank, selector,
+    found_a, found_b, back_a, back_b, spread_a, spread_b, force_a, force_b, given_a, given_b, total, one_total, blank,
     small_sems, keep_sems, in_sems, out_sems,
 ):
     wides, lanes, alives = (wide_a, wide_b), (lane_a, lane_b), (alive_a, alive_b)
     columnses, founds, backs = (columns_a, columns_b), (found_a, found_b), (back_a, back_b)
-    spreads = (spread_a, spread_b)
+    spreads, forces, givens = (spread_a, spread_b), (force_a, force_b), (given_a, given_b)
     me = lax.axis_index("turn")
     count = live_turns[0, me]
     pairs = (count + 1) // 2
@@ -137,13 +137,6 @@
         return carry
 
     lax.fori_loop(used, TS, clear, 0)
-    part = lax.broadcasted_iota(jnp.int32, (128, 128 * RIV), 0)
-    side_of = lax.broadcasted_iota(jnp.int32, (128, 128 * RIV), 1) >> 7
-    selector[...] = jnp.where((part < 3 * RIV) & ((part & 1) == side_of), 1.0, 0.0).astype(
-        jnp.bfloat16
-    )
-    for ref in columnses:
-        ref[...] = jnp.zeros_like(ref)
     for ref in wides + backs:
         ref[...] = jnp.zeros_like(ref)
     total[...] = jnp.zeros_like(total)
@@ -173,6 +166,7 @@
 
     def prepare(slot, side):
         wide, lane, alive, columns, spread = wides[side], lanes[side], alives[side], columnses[side], spreads[side]
+        force, given = forces[side], givens[side]
         for b in range(A):
             regret_copy(slot, b).wait()
         first, second = regrets[slot, 0], regrets[slot, 1]
@@ -229,35 +223,24 @@
                 packed[group].append(
                     jnp.where(offset < 128, parts[0], jnp.where(offset < 256, parts[1], parts[2]))
                 )
+        columns[...] = jnp.concatenate(packed[1], axis=1).T
         for k in range(CP // 128):
-            force = packed[1][k][4 : 4 + RIV, :]
-            parts = []
-            for _ in range(3):
-                parts.append(rounded(force))
-                force = force - parts[-1]
-            parts.append(jnp.zeros((8 - 3 * RIV, 128), jnp.float32))
-            columns[128 * k : 128 * (k + 1), 0:8] = jnp.concatenate(parts, axis=0).T.astype(
-                jnp.bfloat16
-            )
-        given = []
-        for r in range(RIV):
-            pieces = []
-            for k in range(CP // 128):
+            force[:, 128 * k : 128 * (k + 1)] = packed[1][k]
+            zeros = jnp.where(upper, packed[1][k], swap_halves(packed[1][k]))
+            for r in range(RIV):
                 mask = -alive[r, k : k + 1, :]
-                zeros = jnp.where(upper, packed[1][k], swap_halves(packed[1][k]))
-                pieces.append(
-                    jnp.concatenate([packed[0][k] * mask, zeros * mask], axis=0).astype(jnp.bfloat16)
-                )
-            given.append(jnp.concatenate(pieces, axis=1))
-        return packed, given
-
-    def multiply(side, packed, given):
+                given[r, :, 128 * k : 128 * (k + 1)] = jnp.concatenate(
+                    [packed[0][k] * mask, zeros * mask], axis=0
+                ).astype(jnp.bfloat16)
+
+    def multiply(side):
         columns, found = columnses[side], founds[side]
+        force, given = forces[side], givens[side]
         for start, rows in BLOCKS:
-            band = jnp.dot(
-                columns[start : start + rows, :], selector[...], preferred_element_type=jnp.float32
-            )
-            own = [band[:, 128 * r : 128 * (r + 1)] for r in range(RIV)]
+            own = [
+                jnp.broadcast_to(columns[start : start + rows, 4 + r : 5 + r], (rows, 128))
+                for r in range(RIV)
+            ]
             for other in range(0, CP, BLOCK):
                 stop = min(other + BLOCK, CP)
                 most = keep[start : start + rows, other:stop]
@@ -265,14 +248,14 @@
                 for r in range(RIV):
                     gap = jnp.concatenate(
                         [
-                            own[r] - packed[1][k][4 + r : 5 + r, :]
+                            own[r] - force[4 + r : 5 + r, 128 * k : 128 * (k + 1)]
                             for k in range(other // 128, stop // 128)
                         ],
                         axis=1,
                     ).astype(jnp.bfloat16)
                     outcome = jnp.maximum(jnp.minimum(gap, most), least)
                     gave = jnp.dot(
-                        given[r][:, start : start + rows], outcome,
+                        given[r, :, start : start + rows], outcome,
                         preferred_element_type=jnp.float32,
                     )
                     if start == 0:
@@ -316,9 +299,10 @@
     def pair_step(pair, carry):
         slots = (2 * pair, 2 * pair + 1)
         live = (None, (slots[1] < count).astype(jnp.float32))
-        ready = [prepare(slots[side], side) for side in range(2)]
         for side in range(2):
-            multiply(side, *ready[side])
+            prepare(slots[side], side)
+        for side in range(2):
+            multiply(side)
             finish(slots[side], side, live[side])
         return carry
 
@@ -389,14 +373,15 @@
             *[pltpu.VMEM((2, 8, HP), jnp.float32)] * 2,
             *[pltpu.VMEM((2, 16, 128), jnp.int32)] * 2,
             *[pltpu.VMEM((RIV, 16, 128), jnp.float32)] * 2,
-            *[pltpu.VMEM((CP, 128), jnp.bfloat16)] * 2,
+            *[pltpu.VMEM((CP, 8), jnp.float32)] * 2,
             *[pltpu.VMEM((RIV, 16, CP), jnp.float32)] * 2,
             *[pltpu.VMEM((8, HP), jnp.float32)] * 2,
             *[pltpu.VMEM((8, H), jnp.float32)] * 2,
+            *[pltpu.VMEM((8, CP), jnp.float32)] * 2,
+            *[pltpu.VMEM((RIV, 16, CP), jnp.bfloat16)] * 2,
             pltpu.VMEM((8, HP), jnp.float32),
             pltpu.VMEM((8, H), jnp.float32),
             pltpu.VMEM((A, A, H), jnp.float32),
-            pltpu.VMEM((128, 128 * RIV), jnp.bfloat16),
             pltpu.SemaphoreType.DMA((4,)),
             pltpu.SemaphoreType.DMA((len(BLOCKS),)),
             pltpu.SemaphoreType.DMA((TS, A)),

time: 92.4 us -> 84.8 us (0.918)
  Pallas kernels: 57.1 us -> 20.8 us
  starting transfers between devices: 21.1 us -> 49.8 us
    pallas_call x1, Pallas kernels: 57.1 us -> 20.8 us  [on_device(): pl.pallas_call(kernel, out_shape=(jax.ShapeDtypeStruct(turn_regret.shape,...]
    all_to_all x2, starting transfers between devices: 15.5 us -> 44.2 us  [group_sum(): lax.all_to_all(copies, axis, 0, 0, axis_index_groups=groups, tiled=True)]
where the time goes in v8:
time: 84.8 us; the launch traced here: 84.6 us
  starting transfers between devices  49.8 us (59%)
  Pallas kernels  20.8 us (25%)
  waiting for transfers between devices  10.4 us (12%)
  other arithmetic  2.12 us (2%)
    all_to_all x2, starting transfers between devices, group_sum(): lax.all_to_all(copies, axis, 0, 0, axis_index_groups=groups, tiled=True)  44.2 us
    pallas_call x1, Pallas kernels, on_device(): pl.pallas_call(kernel, out_shape=(jax.ShapeDtypeStruct(turn_regret.shape,...  20.8 us
    all_to_all x2, waiting for transfers between devices, group_sum(): lax.all_to_all(copies, axis, 0, 0, axis_index_groups=groups, tiled=True)  9.6 us
    ppermute x3, starting transfers between devices, on_device(): lax.ppermute(sums, 'turn', [(n, n ^ flip) for n in range(4)])  3.34 us
    ppermute x1, starting transfers between devices, flip_sum(): return x + lax.ppermute(x, axis, [(n, n ^ flip) for n in range(size)])  2.32 us
  transfers between devices with their start and end apart: 6, of which 3 were waited for; matrix products, arithmetic and copies ran while one was open for 2% of the time, Pallas kernels for 0%

profile of v8, /device:TPU:1, one launch (start us, length us, event | category | flops | bytes accessed | tf_op | source)
XLA Modules:
  0.0 84.6 jit_solution(3807492857161407903)
XLA Ops:
  0.6 0.0 copy-start
  0.6 20.8 %subtrees.1 = (f32[1,24,4,4,1326]{4,3,2,1,0:T(4,128)}, f32[4,1326]{1,0:T(4,128)}, f32[16,2,1326]{2,1,0:T(2,128)}, f32[4,1326]{1,0:T(4,128)}) custom-call(s32[1,3]{1,0:T(1,128)} %flop_cards.1, s32[1,4]{1,0:T(1,128)} %live_turns.1, s32[1,24]{1,0:T(1,128)} %turn_card.1, s32[1,2,24]{2,1,0:T(2,128)} %bitcast.11, f32[2,1326]{1,0:T(2,128)} %ranges_in.1, ...), custom_call_target="tpu_custom_call" | custom-call | tf_op jit(solution)/shard_map/subtrees/pallas_call | solution.py:356
  21.5 36.0 %all-to-all-start = ((f32[16,2,1326]{2,1,0:T(2,128)}), f32[16,2,1326]{2,1,0:T(2,128)S(1)}, u32[]{:S(2)}, u32[]{:S(2)}) async-start(f32[16,2,1326]{2,1,0:T(2,128)} %get-tuple-element.12), calls=%async_computation | async-start | bytes 360448 | tf_op jit(solution)/shard_map/all_to_all | solution.py:340
  57.5 2.6 %collective-permute-start.3 = (f32[4,1326]{1,0:T(4,128)}, f32[4,1326]{1,0:T(4,128)S(1)}, u32[]{:S(2)}, u32[]{:S(2)}) collective-permute-start(f32[4,1326]{1,0:T(4,128)} %get-tuple-element.11), channel_id=1, source_target_pairs={{0,3},{1,2},{2,1},{3,0},{4,7},{5,6},{6,5},{7,4},{8,11},{9,10},{10,... | collective-permute-start | bytes 63656 | tf_op jit(solution)/shard_map/ppermute | solution.py:397
  60.1 0.6 collective-permute-start.2
  60.6 0.2 collective-permute-start.1
  60.8 3.6 %all-to-all-done = f32[16,2,1326]{2,1,0:T(2,128)S(1)} async-done(((f32[16,2,1326]{2,1,0:T(2,128)}), f32[16,2,1326]{2,1,0:T(2,128)S(1)}, u32[]{:S(2)}, u32[]{:S(2)}) %all-to-all-start) | async-done | bytes 169760 | tf_op jit(solution)/shard_map/all_to_all | solution.py:340
  64.5 0.1 reduce_sum.27
  64.5 2.3 %collective-permute-start = (f32[2,1326]{1,0:T(2,128)S(1)}, f32[2,1326]{1,0:T(2,128)S(1)}, u32[]{:S(2)}, u32[]{:S(2)}) collective-permute-start(f32[2,1326]{1,0:T(2,128)S(1)} %reduce_sum.27), channel_id=1, source_target_pairs={{0,4},{4,0},{8,12},{12,8},{16,20},{20,16},{24,28},{28,24},{32,36},... | collective-permute-start | bytes 31832 | tf_op jit(solution)/shard_map/ppermute | solution.py:346
  66.8 0.8 collective-permute-done
  67.7 0.0 collective-permute-done.3
  67.7 0.0 collective-permute-done.2
  67.7 0.0 collective-permute-done.1
  67.7 0.7 broadcast_in_dim.8
  68.4 8.2 %all-to-all-start.1 = ((f32[8,2,1326]{2,1,0:T(2,128)}), f32[8,2,1326]{2,1,0:T(2,128)S(1)}, u32[]{:S(2)}, u32[]{:S(2)}) async-start(f32[8,2,1326]{2,1,0:T(2,128)} %broadcast_in_dim.8), calls=%async_computation.1 | async-start | bytes 180224 | tf_op jit(solution)/shard_map/all_to_all | solution.py:340
  76.5 0.8 multiply_reduce_fusion
  77.3 0.0 copy-done
  77.3 0.6 fusion.2
  78.0 6.0 %all-to-all-done.1 = f32[8,2,1326]{2,1,0:T(2,128)S(1)} async-done(((f32[8,2,1326]{2,1,0:T(2,128)}), f32[8,2,1326]{2,1,0:T(2,128)S(1)}, u32[]{:S(2)}, u32[]{:S(2)}) %all-to-all-start.1) | async-done | bytes 84896 | tf_op jit(solution)/shard_map/all_to_all | solution.py:340
  83.9 0.6 reduce_sum.29
  (1 shorter events, 0.0 us)
Async XLA Ops:
  0.6 76.7 %copy-start = (f32[1,4,1326]{2,1,0:T(4,128)S(1)}, f32[1,4,1326]{2,1,0:T(4,128)}, u32[]{:S(2)}) copy-start(f32[1,4,1326]{2,1,0:T(4,128)} %flop_regret_in.1) | copy-start | bytes 63652
  21.5 43.0 %all-to-all-start = ((f32[16,2,1326]{2,1,0:T(2,128)}), f32[16,2,1326]{2,1,0:T(2,128)S(1)}, u32[]{:S(2)}, u32[]{:S(2)}) async-start(f32[16,2,1326]{2,1,0:T(2,128)} %get-tuple-element.12), calls=%async_computation | async-start | bytes 360448 | tf_op jit(solution)/shard_map/all_to_all | solution.py:340
  57.5 10.2 %collective-permute-start.3 = (f32[4,1326]{1,0:T(4,128)}, f32[4,1326]{1,0:T(4,128)S(1)}, u32[]{:S(2)}, u32[]{:S(2)}) collective-permute-start(f32[4,1326]{1,0:T(4,128)} %get-tuple-element.11), channel_id=1, source_target_pairs={{0,3},{1,2},{2,1},{3,0},{4,7},{5,6},{6,5},{7,4},{8,11},{9,10},{10,... | collective-permute-start | bytes 63656 | tf_op jit(solution)/shard_map/ppermute | solution.py:397
  60.1 7.6 %collective-permute-start.2 = (f32[4,1326]{1,0:T(4,128)}, f32[4,1326]{1,0:T(4,128)S(1)}, u32[]{:S(2)}, u32[]{:S(2)}) collective-permute-start(f32[4,1326]{1,0:T(4,128)} %get-tuple-element.11), channel_id=1, source_target_pairs={{0,2},{1,3},{2,0},{3,1},{4,6},{5,7},{6,4},{7,5},{8,10},{9,11},{10,... | collective-permute-start | bytes 63656 | tf_op jit(solution)/shard_map/ppermute | solution.py:397
  60.6 7.1 %collective-permute-start.1 = (f32[4,1326]{1,0:T(4,128)}, f32[4,1326]{1,0:T(4,128)S(1)}, u32[]{:S(2)}, u32[]{:S(2)}) collective-permute-start(f32[4,1326]{1,0:T(4,128)} %get-tuple-element.11), channel_id=1, source_target_pairs={{0,1},{1,0},{2,3},{3,2},{4,5},{5,4},{6,7},{7,6},{8,9},{9,8},{10,11... | collective-permute-start | bytes 63656 | tf_op jit(solution)/shard_map/ppermute | solution.py:397
  64.5 3.1 %collective-permute-start = (f32[2,1326]{1,0:T(2,128)S(1)}, f32[2,1326]{1,0:T(2,128)S(1)}, u32[]{:S(2)}, u32[]{:S(2)}) collective-permute-start(f32[2,1326]{1,0:T(2,128)S(1)} %reduce_sum.27), channel_id=1, source_target_pairs={{0,4},{4,0},{8,12},{12,8},{16,20},{20,16},{24,28},{28,24},{32,36},... | collective-permute-start | bytes 31832 | tf_op jit(solution)/shard_map/ppermute | solution.py:346
  68.4 15.6 %all-to-all-start.1 = ((f32[8,2,1326]{2,1,0:T(2,128)}), f32[8,2,1326]{2,1,0:T(2,128)S(1)}, u32[]{:S(2)}, u32[]{:S(2)}) async-start(f32[8,2,1326]{2,1,0:T(2,128)} %broadcast_in_dim.8), calls=%async_computation.1 | async-start | bytes 180224 | tf_op jit(solution)/shard_map/all_to_all | solution.py:340

commit v9 on v7

--- a/solution.py
+++ b/solution.py
@@ -19,6 +19,7 @@
 FLOPS = 64
 NEAR = 16
 BLOCK = 256
+ROWS = 128
 BIG = 2.0**126
 
 bet_sizes = (0.25, 0.5, 1.0, 2.0)
@@ -53,7 +54,7 @@
     return index, disjoint.astype(jnp.bfloat16)
 
 
-BLOCKS = [(start, min(BLOCK, 1136 - start)) for start in range(0, CP, BLOCK)]
+BLOCKS = [(start, min(ROWS, 1136 - start)) for start in range(0, CP, ROWS)]
 
 
 def swap_halves(x):
@@ -70,7 +71,7 @@
     new_turn, sums, copies, root,
     ranges, flop_regret, strength, index, keep,
     regrets, wide_a, wide_b, lane_a, lane_b, alive_a, alive_b, columns_a, columns_b,
-    found_a, found_b, back_a, back_b, spread_a, spread_b, total, one_total, blank, selector,
+    found_a, found_b, back_a, back_b, spread_a, spread_b, total, one_total, blank,
     small_sems, keep_sems, in_sems, out_sems,
 ):
     wides, lanes, alives = (wide_a, wide_b), (lane_a, lane_b), (alive_a, alive_b)
@@ -111,8 +112,8 @@
     ]
     masks = [
         pltpu.make_async_copy(
-            keep_in.at[pl.ds(start, BLOCK if start + BLOCK <= CP else 128)],
-            keep.at[pl.ds(start, BLOCK if start + BLOCK <= CP else 128)],
+            keep_in.at[pl.ds(start, ROWS)],
+            keep.at[pl.ds(start, ROWS)],
             keep_sems.at[n],
         )
         for n, (start, rows) in enumerate(BLOCKS)
@@ -137,13 +138,6 @@
         return carry
 
     lax.fori_loop(used, TS, clear, 0)
-    part = lax.broadcasted_iota(jnp.int32, (128, 128 * RIV), 0)
-    side_of = lax.broadcasted_iota(jnp.int32, (128, 128 * RIV), 1) >> 7
-    selector[...] = jnp.where((part < 3 * RIV) & ((part & 1) == side_of), 1.0, 0.0).astype(
-        jnp.bfloat16
-    )
-    for ref in columnses:
-        ref[...] = jnp.zeros_like(ref)
     for ref in wides + backs:
         ref[...] = jnp.zeros_like(ref)
     total[...] = jnp.zeros_like(total)
@@ -229,16 +223,7 @@
                 packed[group].append(
                     jnp.where(offset < 128, parts[0], jnp.where(offset < 256, parts[1], parts[2]))
                 )
-        for k in range(CP // 128):
-            force = packed[1][k][4 : 4 + RIV, :]
-            parts = []
-            for _ in range(3):
-                parts.append(rounded(force))
-                force = force - parts[-1]
-            parts.append(jnp.zeros((8 - 3 * RIV, 128), jnp.float32))
-            columns[128 * k : 128 * (k + 1), 0:8] = jnp.concatenate(parts, axis=0).T.astype(
-                jnp.bfloat16
-            )
+        columns[...] = jnp.concatenate(packed[1], axis=1).T
         given = []
         for r in range(RIV):
             pieces = []
@@ -254,10 +239,10 @@
     def multiply(side, packed, given):
         columns, found = columnses[side], founds[side]
         for start, rows in BLOCKS:
-            band = jnp.dot(
-                columns[start : start + rows, :], selector[...], preferred_element_type=jnp.float32
-            )
-            own = [band[:, 128 * r : 128 * (r + 1)] for r in range(RIV)]
+            own = [
+                jnp.broadcast_to(columns[start : start + rows, 4 + r : 5 + r], (rows, 128))
+                for r in range(RIV)
+            ]
             for other in range(0, CP, BLOCK):
                 stop = min(other + BLOCK, CP)
                 most = keep[start : start + rows, other:stop]
@@ -389,14 +374,13 @@
             *[pltpu.VMEM((2, 8, HP), jnp.float32)] * 2,
             *[pltpu.VMEM((2, 16, 128), jnp.int32)] * 2,
             *[pltpu.VMEM((RIV, 16, 128), jnp.float32)] * 2,
-            *[pltpu.VMEM((CP, 128), jnp.bfloat16)] * 2,
+            *[pltpu.VMEM((CP, 8), jnp.float32)] * 2,
             *[pltpu.VMEM((RIV, 16, CP), jnp.float32)] * 2,
             *[pltpu.VMEM((8, HP), jnp.float32)] * 2,
             *[pltpu.VMEM((8, H), jnp.float32)] * 2,
             pltpu.VMEM((8, HP), jnp.float32),
             pltpu.VMEM((8, H), jnp.float32),
             pltpu.VMEM((A, A, H), jnp.float32),
-            pltpu.VMEM((128, 128 * RIV), jnp.bfloat16),
             pltpu.SemaphoreType.DMA((4,)),
             pltpu.SemaphoreType.DMA((len(BLOCKS),)),
             pltpu.SemaphoreType.DMA((TS, A)),

time: 92.4 us -> 81.3 us (0.88)
  Pallas kernels: 57.1 us -> 45.9 us
    pallas_call x1, Pallas kernels: 57.1 us -> 45.9 us  [on_device(): pl.pallas_call(kernel, out_shape=(jax.ShapeDtypeStruct(turn_regret.shape,...]
where the time goes in v9:
time: 81.3 us; the launch traced here: 80.8 us
  Pallas kernels  45.9 us (56%)
  starting transfers between devices  21.1 us (26%)
  waiting for transfers between devices  10.5 us (13%)
  other arithmetic  2.12 us (3%)
    pallas_call x1, Pallas kernels, on_device(): pl.pallas_call(kernel, out_shape=(jax.ShapeDtypeStruct(turn_regret.shape,...  45.9 us
    all_to_all x2, starting transfers between devices, group_sum(): lax.all_to_all(copies, axis, 0, 0, axis_index_groups=groups, tiled=True)  15.5 us
    all_to_all x2, waiting for transfers between devices, group_sum(): lax.all_to_all(copies, axis, 0, 0, axis_index_groups=groups, tiled=True)  9.62 us
    ppermute x3, starting transfers between devices, on_device(): lax.ppermute(sums, 'turn', [(n, n ^ flip) for n in range(4)])  3.34 us
    ppermute x1, starting transfers between devices, flip_sum(): return x + lax.ppermute(x, axis, [(n, n ^ flip) for n in range(size)])  2.2 us
  transfers between devices with their start and end apart: 6, of which 3 were waited for; matrix products, arithmetic and copies ran while one was open for 2% of the time, Pallas kernels for 0%

profile of v9, /device:TPU:1, one launch (start us, length us, event | category | flops | bytes accessed | tf_op | source)
XLA Modules:
  0.0 80.8 jit_solution(15862894346915606926)
XLA Ops:
  0.6 0.0 copy-start
  0.6 45.9 %subtrees.1 = (f32[1,24,4,4,1326]{4,3,2,1,0:T(4,128)}, f32[4,1326]{1,0:T(4,128)}, f32[16,2,1326]{2,1,0:T(2,128)}, f32[4,1326]{1,0:T(4,128)}) custom-call(s32[1,3]{1,0:T(1,128)} %flop_cards.1, s32[1,4]{1,0:T(1,128)} %live_turns.1, s32[1,24]{1,0:T(1,128)} %turn_card.1, s32[1,2,24]{2,1,0:T(2,128)} %bitcast.11, f32[2,1326]{1,0:T(2,128)} %ranges_in.1, ...), custom_call_target="tpu_custom_call" | custom-call | tf_op jit(solution)/shard_map/subtrees/pallas_call | solution.py:357
  46.5 7.3 %all-to-all-start = ((f32[16,2,1326]{2,1,0:T(2,128)}), f32[16,2,1326]{2,1,0:T(2,128)S(1)}, u32[]{:S(2)}, u32[]{:S(2)}) async-start(f32[16,2,1326]{2,1,0:T(2,128)} %get-tuple-element.12), calls=%async_computation | async-start | bytes 360448 | tf_op jit(solution)/shard_map/all_to_all | solution.py:341
  53.9 2.6 %collective-permute-start.3 = (f32[4,1326]{1,0:T(4,128)}, f32[4,1326]{1,0:T(4,128)S(1)}, u32[]{:S(2)}, u32[]{:S(2)}) collective-permute-start(f32[4,1326]{1,0:T(4,128)} %get-tuple-element.11), channel_id=1, source_target_pairs={{0,3},{1,2},{2,1},{3,0},{4,7},{5,6},{6,5},{7,4},{8,11},{9,10},{10,... | collective-permute-start | bytes 63656 | tf_op jit(solution)/shard_map/ppermute | solution.py:396
  56.4 0.6 collective-permute-start.2
  57.0 0.2 collective-permute-start.1
  57.2 3.7 %all-to-all-done = f32[16,2,1326]{2,1,0:T(2,128)S(1)} async-done(((f32[16,2,1326]{2,1,0:T(2,128)}), f32[16,2,1326]{2,1,0:T(2,128)S(1)}, u32[]{:S(2)}, u32[]{:S(2)}) %all-to-all-start) | async-done | bytes 169760 | tf_op jit(solution)/shard_map/all_to_all | solution.py:341
  60.9 0.1 reduce_sum.27
  60.9 2.2 %collective-permute-start = (f32[2,1326]{1,0:T(2,128)S(1)}, f32[2,1326]{1,0:T(2,128)S(1)}, u32[]{:S(2)}, u32[]{:S(2)}) collective-permute-start(f32[2,1326]{1,0:T(2,128)S(1)} %reduce_sum.27), channel_id=1, source_target_pairs={{0,4},{4,0},{8,12},{12,8},{16,20},{20,16},{24,28},{28,24},{32,36},... | collective-permute-start | bytes 31832 | tf_op jit(solution)/shard_map/ppermute | solution.py:347
  63.1 0.8 %collective-permute-done = f32[2,1326]{1,0:T(2,128)S(1)} collective-permute-done((f32[2,1326]{1,0:T(2,128)S(1)}, f32[2,1326]{1,0:T(2,128)S(1)}, u32[]{:S(2)}, u32[]{:S(2)}) %collective-permute-start) | collective-permute-done | bytes 10640 | tf_op jit(solution)/shard_map/ppermute | solution.py:347
  64.0 0.0 collective-permute-done.3
  64.0 0.0 collective-permute-done.2
  64.0 0.0 collective-permute-done.1
  64.0 0.7 broadcast_in_dim.8
  64.6 8.2 %all-to-all-start.1 = ((f32[8,2,1326]{2,1,0:T(2,128)}), f32[8,2,1326]{2,1,0:T(2,128)S(1)}, u32[]{:S(2)}, u32[]{:S(2)}) async-start(f32[8,2,1326]{2,1,0:T(2,128)} %broadcast_in_dim.8), calls=%async_computation.1 | async-start | bytes 180224 | tf_op jit(solution)/shard_map/all_to_all | solution.py:341
  72.8 0.8 multiply_reduce_fusion
  73.6 0.0 copy-done
  73.6 0.6 fusion.2
  74.2 6.0 %all-to-all-done.1 = f32[8,2,1326]{2,1,0:T(2,128)S(1)} async-done(((f32[8,2,1326]{2,1,0:T(2,128)}), f32[8,2,1326]{2,1,0:T(2,128)S(1)}, u32[]{:S(2)}, u32[]{:S(2)}) %all-to-all-start.1) | async-done | bytes 84896 | tf_op jit(solution)/shard_map/all_to_all | solution.py:341
  80.2 0.6 reduce_sum.29
  (1 shorter events, 0.0 us)
Async XLA Ops:
  0.6 73.0 %copy-start = (f32[1,4,1326]{2,1,0:T(4,128)S(1)}, f32[1,4,1326]{2,1,0:T(4,128)}, u32[]{:S(2)}) copy-start(f32[1,4,1326]{2,1,0:T(4,128)} %flop_regret_in.1) | copy-start | bytes 63652
  46.5 14.3 %all-to-all-start = ((f32[16,2,1326]{2,1,0:T(2,128)}), f32[16,2,1326]{2,1,0:T(2,128)S(1)}, u32[]{:S(2)}, u32[]{:S(2)}) async-start(f32[16,2,1326]{2,1,0:T(2,128)} %get-tuple-element.12), calls=%async_computation | async-start | bytes 360448 | tf_op jit(solution)/shard_map/all_to_all | solution.py:341
  53.9 10.1 %collective-permute-start.3 = (f32[4,1326]{1,0:T(4,128)}, f32[4,1326]{1,0:T(4,128)S(1)}, u32[]{:S(2)}, u32[]{:S(2)}) collective-permute-start(f32[4,1326]{1,0:T(4,128)} %get-tuple-element.11), channel_id=1, source_target_pairs={{0,3},{1,2},{2,1},{3,0},{4,7},{5,6},{6,5},{7,4},{8,11},{9,10},{10,... | collective-permute-start | bytes 63656 | tf_op jit(solution)/shard_map/ppermute | solution.py:396
  56.4 7.5 %collective-permute-start.2 = (f32[4,1326]{1,0:T(4,128)}, f32[4,1326]{1,0:T(4,128)S(1)}, u32[]{:S(2)}, u32[]{:S(2)}) collective-permute-start(f32[4,1326]{1,0:T(4,128)} %get-tuple-element.11), channel_id=1, source_target_pairs={{0,2},{1,3},{2,0},{3,1},{4,6},{5,7},{6,4},{7,5},{8,10},{9,11},{10,... | collective-permute-start | bytes 63656 | tf_op jit(solution)/shard_map/ppermute | solution.py:396
  57.0 7.0 %collective-permute-start.1 = (f32[4,1326]{1,0:T(4,128)}, f32[4,1326]{1,0:T(4,128)S(1)}, u32[]{:S(2)}, u32[]{:S(2)}) collective-permute-start(f32[4,1326]{1,0:T(4,128)} %get-tuple-element.11), channel_id=1, source_target_pairs={{0,1},{1,0},{2,3},{3,2},{4,5},{5,4},{6,7},{7,6},{8,9},{9,8},{10,11... | collective-permute-start | bytes 63656 | tf_op jit(solution)/shard_map/ppermute | solution.py:396
  60.9 3.0 %collective-permute-start = (f32[2,1326]{1,0:T(2,128)S(1)}, f32[2,1326]{1,0:T(2,128)S(1)}, u32[]{:S(2)}, u32[]{:S(2)}) collective-permute-start(f32[2,1326]{1,0:T(2,128)S(1)} %reduce_sum.27), channel_id=1, source_target_pairs={{0,4},{4,0},{8,12},{12,8},{16,20},{20,16},{24,28},{28,24},{32,36},... | collective-permute-start | bytes 31832 | tf_op jit(solution)/shard_map/ppermute | solution.py:347
  64.6 15.6 %all-to-all-start.1 = ((f32[8,2,1326]{2,1,0:T(2,128)}), f32[8,2,1326]{2,1,0:T(2,128)S(1)}, u32[]{:S(2)}, u32[]{:S(2)}) async-start(f32[8,2,1326]{2,1,0:T(2,128)} %broadcast_in_dim.8), calls=%async_computation.1 | async-start | bytes 180224 | tf_op jit(solution)/shard_map/all_to_all | solution.py:341

commit v10 on v9

--- a/solution.py
+++ b/solution.py
@@ -15,6 +15,7 @@
 A = 4
 TURNS = 49
 TS = 24
+SIDES = 4
 RIV = 2
 FLOPS = 64
 NEAR = 16
@@ -70,17 +71,13 @@
     ranges_in, flop_regret_in, strength_in, turn_regret, index_in, keep_in,
     new_turn, sums, copies, root,
     ranges, flop_regret, strength, index, keep,
-    regrets, wide_a, wide_b, lane_a, lane_b, alive_a, alive_b, columns_a, columns_b,
-    found_a, found_b, back_a, back_b, spread_a, spread_b, total, one_total, blank,
+    regrets, wides, lanes, alives, columnses, founds, backs, spreads, total, one_total, blank,
     small_sems, keep_sems, in_sems, out_sems,
 ):
-    wides, lanes, alives = (wide_a, wide_b), (lane_a, lane_b), (alive_a, alive_b)
-    columnses, founds, backs = (columns_a, columns_b), (found_a, found_b), (back_a, back_b)
-    spreads = (spread_a, spread_b)
     me = lax.axis_index("turn")
     count = live_turns[0, me]
-    pairs = (count + 1) // 2
-    used = 2 * pairs
+    steps = (count + SIDES - 1) // SIDES
+    used = SIDES * steps
 
     def regret_copy(slot, b):
         return pltpu.make_async_copy(
@@ -298,16 +295,18 @@
             result_copy(slot, b).start()
 
 
-    def pair_step(pair, carry):
-        slots = (2 * pair, 2 * pair + 1)
-        live = (None, (slots[1] < count).astype(jnp.float32))
-        ready = [prepare(slots[side], side) for side in range(2)]
-        for side in range(2):
+    def group_step(group, carry):
+        slots = [SIDES * group + side for side in range(SIDES)]
+        ready = [prepare(slots[0], 0)]
+        for side in range(SIDES):
+            if side + 1 < SIDES:
+                ready.append(prepare(slots[side + 1], side + 1))
             multiply(side, *ready[side])
-            finish(slots[side], side, live[side])
+            live = (slots[side] < count).astype(jnp.float32) if side else None
+            finish(slots[side], side, live)
         return carry
 
-    lax.fori_loop(0, pairs, pair_step, 0)
+    lax.fori_loop(0, steps, group_step, 0)
     whole = total[0:4, :H]
     sums[...] = whole
     scale = 1.0 / (TURNS * FLOPS)
@@ -371,13 +370,13 @@
             pltpu.VMEM((4, 16, 128), jnp.int32),
             pltpu.VMEM((CP, CP), jnp.bfloat16),
             pltpu.VMEM((TS, 2, 8, H), jnp.float32),
-            *[pltpu.VMEM((2, 8, HP), jnp.float32)] * 2,
-            *[pltpu.VMEM((2, 16, 128), jnp.int32)] * 2,
-            *[pltpu.VMEM((RIV, 16, 128), jnp.float32)] * 2,
-            *[pltpu.VMEM((CP, 8), jnp.float32)] * 2,
-            *[pltpu.VMEM((RIV, 16, CP), jnp.float32)] * 2,
-            *[pltpu.VMEM((8, HP), jnp.float32)] * 2,
-            *[pltpu.VMEM((8, H), jnp.float32)] * 2,
+            [pltpu.VMEM((2, 8, HP), jnp.float32)] * SIDES,
+            [pltpu.VMEM((2, 16, 128), jnp.int32)] * SIDES,
+            [pltpu.VMEM((RIV, 16, 128), jnp.float32)] * SIDES,
+            [pltpu.VMEM((CP, 8), jnp.float32)] * SIDES,
+            [pltpu.VMEM((RIV, 16, CP), jnp.float32)] * SIDES,
+            [pltpu.VMEM((8, HP), jnp.float32)] * SIDES,
+            [pltpu.VMEM((8, H), jnp.float32)] * SIDES,
             pltpu.VMEM((8, HP), jnp.float32),
             pltpu.VMEM((8, H), jnp.float32),
             pltpu.VMEM((A, A, H), jnp.float32),

time: 81.3 us -> 79 us (0.972)
  Pallas kernels: 45.9 us -> 19 us
  starting transfers between devices: 21.1 us -> 45.8 us
    pallas_call x1, Pallas kernels: 45.9 us -> 19 us  [on_device(): pl.pallas_call(kernel, out_shape=(jax.ShapeDtypeStruct(turn_regret.shape,...]
    all_to_all x2, starting transfers between devices: 15.5 us -> 40.1 us  [group_sum(): lax.all_to_all(copies, axis, 0, 0, axis_index_groups=groups, tiled=True)]
where the time goes in v10:
time: 79 us; the launch traced here: 78.6 us
  starting transfers between devices  45.8 us (58%)
  Pallas kernels  19 us (24%)
  waiting for transfers between devices  10.4 us (13%)
  other arithmetic  2.12 us (3%)
    all_to_all x2, starting transfers between devices, group_sum(): lax.all_to_all(copies, axis, 0, 0, axis_index_groups=groups, tiled=True)  40.1 us
    pallas_call x1, Pallas kernels, on_device(): pl.pallas_call(kernel, out_shape=(jax.ShapeDtypeStruct(turn_regret.shape,...  19 us
    all_to_all x2, waiting for transfers between devices, group_sum(): lax.all_to_all(copies, axis, 0, 0, axis_index_groups=groups, tiled=True)  9.6 us
    ppermute x3, starting transfers between devices, on_device(): lax.ppermute(sums, 'turn', [(n, n ^ flip) for n in range(4)])  3.34 us
    ppermute x1, starting transfers between devices, flip_sum(): return x + lax.ppermute(x, axis, [(n, n ^ flip) for n in range(size)])  2.32 us
  transfers between devices with their start and end apart: 6, of which 3 were waited for; matrix products, arithmetic and copies ran while one was open for 2% of the time, Pallas kernels for 0%

profile of v10, /device:TPU:1, one launch (start us, length us, event | category | flops | bytes accessed | tf_op | source)
XLA Modules:
  0.0 78.6 jit_solution(1057628132816335977)
XLA Ops:
  0.6 0.0 copy-start
  0.6 19.0 %subtrees.1 = (f32[1,24,4,4,1326]{4,3,2,1,0:T(4,128)}, f32[4,1326]{1,0:T(4,128)}, f32[16,2,1326]{2,1,0:T(2,128)}, f32[4,1326]{1,0:T(4,128)}) custom-call(s32[1,3]{1,0:T(1,128)} %flop_cards.1, s32[1,4]{1,0:T(1,128)} %live_turns.1, s32[1,24]{1,0:T(1,128)} %turn_card.1, s32[1,2,24]{2,1,0:T(2,128)} %bitcast.11, f32[2,1326]{1,0:T(2,128)} %ranges_in.1, ...), custom_call_target="tpu_custom_call" | custom-call | tf_op jit(solution)/shard_map/subtrees/pallas_call | solution.py:356
  19.6 31.9 %all-to-all-start = ((f32[16,2,1326]{2,1,0:T(2,128)}), f32[16,2,1326]{2,1,0:T(2,128)S(1)}, u32[]{:S(2)}, u32[]{:S(2)}) async-start(f32[16,2,1326]{2,1,0:T(2,128)} %get-tuple-element.12), calls=%async_computation | async-start | bytes 360448 | tf_op jit(solution)/shard_map/all_to_all | solution.py:340
  51.5 2.6 %collective-permute-start.3 = (f32[4,1326]{1,0:T(4,128)}, f32[4,1326]{1,0:T(4,128)S(1)}, u32[]{:S(2)}, u32[]{:S(2)}) collective-permute-start(f32[4,1326]{1,0:T(4,128)} %get-tuple-element.11), channel_id=1, source_target_pairs={{0,3},{1,2},{2,1},{3,0},{4,7},{5,6},{6,5},{7,4},{8,11},{9,10},{10,... | collective-permute-start | bytes 63656 | tf_op jit(solution)/shard_map/ppermute | solution.py:395
  54.1 0.6 collective-permute-start.2
  54.7 0.2 collective-permute-start.1
  54.9 3.6 %all-to-all-done = f32[16,2,1326]{2,1,0:T(2,128)S(1)} async-done(((f32[16,2,1326]{2,1,0:T(2,128)}), f32[16,2,1326]{2,1,0:T(2,128)S(1)}, u32[]{:S(2)}, u32[]{:S(2)}) %all-to-all-start) | async-done | bytes 169760 | tf_op jit(solution)/shard_map/all_to_all | solution.py:340
  58.5 0.1 reduce_sum.27
  58.6 2.3 %collective-permute-start = (f32[2,1326]{1,0:T(2,128)S(1)}, f32[2,1326]{1,0:T(2,128)S(1)}, u32[]{:S(2)}, u32[]{:S(2)}) collective-permute-start(f32[2,1326]{1,0:T(2,128)S(1)} %reduce_sum.27), channel_id=1, source_target_pairs={{0,4},{4,0},{8,12},{12,8},{16,20},{20,16},{24,28},{28,24},{32,36},... | collective-permute-start | bytes 31832 | tf_op jit(solution)/shard_map/ppermute | solution.py:346
  60.9 0.8 %collective-permute-done = f32[2,1326]{1,0:T(2,128)S(1)} collective-permute-done((f32[2,1326]{1,0:T(2,128)S(1)}, f32[2,1326]{1,0:T(2,128)S(1)}, u32[]{:S(2)}, u32[]{:S(2)}) %collective-permute-start) | collective-permute-done | bytes 10640 | tf_op jit(solution)/shard_map/ppermute | solution.py:346
  61.7 0.0 collective-permute-done.3
  61.7 0.0 collective-permute-done.2
  61.7 0.0 collective-permute-done.1
  61.8 0.7 broadcast_in_dim.8
  62.4 8.2 %all-to-all-start.1 = ((f32[8,2,1326]{2,1,0:T(2,128)}), f32[8,2,1326]{2,1,0:T(2,128)S(1)}, u32[]{:S(2)}, u32[]{:S(2)}) async-start(f32[8,2,1326]{2,1,0:T(2,128)} %broadcast_in_dim.8), calls=%async_computation.1 | async-start | bytes 180224 | tf_op jit(solution)/shard_map/all_to_all | solution.py:340
  70.6 0.8 multiply_reduce_fusion
  71.4 0.0 copy-done
  71.4 0.6 fusion.2
  72.0 6.0 %all-to-all-done.1 = f32[8,2,1326]{2,1,0:T(2,128)S(1)} async-done(((f32[8,2,1326]{2,1,0:T(2,128)}), f32[8,2,1326]{2,1,0:T(2,128)S(1)}, u32[]{:S(2)}, u32[]{:S(2)}) %all-to-all-start.1) | async-done | bytes 84896 | tf_op jit(solution)/shard_map/all_to_all | solution.py:340
  78.0 0.6 reduce_sum.29
  (1 shorter events, 0.0 us)
Async XLA Ops:
  0.6 70.7 %copy-start = (f32[1,4,1326]{2,1,0:T(4,128)S(1)}, f32[1,4,1326]{2,1,0:T(4,128)}, u32[]{:S(2)}) copy-start(f32[1,4,1326]{2,1,0:T(4,128)} %flop_regret_in.1) | copy-start | bytes 63652
  19.6 38.9 %all-to-all-start = ((f32[16,2,1326]{2,1,0:T(2,128)}), f32[16,2,1326]{2,1,0:T(2,128)S(1)}, u32[]{:S(2)}, u32[]{:S(2)}) async-start(f32[16,2,1326]{2,1,0:T(2,128)} %get-tuple-element.12), calls=%async_computation | async-start | bytes 360448 | tf_op jit(solution)/shard_map/all_to_all | solution.py:340
  51.5 10.2 %collective-permute-start.3 = (f32[4,1326]{1,0:T(4,128)}, f32[4,1326]{1,0:T(4,128)S(1)}, u32[]{:S(2)}, u32[]{:S(2)}) collective-permute-start(f32[4,1326]{1,0:T(4,128)} %get-tuple-element.11), channel_id=1, source_target_pairs={{0,3},{1,2},{2,1},{3,0},{4,7},{5,6},{6,5},{7,4},{8,11},{9,10},{10,... | collective-permute-start | bytes 63656 | tf_op jit(solution)/shard_map/ppermute | solution.py:395
  54.1 7.6 %collective-permute-start.2 = (f32[4,1326]{1,0:T(4,128)}, f32[4,1326]{1,0:T(4,128)S(1)}, u32[]{:S(2)}, u32[]{:S(2)}) collective-permute-start(f32[4,1326]{1,0:T(4,128)} %get-tuple-element.11), channel_id=1, source_target_pairs={{0,2},{1,3},{2,0},{3,1},{4,6},{5,7},{6,4},{7,5},{8,10},{9,11},{10,... | collective-permute-start | bytes 63656 | tf_op jit(solution)/shard_map/ppermute | solution.py:395
  54.7 7.1 %collective-permute-start.1 = (f32[4,1326]{1,0:T(4,128)}, f32[4,1326]{1,0:T(4,128)S(1)}, u32[]{:S(2)}, u32[]{:S(2)}) collective-permute-start(f32[4,1326]{1,0:T(4,128)} %get-tuple-element.11), channel_id=1, source_target_pairs={{0,1},{1,0},{2,3},{3,2},{4,5},{5,4},{6,7},{7,6},{8,9},{9,8},{10,11... | collective-permute-start | bytes 63656 | tf_op jit(solution)/shard_map/ppermute | solution.py:395
  58.6 3.1 %collective-permute-start = (f32[2,1326]{1,0:T(2,128)S(1)}, f32[2,1326]{1,0:T(2,128)S(1)}, u32[]{:S(2)}, u32[]{:S(2)}) collective-permute-start(f32[2,1326]{1,0:T(2,128)S(1)} %reduce_sum.27), channel_id=1, source_target_pairs={{0,4},{4,0},{8,12},{12,8},{16,20},{20,16},{24,28},{28,24},{32,36},... | collective-permute-start | bytes 31832 | tf_op jit(solution)/shard_map/ppermute | solution.py:346
  62.4 15.6 %all-to-all-start.1 = ((f32[8,2,1326]{2,1,0:T(2,128)}), f32[8,2,1326]{2,1,0:T(2,128)S(1)}, u32[]{:S(2)}, u32[]{:S(2)}) async-start(f32[8,2,1326]{2,1,0:T(2,128)} %broadcast_in_dim.8), calls=%async_computation.1 | async-start | bytes 180224 | tf_op jit(solution)/shard_map/all_to_all | solution.py:340

commit v11 on v10

--- a/solution.py
+++ b/solution.py
@@ -81,7 +81,7 @@
 
     def regret_copy(slot, b):
         return pltpu.make_async_copy(
-            turn_regret.at[0, slot, :, b],
+            turn_regret.at[0, jnp.minimum(slot, TS - 1), :, b],
             regrets.at[slot, b // 2, pl.ds((b % 2) * 4, 4)],
             in_sems.at[slot, b],
         )
@@ -127,7 +127,7 @@
             regret_copy(slot, b).start()
         return carry
 
-    lax.fori_loop(1, used, fetch, 0)
+    lax.fori_loop(1, used + 1, fetch, 0)
     blank[...] = jnp.zeros_like(blank)
 
     def clear(slot, carry):
@@ -159,10 +159,8 @@
         for n in range(8):
             column = jnp.where(row == n, float(pot[n % 4, 2 * k + n // 4]), column)
         pots.append(column)
-    for copy in masks:
-        copy.wait()
-
     def prepare(slot, side):
+        source = jnp.minimum(slot, TS - 1)
         wide, lane, alive, columns, spread = wides[side], lanes[side], alives[side], columnses[side], spreads[side]
         for b in range(A):
             regret_copy(slot, b).wait()
@@ -179,9 +177,9 @@
         wide[0, :, :H] = jnp.where(upper, weight, weight - rounded(weight))
         spreading = sigma_first * pots[0] + sigma_second * pots[1]
         spread[...] = spreading + swap_halves(spreading)
-        wide[1, 4:6, :H] = strength[0, slot] * BIG
-
-        dead, card = [], turn_card[0, slot]
+        wide[1, 4:6, :H] = strength[0, source] * BIG
+
+        dead, card = [], turn_card[0, source]
         for flop_card in (first_card, second_card, third_card):
             dead.append(jnp.minimum(flop_card, card))
             card = jnp.maximum(flop_card, card)
@@ -192,7 +190,7 @@
             high = high + (high >= card).astype(jnp.int32)
         lane[0] = ((low * (2 * CARDS - 1 - low)) >> 1) + high - low - 1
         for r in range(RIV):
-            river = river_cards[0, r, slot]
+            river = river_cards[0, r, source]
             alive[r] = jnp.where((low == river) | (high == river), 0.0, -1.0)
         low, high = index[2], index[3]
         lost = (low == dead[0]) | (high == dead[0])
@@ -297,16 +295,19 @@
 
     def group_step(group, carry):
         slots = [SIDES * group + side for side in range(SIDES)]
-        ready = [prepare(slots[0], 0)]
+        ready = carry
         for side in range(SIDES):
-            if side + 1 < SIDES:
-                ready.append(prepare(slots[side + 1], side + 1))
-            multiply(side, *ready[side])
+            following = prepare(slots[side] + 1, (side + 1) % SIDES)
+            multiply(side, *ready)
+            ready = following
             live = (slots[side] < count).astype(jnp.float32) if side else None
             finish(slots[side], side, live)
-        return carry
-
-    lax.fori_loop(0, steps, group_step, 0)
+        return ready
+
+    first = prepare(0, 0)
+    for copy in masks:
+        copy.wait()
+    lax.fori_loop(0, steps, group_step, first)
     whole = total[0:4, :H]
     sums[...] = whole
     scale = 1.0 / (TURNS * FLOPS)
@@ -369,7 +370,7 @@
             pltpu.VMEM((1, TS, RIV, H), jnp.float32),
             pltpu.VMEM((4, 16, 128), jnp.int32),
             pltpu.VMEM((CP, CP), jnp.bfloat16),
-            pltpu.VMEM((TS, 2, 8, H), jnp.float32),
+            pltpu.VMEM((TS + 1, 2, 8, H), jnp.float32),
             [pltpu.VMEM((2, 8, HP), jnp.float32)] * SIDES,
             [pltpu.VMEM((2, 16, 128), jnp.int32)] * SIDES,
             [pltpu.VMEM((RIV, 16, 128), jnp.float32)] * SIDES,
@@ -382,7 +383,7 @@
             pltpu.VMEM((A, A, H), jnp.float32),
             pltpu.SemaphoreType.DMA((4,)),
             pltpu.SemaphoreType.DMA((len(BLOCKS),)),
-            pltpu.SemaphoreType.DMA((TS, A)),
+            pltpu.SemaphoreType.DMA((TS + 1, A)),
             pltpu.SemaphoreType.DMA((TS, A)),
         ],
         compiler_params=pltpu.CompilerParams(vmem_limit_bytes=60 * 1024 * 1024),

time: 79 us -> 77.2 us (0.977)
  starting transfers between devices: 45.8 us -> 21.1 us
  Pallas kernels: 19 us -> 41.7 us
    all_to_all x2, starting transfers between devices: 40.1 us -> 15.5 us  [group_sum(): lax.all_to_all(copies, axis, 0, 0, axis_index_groups=groups, tiled=True)]
    pallas_call x1, Pallas kernels: 19 us -> 41.7 us  [on_device(): pl.pallas_call(kernel, out_shape=(jax.ShapeDtypeStruct(turn_regret.shape,...]
where the time goes in v11:
time: 77.2 us; the launch traced here: 76.7 us
  Pallas kernels  41.7 us (54%)
  starting transfers between devices  21.1 us (27%)
  waiting for transfers between devices  10.5 us (14%)
  other arithmetic  2.12 us (3%)
    pallas_call x1, Pallas kernels, on_device(): pl.pallas_call(kernel, out_shape=(jax.ShapeDtypeStruct(turn_regret.shape,...  41.7 us
    all_to_all x2, starting transfers between devices, group_sum(): lax.all_to_all(copies, axis, 0, 0, axis_index_groups=groups, tiled=True)  15.5 us
    all_to_all x2, waiting for transfers between devices, group_sum(): lax.all_to_all(copies, axis, 0, 0, axis_index_groups=groups, tiled=True)  9.62 us
    ppermute x3, starting transfers between devices, on_device(): lax.ppermute(sums, 'turn', [(n, n ^ flip) for n in range(4)])  3.34 us
    ppermute x1, starting transfers between devices, flip_sum(): return x + lax.ppermute(x, axis, [(n, n ^ flip) for n in range(size)])  2.2 us
  transfers between devices with their start and end apart: 6, of which 3 were waited for; matrix products, arithmetic and copies ran while one was open for 2% of the time, Pallas kernels for 0%

profile of v11, /device:TPU:1, one launch (start us, length us, event | category | flops | bytes accessed | tf_op | source)
XLA Modules:
  0.0 76.7 jit_solution(13874278526021980360)
XLA Ops:
  0.6 0.0 copy-start
  0.6 41.7 %subtrees.1 = (f32[1,24,4,4,1326]{4,3,2,1,0:T(4,128)}, f32[4,1326]{1,0:T(4,128)}, f32[16,2,1326]{2,1,0:T(2,128)}, f32[4,1326]{1,0:T(4,128)}) custom-call(s32[1,3]{1,0:T(1,128)} %flop_cards.1, s32[1,4]{1,0:T(1,128)} %live_turns.1, s32[1,24]{1,0:T(1,128)} %turn_card.1, s32[1,2,24]{2,1,0:T(2,128)} %bitcast.11, f32[2,1326]{1,0:T(2,128)} %ranges_in.1, ...), custom_call_target="tpu_custom_call" | custom-call | tf_op jit(solution)/shard_map/subtrees/pallas_call | solution.py:357
  42.3 7.3 %all-to-all-start = ((f32[16,2,1326]{2,1,0:T(2,128)}), f32[16,2,1326]{2,1,0:T(2,128)S(1)}, u32[]{:S(2)}, u32[]{:S(2)}) async-start(f32[16,2,1326]{2,1,0:T(2,128)} %get-tuple-element.12), calls=%async_computation | async-start | bytes 360448 | tf_op jit(solution)/shard_map/all_to_all | solution.py:341
  49.7 2.6 %collective-permute-start.3 = (f32[4,1326]{1,0:T(4,128)}, f32[4,1326]{1,0:T(4,128)S(1)}, u32[]{:S(2)}, u32[]{:S(2)}) collective-permute-start(f32[4,1326]{1,0:T(4,128)} %get-tuple-element.11), channel_id=1, source_target_pairs={{0,3},{1,2},{2,1},{3,0},{4,7},{5,6},{6,5},{7,4},{8,11},{9,10},{10,... | collective-permute-start | bytes 63656 | tf_op jit(solution)/shard_map/ppermute | solution.py:396
  52.2 0.6 collective-permute-start.2
  52.8 0.2 collective-permute-start.1
  53.0 3.7 %all-to-all-done = f32[16,2,1326]{2,1,0:T(2,128)S(1)} async-done(((f32[16,2,1326]{2,1,0:T(2,128)}), f32[16,2,1326]{2,1,0:T(2,128)S(1)}, u32[]{:S(2)}, u32[]{:S(2)}) %all-to-all-start) | async-done | bytes 169760 | tf_op jit(solution)/shard_map/all_to_all | solution.py:341
  56.7 0.1 reduce_sum.27
  56.7 2.2 %collective-permute-start = (f32[2,1326]{1,0:T(2,128)S(1)}, f32[2,1326]{1,0:T(2,128)S(1)}, u32[]{:S(2)}, u32[]{:S(2)}) collective-permute-start(f32[2,1326]{1,0:T(2,128)S(1)} %reduce_sum.27), channel_id=1, source_target_pairs={{0,4},{4,0},{8,12},{12,8},{16,20},{20,16},{24,28},{28,24},{32,36},... | collective-permute-start | bytes 31832 | tf_op jit(solution)/shard_map/ppermute | solution.py:347
  58.9 0.8 %collective-permute-done = f32[2,1326]{1,0:T(2,128)S(1)} collective-permute-done((f32[2,1326]{1,0:T(2,128)S(1)}, f32[2,1326]{1,0:T(2,128)S(1)}, u32[]{:S(2)}, u32[]{:S(2)}) %collective-permute-start) | collective-permute-done | bytes 10640 | tf_op jit(solution)/shard_map/ppermute | solution.py:347
  59.8 0.0 collective-permute-done.3
  59.8 0.0 collective-permute-done.2
  59.8 0.0 collective-permute-done.1
  59.8 0.7 broadcast_in_dim.8
  60.5 8.2 %all-to-all-start.1 = ((f32[8,2,1326]{2,1,0:T(2,128)}), f32[8,2,1326]{2,1,0:T(2,128)S(1)}, u32[]{:S(2)}, u32[]{:S(2)}) async-start(f32[8,2,1326]{2,1,0:T(2,128)} %broadcast_in_dim.8), calls=%async_computation.1 | async-start | bytes 180224 | tf_op jit(solution)/shard_map/all_to_all | solution.py:341
  68.6 0.8 %multiply_reduce_fusion = (f32[1326]{0:T(1024)S(1)}, f32[4,1326]{1,0:T(4,128)S(1)}) fusion(f32[4,1326]{1,0:T(4,128)} %get-tuple-element.16, f32[4,1326]{1,0:T(4,128)S(1)} %collective-permute-done.2, f32[4,1326]{1,0:T(4,128)S(1)} %collective-permute-done.3, f32[4,1326]{1,0:T(4,128)} %get-tuple-element.11, f32[4,1326]{1,0:T(4,128)S(1)} %collective-permute-done.1), kind=kLoop, calls=%fused_computation.4 | loop fusion | flops 30498 | bytes 132600 | tf_op jit(solution)/shard_map/reduce_sum | solution.py:409
  69.4 0.0 copy-done
  69.4 0.6 fusion.2
  70.1 6.0 %all-to-all-done.1 = f32[8,2,1326]{2,1,0:T(2,128)S(1)} async-done(((f32[8,2,1326]{2,1,0:T(2,128)}), f32[8,2,1326]{2,1,0:T(2,128)S(1)}, u32[]{:S(2)}, u32[]{:S(2)}) %all-to-all-start.1) | async-done | bytes 84896 | tf_op jit(solution)/shard_map/all_to_all | solution.py:341
  76.0 0.6 reduce_sum.29
  (1 shorter events, 0.0 us)
Async XLA Ops:
  0.6 68.8 %copy-start = (f32[1,4,1326]{2,1,0:T(4,128)S(1)}, f32[1,4,1326]{2,1,0:T(4,128)}, u32[]{:S(2)}) copy-start(f32[1,4,1326]{2,1,0:T(4,128)} %flop_regret_in.1) | copy-start | bytes 63652
  42.3 14.3 %all-to-all-start = ((f32[16,2,1326]{2,1,0:T(2,128)}), f32[16,2,1326]{2,1,0:T(2,128)S(1)}, u32[]{:S(2)}, u32[]{:S(2)}) async-start(f32[16,2,1326]{2,1,0:T(2,128)} %get-tuple-element.12), calls=%async_computation | async-start | bytes 360448 | tf_op jit(solution)/shard_map/all_to_all | solution.py:341
  49.7 10.1 %collective-permute-start.3 = (f32[4,1326]{1,0:T(4,128)}, f32[4,1326]{1,0:T(4,128)S(1)}, u32[]{:S(2)}, u32[]{:S(2)}) collective-permute-start(f32[4,1326]{1,0:T(4,128)} %get-tuple-element.11), channel_id=1, source_target_pairs={{0,3},{1,2},{2,1},{3,0},{4,7},{5,6},{6,5},{7,4},{8,11},{9,10},{10,... | collective-permute-start | bytes 63656 | tf_op jit(solution)/shard_map/ppermute | solution.py:396
  52.2 7.5 %collective-permute-start.2 = (f32[4,1326]{1,0:T(4,128)}, f32[4,1326]{1,0:T(4,128)S(1)}, u32[]{:S(2)}, u32[]{:S(2)}) collective-permute-start(f32[4,1326]{1,0:T(4,128)} %get-tuple-element.11), channel_id=1, source_target_pairs={{0,2},{1,3},{2,0},{3,1},{4,6},{5,7},{6,4},{7,5},{8,10},{9,11},{10,... | collective-permute-start | bytes 63656 | tf_op jit(solution)/shard_map/ppermute | solution.py:396
  52.8 7.0 %collective-permute-start.1 = (f32[4,1326]{1,0:T(4,128)}, f32[4,1326]{1,0:T(4,128)S(1)}, u32[]{:S(2)}, u32[]{:S(2)}) collective-permute-start(f32[4,1326]{1,0:T(4,128)} %get-tuple-element.11), channel_id=1, source_target_pairs={{0,1},{1,0},{2,3},{3,2},{4,5},{5,4},{6,7},{7,6},{8,9},{9,8},{10,11... | collective-permute-start | bytes 63656 | tf_op jit(solution)/shard_map/ppermute | solution.py:396
  56.7 3.0 %collective-permute-start = (f32[2,1326]{1,0:T(2,128)S(1)}, f32[2,1326]{1,0:T(2,128)S(1)}, u32[]{:S(2)}, u32[]{:S(2)}) collective-permute-start(f32[2,1326]{1,0:T(2,128)S(1)} %reduce_sum.27), channel_id=1, source_target_pairs={{0,4},{4,0},{8,12},{12,8},{16,20},{20,16},{24,28},{28,24},{32,36},... | collective-permute-start | bytes 31832 | tf_op jit(solution)/shard_map/ppermute | solution.py:347
  60.5 15.6 %all-to-all-start.1 = ((f32[8,2,1326]{2,1,0:T(2,128)}), f32[8,2,1326]{2,1,0:T(2,128)S(1)}, u32[]{:S(2)}, u32[]{:S(2)}) async-start(f32[8,2,1326]{2,1,0:T(2,128)} %broadcast_in_dim.8), calls=%async_computation.1 | async-start | bytes 180224 | tf_op jit(solution)/shard_map/all_to_all | solution.py:341

commit v12 on v11

--- a/solution.py
+++ b/solution.py
@@ -20,7 +20,7 @@
 FLOPS = 64
 NEAR = 16
 BLOCK = 256
-ROWS = 128
+ROWS = 64
 BIG = 2.0**126
 
 bet_sizes = (0.25, 0.5, 1.0, 2.0)

time: 77.2 us -> 78 us (1.010)
  Pallas kernels: 41.7 us -> 42.6 us
    pallas_call x1, Pallas kernels: 41.7 us -> 42.6 us  [on_device(): pl.pallas_call(kernel, out_shape=(jax.ShapeDtypeStruct(turn_regret.shape,...]
where the time goes in v12:
time: 78 us; the launch traced here: 77.6 us
  Pallas kernels  42.6 us (55%)
  starting transfers between devices  21.1 us (27%)
  waiting for transfers between devices  10.5 us (13%)
  other arithmetic  2.12 us (3%)
    pallas_call x1, Pallas kernels, on_device(): pl.pallas_call(kernel, out_shape=(jax.ShapeDtypeStruct(turn_regret.shape,...  42.6 us
    all_to_all x2, starting transfers between devices, group_sum(): lax.all_to_all(copies, axis, 0, 0, axis_index_groups=groups, tiled=True)  15.5 us
    all_to_all x2, waiting for transfers between devices, group_sum(): lax.all_to_all(copies, axis, 0, 0, axis_index_groups=groups, tiled=True)  9.62 us
    ppermute x3, starting transfers between devices, on_device(): lax.ppermute(sums, 'turn', [(n, n ^ flip) for n in range(4)])  3.34 us
    ppermute x1, starting transfers between devices, flip_sum(): return x + lax.ppermute(x, axis, [(n, n ^ flip) for n in range(size)])  2.21 us
  transfers between devices with their start and end apart: 6, of which 3 were waited for; matrix products, arithmetic and copies ran while one was open for 2% of the time, Pallas kernels for 0%

profile of v12, /device:TPU:1, one launch (start us, length us, event | category | flops | bytes accessed | tf_op | source)
XLA Modules:
  0.0 77.6 jit_solution(10255817718814126168)
XLA Ops:
  0.6 0.0 copy-start
  0.6 42.6 %subtrees.1 = (f32[1,24,4,4,1326]{4,3,2,1,0:T(4,128)}, f32[4,1326]{1,0:T(4,128)}, f32[16,2,1326]{2,1,0:T(2,128)}, f32[4,1326]{1,0:T(4,128)}) custom-call(s32[1,3]{1,0:T(1,128)} %flop_cards.1, s32[1,4]{1,0:T(1,128)} %live_turns.1, s32[1,24]{1,0:T(1,128)} %turn_card.1, s32[1,2,24]{2,1,0:T(2,128)} %bitcast.11, f32[2,1326]{1,0:T(2,128)} %ranges_in.1, ...), custom_call_target="tpu_custom_call" | custom-call | tf_op jit(solution)/shard_map/subtrees/pallas_call | solution.py:357
  43.2 7.3 %all-to-all-start = ((f32[16,2,1326]{2,1,0:T(2,128)}), f32[16,2,1326]{2,1,0:T(2,128)S(1)}, u32[]{:S(2)}, u32[]{:S(2)}) async-start(f32[16,2,1326]{2,1,0:T(2,128)} %get-tuple-element.12), calls=%async_computation | async-start | bytes 360448 | tf_op jit(solution)/shard_map/all_to_all | solution.py:341
  50.6 2.6 %collective-permute-start.3 = (f32[4,1326]{1,0:T(4,128)}, f32[4,1326]{1,0:T(4,128)S(1)}, u32[]{:S(2)}, u32[]{:S(2)}) collective-permute-start(f32[4,1326]{1,0:T(4,128)} %get-tuple-element.11), channel_id=1, source_target_pairs={{0,3},{1,2},{2,1},{3,0},{4,7},{5,6},{6,5},{7,4},{8,11},{9,10},{10,... | collective-permute-start | bytes 63656 | tf_op jit(solution)/shard_map/ppermute | solution.py:396
  53.1 0.6 collective-permute-start.2
  53.7 0.2 collective-permute-start.1
  53.9 3.7 %all-to-all-done = f32[16,2,1326]{2,1,0:T(2,128)S(1)} async-done(((f32[16,2,1326]{2,1,0:T(2,128)}), f32[16,2,1326]{2,1,0:T(2,128)S(1)}, u32[]{:S(2)}, u32[]{:S(2)}) %all-to-all-start) | async-done | bytes 169760 | tf_op jit(solution)/shard_map/all_to_all | solution.py:341
  57.6 0.1 reduce_sum.27
  57.6 2.2 %collective-permute-start = (f32[2,1326]{1,0:T(2,128)S(1)}, f32[2,1326]{1,0:T(2,128)S(1)}, u32[]{:S(2)}, u32[]{:S(2)}) collective-permute-start(f32[2,1326]{1,0:T(2,128)S(1)} %reduce_sum.27), channel_id=1, source_target_pairs={{0,4},{4,0},{8,12},{12,8},{16,20},{20,16},{24,28},{28,24},{32,36},... | collective-permute-start | bytes 31832 | tf_op jit(solution)/shard_map/ppermute | solution.py:347
  59.8 0.8 %collective-permute-done = f32[2,1326]{1,0:T(2,128)S(1)} collective-permute-done((f32[2,1326]{1,0:T(2,128)S(1)}, f32[2,1326]{1,0:T(2,128)S(1)}, u32[]{:S(2)}, u32[]{:S(2)}) %collective-permute-start) | collective-permute-done | bytes 10640 | tf_op jit(solution)/shard_map/ppermute | solution.py:347
  60.7 0.0 collective-permute-done.3
  60.7 0.0 collective-permute-done.2
  60.7 0.0 collective-permute-done.1
  60.7 0.7 broadcast_in_dim.8
  61.4 8.2 %all-to-all-start.1 = ((f32[8,2,1326]{2,1,0:T(2,128)}), f32[8,2,1326]{2,1,0:T(2,128)S(1)}, u32[]{:S(2)}, u32[]{:S(2)}) async-start(f32[8,2,1326]{2,1,0:T(2,128)} %broadcast_in_dim.8), calls=%async_computation.1 | async-start | bytes 180224 | tf_op jit(solution)/shard_map/all_to_all | solution.py:341
  69.5 0.8 %multiply_reduce_fusion = (f32[1326]{0:T(1024)S(1)}, f32[4,1326]{1,0:T(4,128)S(1)}) fusion(f32[4,1326]{1,0:T(4,128)} %get-tuple-element.16, f32[4,1326]{1,0:T(4,128)S(1)} %collective-permute-done.2, f32[4,1326]{1,0:T(4,128)S(1)} %collective-permute-done.3, f32[4,1326]{1,0:T(4,128)} %get-tuple-element.11, f32[4,1326]{1,0:T(4,128)S(1)} %collective-permute-done.1), kind=kLoop, calls=%fused_computation.4 | loop fusion | flops 30498 | bytes 132600 | tf_op jit(solution)/shard_map/reduce_sum | solution.py:409
  70.3 0.0 copy-done
  70.3 0.6 fusion.2
  71.0 6.0 %all-to-all-done.1 = f32[8,2,1326]{2,1,0:T(2,128)S(1)} async-done(((f32[8,2,1326]{2,1,0:T(2,128)}), f32[8,2,1326]{2,1,0:T(2,128)S(1)}, u32[]{:S(2)}, u32[]{:S(2)}) %all-to-all-start.1) | async-done | bytes 84896 | tf_op jit(solution)/shard_map/all_to_all | solution.py:341
  76.9 0.6 reduce_sum.29
  (1 shorter events, 0.0 us)
Async XLA Ops:
  0.6 69.7 %copy-start = (f32[1,4,1326]{2,1,0:T(4,128)S(1)}, f32[1,4,1326]{2,1,0:T(4,128)}, u32[]{:S(2)}) copy-start(f32[1,4,1326]{2,1,0:T(4,128)} %flop_regret_in.1) | copy-start | bytes 63652
  43.2 14.3 %all-to-all-start = ((f32[16,2,1326]{2,1,0:T(2,128)}), f32[16,2,1326]{2,1,0:T(2,128)S(1)}, u32[]{:S(2)}, u32[]{:S(2)}) async-start(f32[16,2,1326]{2,1,0:T(2,128)} %get-tuple-element.12), calls=%async_computation | async-start | bytes 360448 | tf_op jit(solution)/shard_map/all_to_all | solution.py:341
  50.6 10.1 %collective-permute-start.3 = (f32[4,1326]{1,0:T(4,128)}, f32[4,1326]{1,0:T(4,128)S(1)}, u32[]{:S(2)}, u32[]{:S(2)}) collective-permute-start(f32[4,1326]{1,0:T(4,128)} %get-tuple-element.11), channel_id=1, source_target_pairs={{0,3},{1,2},{2,1},{3,0},{4,7},{5,6},{6,5},{7,4},{8,11},{9,10},{10,... | collective-permute-start | bytes 63656 | tf_op jit(solution)/shard_map/ppermute | solution.py:396
  53.1 7.5 %collective-permute-start.2 = (f32[4,1326]{1,0:T(4,128)}, f32[4,1326]{1,0:T(4,128)S(1)}, u32[]{:S(2)}, u32[]{:S(2)}) collective-permute-start(f32[4,1326]{1,0:T(4,128)} %get-tuple-element.11), channel_id=1, source_target_pairs={{0,2},{1,3},{2,0},{3,1},{4,6},{5,7},{6,4},{7,5},{8,10},{9,11},{10,... | collective-permute-start | bytes 63656 | tf_op jit(solution)/shard_map/ppermute | solution.py:396
  53.7 7.0 %collective-permute-start.1 = (f32[4,1326]{1,0:T(4,128)}, f32[4,1326]{1,0:T(4,128)S(1)}, u32[]{:S(2)}, u32[]{:S(2)}) collective-permute-start(f32[4,1326]{1,0:T(4,128)} %get-tuple-element.11), channel_id=1, source_target_pairs={{0,1},{1,0},{2,3},{3,2},{4,5},{5,4},{6,7},{7,6},{8,9},{9,8},{10,11... | collective-permute-start | bytes 63656 | tf_op jit(solution)/shard_map/ppermute | solution.py:396
  57.6 3.0 %collective-permute-start = (f32[2,1326]{1,0:T(2,128)S(1)}, f32[2,1326]{1,0:T(2,128)S(1)}, u32[]{:S(2)}, u32[]{:S(2)}) collective-permute-start(f32[2,1326]{1,0:T(2,128)S(1)} %reduce_sum.27), channel_id=1, source_target_pairs={{0,4},{4,0},{8,12},{12,8},{16,20},{20,16},{24,28},{28,24},{32,36},... | collective-permute-start | bytes 31832 | tf_op jit(solution)/shard_map/ppermute | solution.py:347
  61.4 15.6 %all-to-all-start.1 = ((f32[8,2,1326]{2,1,0:T(2,128)}), f32[8,2,1326]{2,1,0:T(2,128)S(1)}, u32[]{:S(2)}, u32[]{:S(2)}) async-start(f32[8,2,1326]{2,1,0:T(2,128)} %broadcast_in_dim.8), calls=%async_computation.1 | async-start | bytes 180224 | tf_op jit(solution)/shard_map/all_to_all | solution.py:341
